TPU v7x, 128 devices: a whole 4x4x4 slice. The times are simulated.
128 devices in a mesh: dp: 32 (over x, z_lo, y), seq: 4 (over z_hi, core).
Axes of the slice: x: 4, y: 4, z: 4 (z_hi: 2, z_lo: 2; z = z_hi * 2 + z_lo), core: 2. Of those that a mesh axis runs over, the one named last changes fastest.
Arguments:
- latents: bfloat16 [64, 32, 32, 768], P('dp', 'seq'), may hold values from -6 to 6
- conditioning: bfloat16 [64, 768], P('dp'), may hold values from -6 to 6
- timesteps: int32 [64], P('dp'), may hold values from 0 to 999
- item_counts: int32 [32], P('dp'), may hold values from 1 to 2, as said below
- cotangent: bfloat16 [64, 32, 32, 768], P('dp', 'seq'), may hold values from -6 to 6
- time_table: bfloat16 [1000, 768], replicated, may hold values from -3 to 3
- mod_weight: bfloat16 [768, 4608], replicated, may hold values from -0.21875 to 0.21875
- mod_bias: bfloat16 [4608], replicated, may hold values from -1.796875 to 1.796875
- conv_attn_weight: bfloat16 [9, 768], replicated, may hold values from -2 to 2
- conv_attn_bias: bfloat16 [768], replicated, may hold values from -3 to 3
- qkv_weight: bfloat16 [768, 2304], replicated, may hold values from -0.21875 to 0.21875
- query_bias: bfloat16 [768], replicated, may hold values from -3 to 3
- value_bias: bfloat16 [768], replicated, may hold values from -3 to 3
- out_weight: bfloat16 [768, 768], replicated, may hold values from -3.5 to 3.5
- out_bias: bfloat16 [768], replicated, may hold values from -1.796875 to 1.796875
- fc1_weight: bfloat16 [768, 3072], replicated, may hold values from -0.21875 to 0.21875
- fc1_bias: bfloat16 [3072], replicated, may hold values from -3 to 3
- conv_ffn_weight: bfloat16 [9, 3072], replicated, may hold values from -2 to 2
- conv_ffn_bias: bfloat16 [3072], replicated, may hold values from -3 to 3
- fc2_weight: bfloat16 [3072, 768], replicated, may hold values from -0.109375 to 0.109375
- fc2_bias: bfloat16 [768], replicated, may hold values from -1.796875 to 1.796875
Outputs:
- output: bfloat16 [64, 32, 32, 768], P('dp', 'seq')
- input_grad: float32 [64, 32, 32, 768], P('dp', 'seq')
- conditioning_grad: float32 [64, 768], P('dp')
- time_table_grad: float32 [1000, 768], P(None, ('dp', 'seq'))
- mod_weight_grad: float32 [768, 4608], P(('dp', 'seq'))
- mod_bias_grad: float32 [4608], P(('dp', 'seq'))
- conv_attn_weight_grad: float32 [9, 768], P(None, ('dp', 'seq'))
- conv_attn_bias_grad: float32 [768], P(('dp', 'seq'))
- qkv_weight_grad: float32 [768, 2304], P(('dp', 'seq'))
- query_bias_grad: float32 [768], P(('dp', 'seq'))
- value_bias_grad: float32 [768], P(('dp', 'seq'))
- out_weight_grad: float32 [768, 768], P(('dp', 'seq'))
- out_bias_grad: float32 [768], P(('dp', 'seq'))
- fc1_weight_grad: float32 [768, 3072], P(('dp', 'seq'))
- fc1_bias_grad: float32 [3072], P(('dp', 'seq'))
- conv_ffn_weight_grad: float32 [9, 3072], P(None, ('dp', 'seq'))
- conv_ffn_bias_grad: float32 [3072], P(('dp', 'seq'))
- fc2_weight_grad: float32 [3072, 768], P(('dp', 'seq'))
- fc2_bias_grad: float32 [768], P(('dp', 'seq'))
Inputs may be any that keep to these rules, and one draw needn't show every extreme that they name: Item j of index i of dp is live when j < item_counts[i]; some index has 2 live items and some index one.
All inputs are finite; a program needn't handle non-finite values.
Results may differ from a plain program's by a relative error of at most 0.023.
Values may be sent and summed in bfloat16 or wider, within the bound.
A program may use at most 256 MiB of HBM per device.

v0:
```python
from functools import partial

import jax
import jax.numpy as jnp
from jax import lax
from jax.sharding import PartitionSpec as P

HEADS = 12


def with_halo(cells, sides, width):
    for axis, dim in sides:
        count = lax.axis_size(axis)
        ends = count - 1
        head = lax.slice_in_dim(cells, 0, width, axis=dim)
        tail = lax.slice_in_dim(cells, cells.shape[dim] - width, cells.shape[dim], axis=dim)
        cells = jnp.concatenate(
            [
                lax.ppermute(tail, axis, [(i, (i + 1) % count) for i in range(ends)]),
                cells,
                lax.ppermute(head, axis, [((i + 1) % count, i) for i in range(ends)]),
            ],
            axis=dim,
        )
    return cells


def layer_norm(values):
    center = values - jnp.mean(values, axis=-1, keepdims=True)
    spread = jnp.mean(center * center, axis=-1, keepdims=True)
    return center * lax.rsqrt(spread + 1e-06)


def norm_modulate(values, shift_term, scale_term):
    return layer_norm(values) * (1.0 + scale_term) + shift_term


def depthwise(padded, taps):
    row_count = padded.shape[1] - 2
    col_count = padded.shape[2]
    widened = jnp.pad(padded, ((0, 0), (0, 0), (1, 1), (0, 0)))
    total = jnp.zeros((padded.shape[0], row_count, col_count, padded.shape[3]), jnp.float32)
    for row_tap in range(3):
        for col_tap in range(3):
            total = (
                total
                + taps[row_tap * 3 + col_tap]
                * widened[:, row_tap : row_tap + row_count, col_tap : col_tap + col_count, :]
            )
    return total


def tap_grads(grad_out, padded):
    row_count = grad_out.shape[1]
    col_count = grad_out.shape[2]
    widened = jnp.pad(padded, ((0, 0), (0, 0), (1, 1), (0, 0)))
    return jnp.stack(
        [
            jnp.sum(
                grad_out
                * widened[:, row_tap : row_tap + row_count, col_tap : col_tap + col_count, :],
                axis=(0, 1, 2),
            )
            for row_tap in range(3)
            for col_tap in range(3)
        ]
    )


def to_groups(values):
    extent = values.shape
    halved = values.reshape(extent[0], extent[1] // 2, 2, extent[2] // 2, 2, extent[3])
    return halved.transpose(0, 2, 4, 1, 3, 5).reshape(
        extent[0], 4, extent[1] // 2, extent[2] // 2, extent[3]
    )


def from_groups(values):
    extent = values.shape
    halved = values.reshape(extent[0], 2, 2, extent[2], extent[3], extent[4])
    return halved.transpose(0, 3, 1, 4, 2, 5).reshape(
        extent[0], 2 * extent[2], 2 * extent[3], extent[4]
    )


def project(values, matrix):
    return jnp.einsum("srwc,cd->srwd", values, matrix, preferred_element_type=jnp.float32)


def project_back(values, matrix):
    return jnp.einsum("srwd,cd->srwc", values, matrix, preferred_element_type=jnp.float32)


def outer_sum(left, right):
    return jnp.einsum("srwc,srwd->cd", left, right, preferred_element_type=jnp.float32)


def token_sum(values):
    return jnp.sum(values.astype(jnp.float32), axis=(0, 1, 2))


def attention_scores(queries, keys_all):
    return 0.125 * jnp.einsum(
        "sgqhd,sgkhd->sghqk", queries, keys_all, preferred_element_type=jnp.float32
    )


def attention_probs(queries, keys_all):
    return jax.nn.softmax(attention_scores(queries, keys_all), axis=-1)


def local(
    latents,
    conditioning,
    timesteps,
    item_counts,
    cotangent,
    time_table,
    mod_weight,
    mod_bias,
    conv_attn_weight,
    conv_attn_bias,
    qkv_weight,
    query_bias,
    value_bias,
    out_weight,
    out_bias,
    fc1_weight,
    fc1_bias,
    conv_ffn_weight,
    conv_ffn_bias,
    fc2_weight,
    fc2_bias,
):
    slot_count, row_count, col_count, model_dim = latents.shape
    head_dim = model_dim // HEADS
    group_rows = row_count // 2
    group_cols = col_count // 2
    share = 1.0 / lax.axis_size("seq")
    alive_mask = (jnp.arange(slot_count) < item_counts[0]).astype(jnp.float32)[:, None, None, None]
    one_hot = (timesteps[:, None] == jnp.arange(time_table.shape[0])[None, :]).astype(jnp.bfloat16)
    cond_full = conditioning.astype(jnp.float32) + jnp.dot(
        one_hot, time_table, preferred_element_type=jnp.float32
    )
    silu_cond = jax.nn.silu(cond_full).astype(jnp.bfloat16)
    modulation = jnp.dot(
        silu_cond, mod_weight, preferred_element_type=jnp.float32
    ) + mod_bias.astype(jnp.float32)
    pieces = [
        modulation[:, index * model_dim : (index + 1) * model_dim][:, None, None, :]
        for index in range(6)
    ]
    shift_one, scale_one, gate_one, shift_two, scale_two, gate_two = pieces

    def split_heads(values):
        return values.reshape(slot_count, 4, -1, HEADS, head_dim)

    inputs = latents.astype(jnp.float32)
    normed = norm_modulate(inputs, shift_one, scale_one).astype(jnp.bfloat16)
    normed_pad = with_halo(normed, (("seq", 1),), 1)
    taps_attn = conv_attn_weight.astype(jnp.float32)
    mixed_in = (
        depthwise(normed_pad.astype(jnp.float32), taps_attn) + conv_attn_bias.astype(jnp.float32)
    ).astype(jnp.bfloat16)
    qkv_bias = jnp.concatenate(
        (
            query_bias.astype(jnp.float32),
            jnp.zeros((model_dim,), jnp.float32),
            value_bias.astype(jnp.float32),
        )
    )
    qkv_all = (project(mixed_in, qkv_weight) + qkv_bias).astype(jnp.bfloat16)
    queries = split_heads(to_groups(qkv_all[..., :model_dim]))
    key_value = jnp.stack(
        (
            to_groups(qkv_all[..., model_dim : 2 * model_dim]),
            to_groups(qkv_all[..., 2 * model_dim :]),
        )
    )
    gathered = lax.all_gather(key_value, "seq", axis=3, tiled=True)
    keys_all = split_heads(gathered[0])
    values_all = split_heads(gathered[1])
    probs = attention_probs(queries, keys_all)
    probs_low = probs.astype(jnp.bfloat16)
    attended = jnp.einsum(
        "sghqk,sgkhd->sgqhd", probs_low, values_all, preferred_element_type=jnp.float32
    )
    attended = from_groups(
        attended.reshape(slot_count, 4, group_rows, group_cols, model_dim)
    ).astype(jnp.bfloat16)
    branch = project(attended, out_weight) + out_bias.astype(jnp.float32)
    hidden_one = inputs + gate_one * branch
    normed_two = norm_modulate(hidden_one, shift_two, scale_two).astype(jnp.bfloat16)
    expanded = (project(normed_two, fc1_weight) + fc1_bias.astype(jnp.float32)).astype(jnp.bfloat16)
    expanded_pad = with_halo(expanded, (("seq", 1),), 1)
    taps_ffn = conv_ffn_weight.astype(jnp.float32)
    mixed_ffn = depthwise(expanded_pad.astype(jnp.float32), taps_ffn) + conv_ffn_bias.astype(
        jnp.float32
    )
    activated, gelu_back = jax.vjp(partial(jax.nn.gelu, approximate=False), mixed_ffn)
    activated = activated.astype(jnp.bfloat16)
    ffn_out = project(activated, fc2_weight) + fc2_bias.astype(jnp.float32)
    hidden_two = hidden_one + gate_two * ffn_out
    output = (hidden_two * alive_mask).astype(jnp.bfloat16)
    grad_out = cotangent.astype(jnp.float32) * alive_mask
    grad_gate_two = jnp.sum(grad_out * ffn_out, axis=(1, 2), keepdims=True)
    grad_ffn = (grad_out * gate_two).astype(jnp.bfloat16)
    fc2_grad = outer_sum(activated, grad_ffn)
    fc2_bias_grad = token_sum(grad_ffn)
    grad_mixed_ffn = gelu_back(project_back(grad_ffn, fc2_weight))[0].astype(jnp.bfloat16)
    grad_ffn_pad = with_halo(grad_mixed_ffn, (("seq", 1),), 1)
    grad_expanded = depthwise(grad_ffn_pad.astype(jnp.float32), taps_ffn[::-1]).astype(jnp.bfloat16)
    conv_ffn_grad = tap_grads(grad_mixed_ffn.astype(jnp.float32), expanded_pad.astype(jnp.float32))
    conv_ffn_bias_grad = token_sum(grad_mixed_ffn)
    fc1_grad = outer_sum(normed_two, grad_expanded)
    fc1_bias_grad = token_sum(grad_expanded)
    grad_normed_two = project_back(grad_expanded, fc1_weight)
    _, norm_two_back = jax.vjp(norm_modulate, hidden_one, shift_two, scale_two)
    grad_hidden_part, grad_shift_two, grad_scale_two = norm_two_back(grad_normed_two)
    grad_hidden = grad_out + grad_hidden_part
    grad_gate_one = jnp.sum(grad_hidden * branch, axis=(1, 2), keepdims=True)
    grad_branch = (grad_hidden * gate_one).astype(jnp.bfloat16)
    out_grad = outer_sum(attended, grad_branch)
    out_bias_grad = token_sum(grad_branch)
    grad_attended = project_back(grad_branch, out_weight).astype(jnp.bfloat16)
    grad_groups = split_heads(to_groups(grad_attended))
    grad_probs = jnp.einsum(
        "sgqhd,sgkhd->sghqk", grad_groups, values_all, preferred_element_type=jnp.float32
    )
    row_terms = jnp.sum(probs * grad_probs, axis=-1, keepdims=True)
    grad_scores = (probs * (grad_probs - row_terms)).astype(jnp.bfloat16)
    grad_queries = 0.125 * jnp.einsum(
        "sghqk,sgkhd->sgqhd", grad_scores, keys_all, preferred_element_type=jnp.float32
    )
    key_rows = keys_all.shape[2] // group_cols
    grad_keys = 0.125 * jnp.einsum(
        "sghqk,sgqhd->sgkhd", grad_scores, queries, preferred_element_type=jnp.float32
    )
    grad_values = jnp.einsum(
        "sghqk,sgqhd->sgkhd", probs_low, grad_groups, preferred_element_type=jnp.float32
    )
    grad_pairs = jnp.stack((grad_keys, grad_values)).reshape(
        2, slot_count, 4, key_rows, group_cols, model_dim
    )
    grad_pairs = lax.psum_scatter(
        grad_pairs.astype(jnp.bfloat16), "seq", scatter_dimension=3, tiled=True
    ).astype(jnp.float32)
    grad_query_grid = from_groups(
        grad_queries.reshape(slot_count, 4, group_rows, group_cols, model_dim)
    )
    grad_qkv = jnp.concatenate(
        (grad_query_grid, from_groups(grad_pairs[0]), from_groups(grad_pairs[1])), axis=-1
    ).astype(jnp.bfloat16)
    qkv_grad = outer_sum(mixed_in, grad_qkv)
    query_bias_grad = token_sum(grad_qkv[..., :model_dim])
    value_bias_grad = token_sum(grad_qkv[..., 2 * model_dim :])
    grad_mixed_attn = project_back(grad_qkv, qkv_weight).astype(jnp.bfloat16)
    grad_attn_pad = with_halo(grad_mixed_attn, (("seq", 1),), 1)
    grad_normed = depthwise(grad_attn_pad.astype(jnp.float32), taps_attn[::-1])
    conv_attn_grad = tap_grads(grad_mixed_attn.astype(jnp.float32), normed_pad.astype(jnp.float32))
    conv_attn_bias_grad = token_sum(grad_mixed_attn)
    _, norm_one_back = jax.vjp(norm_modulate, inputs, shift_one, scale_one)
    grad_input_part, grad_shift_one, grad_scale_one = norm_one_back(grad_normed)
    input_grad = grad_hidden + grad_input_part
    grad_mod_part = jnp.concatenate(
        [
            term.reshape(slot_count, model_dim)
            for term in (
                grad_shift_one,
                grad_scale_one,
                grad_gate_one,
                grad_shift_two,
                grad_scale_two,
                grad_gate_two,
            )
        ],
        axis=1,
    )
    grad_mod = lax.psum(grad_mod_part.astype(jnp.bfloat16), "seq")
    mod_grad = jnp.dot(silu_cond.T, grad_mod, preferred_element_type=jnp.float32) * share
    mod_bias_grad = jnp.sum(grad_mod.astype(jnp.float32), axis=0) * share
    _, silu_back = jax.vjp(jax.nn.silu, cond_full)
    cond_grad = silu_back(
        jnp.einsum("se,de->sd", grad_mod, mod_weight, preferred_element_type=jnp.float32)
    )[0]
    table_grad = (
        jnp.dot(one_hot.astype(jnp.float32).T, cond_grad, precision=lax.Precision.HIGHEST) * share
    )
    reduced = (
        lax.psum_scatter(table_grad, ("dp", "seq"), scatter_dimension=1, tiled=True),
        lax.psum_scatter(mod_grad, ("dp", "seq"), scatter_dimension=0, tiled=True),
        lax.psum_scatter(mod_bias_grad, ("dp", "seq"), scatter_dimension=0, tiled=True),
        lax.psum_scatter(conv_attn_grad, ("dp", "seq"), scatter_dimension=1, tiled=True),
        lax.psum_scatter(conv_attn_bias_grad, ("dp", "seq"), scatter_dimension=0, tiled=True),
        lax.psum_scatter(qkv_grad, ("dp", "seq"), scatter_dimension=0, tiled=True),
        lax.psum_scatter(query_bias_grad, ("dp", "seq"), scatter_dimension=0, tiled=True),
        lax.psum_scatter(value_bias_grad, ("dp", "seq"), scatter_dimension=0, tiled=True),
        lax.psum_scatter(out_grad, ("dp", "seq"), scatter_dimension=0, tiled=True),
        lax.psum_scatter(out_bias_grad, ("dp", "seq"), scatter_dimension=0, tiled=True),
        lax.psum_scatter(fc1_grad, ("dp", "seq"), scatter_dimension=0, tiled=True),
        lax.psum_scatter(fc1_bias_grad, ("dp", "seq"), scatter_dimension=0, tiled=True),
        lax.psum_scatter(conv_ffn_grad, ("dp", "seq"), scatter_dimension=1, tiled=True),
        lax.psum_scatter(conv_ffn_bias_grad, ("dp", "seq"), scatter_dimension=0, tiled=True),
        lax.psum_scatter(fc2_grad, ("dp", "seq"), scatter_dimension=0, tiled=True),
        lax.psum_scatter(fc2_bias_grad, ("dp", "seq"), scatter_dimension=0, tiled=True),
    )
    return (output, input_grad, cond_grad) + tuple(reduced)


def solution(mesh):
    return jax.shard_map(
        local,
        mesh=mesh,
        in_specs=(
            P("dp", "seq", None, None),
            P("dp", None),
            P("dp"),
            P("dp"),
            P("dp", "seq", None, None),
            P(),
            P(),
            P(),
            P(),
            P(),
            P(),
            P(),
            P(),
            P(),
            P(),
            P(),
            P(),
            P(),
            P(),
            P(),
            P(),
        ),
        out_specs=(
            P("dp", "seq", None, None),
            P("dp", "seq", None, None),
            P("dp", None),
            P(None, ("dp", "seq")),
            P(("dp", "seq"), None),
            P(("dp", "seq")),
            P(None, ("dp", "seq")),
            P(("dp", "seq")),
            P(("dp", "seq"), None),
            P(("dp", "seq")),
            P(("dp", "seq")),
            P(("dp", "seq"), None),
            P(("dp", "seq")),
            P(("dp", "seq"), None),
            P(("dp", "seq")),
            P(None, ("dp", "seq")),
            P(("dp", "seq")),
            P(("dp", "seq"), None),
            P(("dp", "seq")),
        ),
        check_vma=False,
    )
```

profile of v0, /device:TPU:0, one launch (start us, length us, event | category | flops | bytes accessed | tf_op | source)
XLA Modules:
  0.0 1983.3 jit_solution(12772474213660548129)
XLA Ops:
  18.8 5.8 collective-permute-done.1
  56.8 39.8 %all-gather.2.cloned.1.call-done = bf16[2,2,4,16,16,768]{5,4,3,2,1,0:T(8,128)(2,1)} async-done(((bf16[2,2,4,4,16,768]{5,4,3,2,1,0:T(8,128)(2,1)}), bf16[2,2,4,16,16,768]{5,4,3,2,1,0:T(8,128)(2,1)}) %all-gather.2.cloned.1.call-update) | async-done | bytes 6291472 | tf_op jit(solution)/shard_map/all_gather | solution.py:180
  96.7 6.1 fusion.127
  102.8 10.6 reshape_squeeze.15
  113.4 9.4 copy.147
  122.8 10.6 reshape_squeeze.14
  133.3 9.4 copy.148
  142.7 7.5 fusion.135
  150.3 5.9 fusion.98
  171.8 5.4 add_convert_fusion.1
  183.8 23.5 %multiply_convert_fusion.2 = (bf16[2,8,32,3072]{3,2,1,0:T(8,128)(2,1)}, f32[2,8,32,3072]{3,2,1,0:T(8,128)}, f32[2,8,32,3072]{3,2,1,0:T(8,128)}) fusion(f32[3072]{0:T(1024)} %convert_element_type.187, f32[3072]{0:T(1024)S(1)} %bitcast.193, f32[2,10,32,3072]{3,2,1,0:T(8,128)S(1)} %maximum_convert_fusion, f32[3072]{0:T(1024)S(1)} %bitcast.191, ...), kind=kLoop, calls=%fused_computation.59 | loop fusion | flops 130547712 | bytes 42590208 | tf_op jit(solution)/shard_map/convert_element_type | solution.py:201
  207.2 36.7 %fusion.30 = (f32[3072]{0:T(1024)}, f32[3072]{0:T(1024)}, f32[3072]{0:T(1024)}, f32[3072]{0:T(1024)}, f32[3072]{0:T(1024)}, /*index=5*/f32[3072]{0:T(1024)}, f32...) fusion(f32[2,10,32,3072]{3,2,1,0:T(8,128)} %copy-done.1, ...), kind=kOutput, calls=%fused_computation.49 | convolution fusion | flops 2469365760 | bytes 48095232 | tf_op jit(solution)/shard_map/srwd,cd->srwc/dot_general | solution.py:91
  245.1 8.9 collective-permute-start.4
  262.6 26.1 %convert_reduce_fusion.1 = (f32[3072]{0:T(1024)}, bf16[2,8,32,3072]{3,2,1,0:T(8,128)(2,1)}) fusion(f32[3072]{0:T(1024)S(1)} %bitcast.178, f32[2,10,32,3072]{3,2,1,0:T(8,128)} %maximum_convert_fusion.1, f32[3072]{0:T(1024)S(1)} %bitcast.180, f32[3072]{0:T(1024)S(1)} %bitcast.182, f32[3072]{0:T(1024)S(1)} %bitcast.184, f32[3072]{0:T(1024)S(1)} %bitcast.186, ...), kind=kLoop, calls=%fused_computation.54 | loop fusion | flops 31454208 | bytes 30007296 | tf_op jit(solution)/shard_map/reduce_sum | solution.py:99
  288.8 6.2 multiply_reduce_fusion.5
  318.0 6.6 multiply_reduce_fusion
  324.6 5.6 convert_bitcast_fusion
  339.0 10.5 copy.159
  349.5 11.1 stack.73
  360.6 10.5 copy.161
  371.1 11.2 stack.74
  382.2 6.1 pad_maximum_fusion
  415.9 106.1 %all-reduce.31.cloned.1.call-done = bf16[2,2,4,16,16,768]{5,4,3,2,1,0:T(8,128)(2,1)} async-done(((bf16[2,2,4,16,16,768]{5,4,3,2,1,0:T(8,128)(2,1)}), bf16[2,2,4,16,16,768]{5,4,3,2,1,0:T(8,128)(2,1)}) %all-reduce.31.cloned.1.call-update) | async-done | bytes 6291472
  539.0 9.6 fusion.95
  574.6 15.5 psum.7
  591.5 8.4 convolution_bitcast_fusion
  603.8 6.0 convolution_bitcast_fusion.1
  620.0 7.1 convolution_multiply_fusion
  627.1 532.3 %fusion.122 = (f32[1000,8]{0,1:T(8,128)}, f32[8,4608]{1,0:T(8,128)}, f32[8,2304]{1,0:T(8,128)}, f32[8,768]{1,0:T(8,128)}, f32[8,3072]{1,0:T(8,128)}) fusion(f32[1000,768]{0,1:T(8,128)} %convolution_multiply_fusion.1, f32[768,4608]{1,0:T(8,128)} %convolution_multiply_fusion, f32[768,2304]{1,0:T(8,128)} %convolution_bitcast_fusion.2, ...), kind=kCustom, calls=%all-reduce-scatter.5 | all-reduce-scatter fusion | flops 12034049 | bytes 36478208
  1166.6 5.6 collective-permute-start.105
  1172.2 8.1 collective-permute-start.106
  1188.6 6.3 collective-permute-start.110
  1202.6 7.0 collective-permute-start.113
  1279.3 5.9 collective-permute-start.17
  1377.3 6.2 collective-permute-start.81
  1422.5 6.3 collective-permute-start.138
  1437.4 5.8 collective-permute-start.142
  1452.6 5.2 collective-permute-start.145
  1457.9 5.9 collective-permute-start.146
  1523.6 5.4 collective-permute-start.45
  1532.0 6.7 collective-permute-start.47
  1541.0 7.6 collective-permute-start.49
  1566.0 47.2 %concatenate.35 = f32[262,768]{1,0:T(8,128)} concatenate(f32[6,768]{1,0:T(8,128)} %copy-done.160, f32[8,768]{1,0:T(8,128)} %copy-done.189, f32[8,768]{1,0:T(8,128)} %copy-done.188, f32[8,768]{1,0:T(8,128)} %collective-permute-done.132, f32[8,768]{1,0:T(8,128)} %collective-permute-done.131, f32[8,768]{1,0:T(8,128)} %copy-done.187, f32[8,768]{1,0:T(8,128)} %copy-done.186, ...), dimensions={0} | concatenate | bytes 1609728
  1614.7 48.5 %concatenate.32 = f32[1000,262]{0,1:T(8,128)} concatenate(f32[1000,6]{0,1:T(8,128)} %copy-done.123, f32[1000,8]{0,1:T(8,128)} %collective-permute-done.38, f32[1000,8]{0,1:T(8,128)} %collective-permute-done.37, f32[1000,8]{0,1:T(8,128)} %collective-permute-done.36, f32[1000,8]{0,1:T(8,128)} %copy-done.149, f32[1000,8]{0,1:T(8,128)} %copy-done.148, f32[1000,8]{0,1:T(8,128)} %copy-done.147, ...), dimensions={1} | concatenate | bytes 2096000
  1686.2 54.1 %concatenate.34 = f32[262,2304]{1,0:T(8,128)} concatenate(f32[6,2304]{1,0:T(8,128)} %copy-done.73, f32[8,2304]{1,0:T(8,128)} %copy-done.76, f32[8,2304]{1,0:T(8,128)} %copy-done.75, f32[8,2304]{1,0:T(8,128)} %copy-done.74, f32[8,2304]{1,0:T(8,128)} %copy-done.102, f32[8,2304]{1,0:T(8,128)} %copy-done.101, f32[8,2304]{1,0:T(8,128)} %collective-permute-done.97, ...), dimensions={0} | concatenate | bytes 4829184
  1752.7 56.1 %concatenate.36 = f32[262,3072]{1,0:T(8,128)} concatenate(f32[6,3072]{1,0:T(8,128)} %copy-done.34, f32[8,3072]{1,0:T(8,128)} %copy-done.65, f32[8,3072]{1,0:T(8,128)} %copy-done.64, f32[8,3072]{1,0:T(8,128)} %copy-done.63, f32[8,3072]{1,0:T(8,128)} %copy-done.62, f32[8,3072]{1,0:T(8,128)} %copy-done.61, f32[8,3072]{1,0:T(8,128)} %copy-done.60, f32[8,3072]{1,0:T(8,128)} %copy-done.59, ...), dimensions={0} | concatenate | bytes 6438912
  1826.6 102.5 %concatenate.33 = f32[262,4608]{1,0:T(8,128)} concatenate(f32[6,4608]{1,0:T(8,128)} %copy-done.28, f32[8,4608]{1,0:T(8,128)} %collective-permute-done.70, f32[8,4608]{1,0:T(8,128)} %collective-permute-done.69, f32[8,4608]{1,0:T(8,128)} %collective-permute-done.68, f32[8,4608]{1,0:T(8,128)} %collective-permute-done.67, f32[8,4608]{1,0:T(8,128)} %collective-permute-done.66, ...), dimensions={0} | concatenate | bytes 9658368
  1930.7 45.8 %reduce-scatter.17.cloned.1.call-done = f32[24,768]{1,0:T(8,128)} async-done(((f32[3072,768]{1,0:T(8,128)}), f32[24,768]{1,0:T(8,128)}) %reduce-scatter.17.cloned.1.call-update) | async-done | bytes 73744 | tf_op jit(solution)/shard_map/reduce_scatter | solution.py:304
  (881 shorter events, 568.5 us)
Async XLA Ops:
  7.2 89.5 %all-gather.2.cloned.1.call-start = ((), (), s32[]{:S(2)}) async-start(), calls=%async_computation.1 | async-start | bytes 7864320 | tf_op jit(solution)/shard_map/all_gather | solution.py:180
  42.2 479.7 %all-reduce.31.cloned.1.call-start = ((), (), s32[]{:S(2)}) async-start(), calls=%async_computation.3 | async-start | bytes 12582912
  388.3 1176.3 %all-reduce.33.cloned.1.call-start = ((), (), s32[]{:S(2)}) async-start(), calls=%async_computation.4 | async-start | bytes 393216
  392.5 1282.1 %all-reduce.35.cloned.1.call-start = ((), (), s32[]{:S(2)}) async-start(), calls=%async_computation.5 | async-start | bytes 229376
  591.4 1385.1 %reduce-scatter.17.cloned.1.call-start = ((), (), s32[]{:S(2)}) async-start(), calls=%async_computation.2 | async-start | bytes 9510912 | tf_op jit(solution)/shard_map/reduce_scatter | solution.py:304
  1160.2 20.1 %collective-permute-start.135 = (f32[6,768]{1,0:T(8,128)S(1)}, f32[6,768]{1,0:T(8,128)S(1)}, u32[]{:S(2)}, u32[]{:S(2)}) collective-permute-start(f32[6,768]{1,0:T(8,128)S(1)} %slice.422), channel_id=1, source_target_pairs={{0,32},{1,33},{2,34},{3,35},{4,36},{5,37},{6,38},{7,39},{8,40},{9,... | collective-permute-start | bytes 55304
  1162.2 21.2 %collective-permute-start.39 = (f32[1000,6]{0,1:T(8,128)S(1)}, f32[1000,6]{0,1:T(8,128)S(1)}, u32[]{:S(2)}, u32[]{:S(2)}) collective-permute-start(f32[1000,6]{0,1:T(8,128)S(1)} %slice.419), channel_id=1, source_target_pairs={{0,32},{1,33},{2,34},{3,35},{4,36},{5,37},{6,38},{7,39},{8,40},{9,... | collective-permute-start | bytes 72008
  1165.3 19.4 collective-permute-start.104
  1166.6 22.0 %collective-permute-start.105 = (f32[8,768]{1,0:T(8,128)}, f32[8,768]{1,0:T(8,128)S(1)}, u32[]{:S(2)}, u32[]{:S(2)}) collective-permute-start(f32[8,768]{1,0:T(8,128)} %get-tuple-element.147), channel_id=1, source_target_pairs={{0,2},{1,3},{2,4},{3,5},{4,6},{5,7},{6,8},{7,9},{8,10},{9,11},{10,... | collective-permute-start | bytes 73736
  1172.2 22.7 %collective-permute-start.106 = (f32[8,768]{1,0:T(8,128)}, f32[8,768]{1,0:T(8,128)S(1)}, u32[]{:S(2)}, u32[]{:S(2)}) collective-permute-start(f32[8,768]{1,0:T(8,128)} %get-tuple-element.147), channel_id=1, source_target_pairs={{0,3},{1,4},{2,5},{3,6},{4,7},{5,8},{6,9},{7,10},{8,11},{9,12},{10... | collective-permute-start | bytes 73736
  1183.4 19.2 collective-permute-start.108
  1184.7 24.9 %collective-permute-start.109 = (f32[8,768]{1,0:T(8,128)}, f32[8,768]{1,0:T(8,128)S(1)}, u32[]{:S(2)}, u32[]{:S(2)}) collective-permute-start(f32[8,768]{1,0:T(8,128)} %get-tuple-element.147), channel_id=1, source_target_pairs={{0,6},{1,7},{2,8},{3,9},{4,10},{5,11},{6,12},{7,13},{8,14},{9,15},... | collective-permute-start | bytes 73736
  1188.6 25.7 %collective-permute-start.110 = (f32[8,768]{1,0:T(8,128)}, f32[8,768]{1,0:T(8,128)S(1)}, u32[]{:S(2)}, u32[]{:S(2)}) collective-permute-start(f32[8,768]{1,0:T(8,128)} %get-tuple-element.147), channel_id=1, source_target_pairs={{0,7},{1,8},{2,9},{3,10},{4,11},{5,12},{6,13},{7,14},{8,15},{9,16}... | collective-permute-start | bytes 73736
  1194.9 24.3 %collective-permute-start.111 = (f32[8,768]{1,0:T(8,128)}, f32[8,768]{1,0:T(8,128)S(1)}, u32[]{:S(2)}, u32[]{:S(2)}) collective-permute-start(f32[8,768]{1,0:T(8,128)} %get-tuple-element.147), channel_id=1, source_target_pairs={{0,8},{1,9},{2,10},{3,11},{4,12},{5,13},{6,14},{7,15},{8,16},{9,17... | collective-permute-start | bytes 73736
  1198.3 22.2 %collective-permute-start.112 = (f32[8,768]{1,0:T(8,128)}, f32[8,768]{1,0:T(8,128)S(1)}, u32[]{:S(2)}, u32[]{:S(2)}) collective-permute-start(f32[8,768]{1,0:T(8,128)} %get-tuple-element.147), channel_id=1, source_target_pairs={{0,9},{1,10},{2,11},{3,12},{4,13},{5,14},{6,15},{7,16},{8,17},{9,1... | collective-permute-start | bytes 73736
  1202.6 19.6 collective-permute-start.113
  1264.8 20.4 %collective-permute-start.13 = (f32[1000,8]{0,1:T(8,128)}, f32[1000,8]{0,1:T(8,128)S(1)}, u32[]{:S(2)}, u32[]{:S(2)}) collective-permute-start(f32[1000,8]{0,1:T(8,128)} %get-tuple-element.144), channel_id=1, source_target_pairs={{0,6},{1,7},{2,8},{3,9},{4,10},{5,11},{6,12},{7,13},{8,14},{9,15},... | collective-permute-start | bytes 96008
  1268.6 19.9 %collective-permute-start.14 = (f32[1000,8]{0,1:T(8,128)}, f32[1000,8]{0,1:T(8,128)S(1)}, u32[]{:S(2)}, u32[]{:S(2)}) collective-permute-start(f32[1000,8]{0,1:T(8,128)} %get-tuple-element.144), channel_id=1, source_target_pairs={{0,7},{1,8},{2,9},{3,10},{4,11},{5,12},{6,13},{7,14},{8,15},{9,16}... | collective-permute-start | bytes 96008
  1362.3 21.2 %collective-permute-start.77 = (f32[8,2304]{1,0:T(8,128)}, f32[8,2304]{1,0:T(8,128)S(1)}, u32[]{:S(2)}, u32[]{:S(2)}) collective-permute-start(f32[8,2304]{1,0:T(8,128)} %get-tuple-element.146), channel_id=1, source_target_pairs={{0,6},{1,7},{2,8},{3,9},{4,10},{5,11},{6,12},{7,13},{8,14},{9,15},... | collective-permute-start | bytes 221192
  1422.5 20.7 %collective-permute-start.138 = (f32[8,3072]{1,0:T(8,128)}, f32[8,3072]{1,0:T(8,128)S(1)}, u32[]{:S(2)}, u32[]{:S(2)}) collective-permute-start(f32[8,3072]{1,0:T(8,128)} %get-tuple-element.148), channel_id=1, source_target_pairs={{0,3},{1,4},{2,5},{3,6},{4,7},{5,8},{6,9},{7,10},{8,11},{9,12},{10... | collective-permute-start | bytes 294920
  1432.4 20.2 %collective-permute-start.140 = (f32[8,3072]{1,0:T(8,128)}, f32[8,3072]{1,0:T(8,128)S(1)}, u32[]{:S(2)}, u32[]{:S(2)}) collective-permute-start(f32[8,3072]{1,0:T(8,128)} %get-tuple-element.148), channel_id=1, source_target_pairs={{0,5},{1,6},{2,7},{3,8},{4,9},{5,10},{6,11},{7,12},{8,13},{9,14},{... | collective-permute-start | bytes 294920
  1433.7 24.1 %collective-permute-start.141 = (f32[8,3072]{1,0:T(8,128)}, f32[8,3072]{1,0:T(8,128)S(1)}, u32[]{:S(2)}, u32[]{:S(2)}) collective-permute-start(f32[8,3072]{1,0:T(8,128)} %get-tuple-element.148), channel_id=1, source_target_pairs={{0,6},{1,7},{2,8},{3,9},{4,10},{5,11},{6,12},{7,13},{8,14},{9,15},... | collective-permute-start | bytes 294920
  1437.4 26.5 %collective-permute-start.142 = (f32[8,3072]{1,0:T(8,128)}, f32[8,3072]{1,0:T(8,128)S(1)}, u32[]{:S(2)}, u32[]{:S(2)}) collective-permute-start(f32[8,3072]{1,0:T(8,128)} %get-tuple-element.148), channel_id=1, source_target_pairs={{0,7},{1,8},{2,9},{3,10},{4,11},{5,12},{6,13},{7,14},{8,15},{9,16}... | collective-permute-start | bytes 294920
  1443.1 22.8 %collective-permute-start.143 = (f32[8,3072]{1,0:T(8,128)}, f32[8,3072]{1,0:T(8,128)S(1)}, u32[]{:S(2)}, u32[]{:S(2)}) collective-permute-start(f32[8,3072]{1,0:T(8,128)} %get-tuple-element.148), channel_id=1, source_target_pairs={{0,8},{1,9},{2,10},{3,11},{4,12},{5,13},{6,14},{7,15},{8,16},{9,17... | collective-permute-start | bytes 294920
  1497.2 26.4 %collective-permute-start.40 = (f32[8,4608]{1,0:T(8,128)}, f32[8,4608]{1,0:T(8,128)}, u32[]{:S(2)}, u32[]{:S(2)}) collective-permute-start(f32[8,4608]{1,0:T(8,128)} %get-tuple-element.145), channel_id=1, source_target_pairs={{0,1},{1,2},{2,3},{3,4},{4,5},{5,6},{6,7},{7,8},{8,9},{9,10},{10,1... | collective-permute-start | bytes 442376
  1500.2 20.8 %collective-permute-start.71 = (f32[6,4608]{1,0:T(8,128)S(1)}, f32[6,4608]{1,0:T(8,128)S(1)}, u32[]{:S(2)}, u32[]{:S(2)}) collective-permute-start(f32[6,4608]{1,0:T(8,128)S(1)} %slice.420), channel_id=1, source_target_pairs={{0,32},{1,33},{2,34},{3,35},{4,36},{5,37},{6,38},{7,39},{8,40},{9,... | collective-permute-start | bytes 331784
  1518.0 20.8 %collective-permute-start.43 = (f32[8,4608]{1,0:T(8,128)}, f32[8,4608]{1,0:T(8,128)}, u32[]{:S(2)}, u32[]{:S(2)}) collective-permute-start(f32[8,4608]{1,0:T(8,128)} %get-tuple-element.145), channel_id=1, source_target_pairs={{0,4},{1,5},{2,6},{3,7},{4,8},{5,9},{6,10},{7,11},{8,12},{9,13},{1... | collective-permute-start | bytes 442376
  1521.7 19.3 collective-permute-start.44
  1523.6 25.0 %collective-permute-start.45 = (f32[8,4608]{1,0:T(8,128)}, f32[8,4608]{1,0:T(8,128)}, u32[]{:S(2)}, u32[]{:S(2)}) collective-permute-start(f32[8,4608]{1,0:T(8,128)} %get-tuple-element.145), channel_id=1, source_target_pairs={{0,6},{1,7},{2,8},{3,9},{4,10},{5,11},{6,12},{7,13},{8,14},{9,15},... | collective-permute-start | bytes 442376
  1529.1 23.3 %collective-permute-start.46 = (f32[8,4608]{1,0:T(8,128)}, f32[8,4608]{1,0:T(8,128)}, u32[]{:S(2)}, u32[]{:S(2)}) collective-permute-start(f32[8,4608]{1,0:T(8,128)} %get-tuple-element.145), channel_id=1, source_target_pairs={{0,7},{1,8},{2,9},{3,10},{4,11},{5,12},{6,13},{7,14},{8,15},{9,16}... | collective-permute-start | bytes 442376
  1532.0 24.8 %collective-permute-start.47 = (f32[8,4608]{1,0:T(8,128)}, f32[8,4608]{1,0:T(8,128)}, u32[]{:S(2)}, u32[]{:S(2)}) collective-permute-start(f32[8,4608]{1,0:T(8,128)} %get-tuple-element.145), channel_id=1, source_target_pairs={{0,8},{1,9},{2,10},{3,11},{4,12},{5,13},{6,14},{7,15},{8,16},{9,17... | collective-permute-start | bytes 442376
  1538.8 20.0 %collective-permute-start.48 = (f32[8,4608]{1,0:T(8,128)}, f32[8,4608]{1,0:T(8,128)}, u32[]{:S(2)}, u32[]{:S(2)}) collective-permute-start(f32[8,4608]{1,0:T(8,128)} %get-tuple-element.145), channel_id=1, source_target_pairs={{0,9},{1,10},{2,11},{3,12},{4,13},{5,14},{6,15},{7,16},{8,17},{9,1... | collective-permute-start | bytes 442376
  1541.0 19.7 collective-permute-start.49
  1552.4 110.8 %collective-permute-start.51 = (f32[8,4608]{1,0:T(8,128)}, f32[8,4608]{1,0:T(8,128)}, u32[]{:S(2)}, u32[]{:S(2)}) collective-permute-start(f32[8,4608]{1,0:T(8,128)} %get-tuple-element.145), channel_id=1, source_target_pairs={{0,12},{1,13},{2,14},{3,15},{4,16},{5,17},{6,18},{7,19},{8,20},{9,... | collective-permute-start | bytes 442376
  1556.9 108.3 %collective-permute-start.52 = (f32[8,4608]{1,0:T(8,128)}, f32[8,4608]{1,0:T(8,128)}, u32[]{:S(2)}, u32[]{:S(2)}) collective-permute-start(f32[8,4608]{1,0:T(8,128)} %get-tuple-element.145), channel_id=1, source_target_pairs={{0,13},{1,14},{2,15},{3,16},{4,17},{5,18},{6,19},{7,20},{8,21},{9,... | collective-permute-start | bytes 442376
  1558.8 108.3 %collective-permute-start.53 = (f32[8,4608]{1,0:T(8,128)}, f32[8,4608]{1,0:T(8,128)}, u32[]{:S(2)}, u32[]{:S(2)}) collective-permute-start(f32[8,4608]{1,0:T(8,128)} %get-tuple-element.145), channel_id=1, source_target_pairs={{0,14},{1,15},{2,16},{3,17},{4,18},{5,19},{6,20},{7,21},{8,22},{9,... | collective-permute-start | bytes 442376
  1560.8 108.3 %collective-permute-start.54 = (f32[8,4608]{1,0:T(8,128)}, f32[8,4608]{1,0:T(8,128)}, u32[]{:S(2)}, u32[]{:S(2)}) collective-permute-start(f32[8,4608]{1,0:T(8,128)} %get-tuple-element.145), channel_id=1, source_target_pairs={{0,15},{1,16},{2,17},{3,18},{4,19},{5,20},{6,21},{7,22},{8,23},{9,... | collective-permute-start | bytes 442376
  1562.7 108.3 %collective-permute-start.55 = (f32[8,4608]{1,0:T(8,128)}, f32[8,4608]{1,0:T(8,128)}, u32[]{:S(2)}, u32[]{:S(2)}) collective-permute-start(f32[8,4608]{1,0:T(8,128)} %get-tuple-element.145), channel_id=1, source_target_pairs={{0,16},{1,17},{2,18},{3,19},{4,20},{5,21},{6,22},{7,23},{8,24},{9,... | collective-permute-start | bytes 442376
  1663.2 77.1 %collective-permute-start.56 = (f32[8,4608]{1,0:T(8,128)}, f32[8,4608]{1,0:T(8,128)}, u32[]{:S(2)}, u32[]{:S(2)}) collective-permute-start(f32[8,4608]{1,0:T(8,128)} %get-tuple-element.145), channel_id=1, source_target_pairs={{0,17},{1,18},{2,19},{3,20},{4,21},{5,22},{6,23},{7,24},{8,25},{9,... | collective-permute-start | bytes 442376
  1665.1 77.1 %collective-permute-start.57 = (f32[8,4608]{1,0:T(8,128)}, f32[8,4608]{1,0:T(8,128)}, u32[]{:S(2)}, u32[]{:S(2)}) collective-permute-start(f32[8,4608]{1,0:T(8,128)} %get-tuple-element.145), channel_id=1, source_target_pairs={{0,18},{1,19},{2,20},{3,21},{4,22},{5,23},{6,24},{7,25},{8,26},{9,... | collective-permute-start | bytes 442376
  1667.1 77.1 %collective-permute-start.58 = (f32[8,4608]{1,0:T(8,128)}, f32[8,4608]{1,0:T(8,128)}, u32[]{:S(2)}, u32[]{:S(2)}) collective-permute-start(f32[8,4608]{1,0:T(8,128)} %get-tuple-element.145), channel_id=1, source_target_pairs={{0,19},{1,20},{2,21},{3,22},{4,23},{5,24},{6,25},{7,26},{8,27},{9,... | collective-permute-start | bytes 442376
  1669.0 77.1 %collective-permute-start.59 = (f32[8,4608]{1,0:T(8,128)}, f32[8,4608]{1,0:T(8,128)}, u32[]{:S(2)}, u32[]{:S(2)}) collective-permute-start(f32[8,4608]{1,0:T(8,128)} %get-tuple-element.145), channel_id=1, source_target_pairs={{0,20},{1,21},{2,22},{3,23},{4,24},{5,25},{6,26},{7,27},{8,28},{9,... | collective-permute-start | bytes 442376
  1671.0 77.1 %collective-permute-start.60 = (f32[8,4608]{1,0:T(8,128)}, f32[8,4608]{1,0:T(8,128)}, u32[]{:S(2)}, u32[]{:S(2)}) collective-permute-start(f32[8,4608]{1,0:T(8,128)} %get-tuple-element.145), channel_id=1, source_target_pairs={{0,21},{1,22},{2,23},{3,24},{4,25},{5,26},{6,27},{7,28},{8,29},{9,... | collective-permute-start | bytes 442376
  1740.3 68.5 %collective-permute-start.61 = (f32[8,4608]{1,0:T(8,128)}, f32[8,4608]{1,0:T(8,128)}, u32[]{:S(2)}, u32[]{:S(2)}) collective-permute-start(f32[8,4608]{1,0:T(8,128)} %get-tuple-element.145), channel_id=1, source_target_pairs={{0,22},{1,23},{2,24},{3,25},{4,26},{5,27},{6,28},{7,29},{8,30},{9,... | collective-permute-start | bytes 442376
  1742.2 68.5 %collective-permute-start.62 = (f32[8,4608]{1,0:T(8,128)}, f32[8,4608]{1,0:T(8,128)}, u32[]{:S(2)}, u32[]{:S(2)}) collective-permute-start(f32[8,4608]{1,0:T(8,128)} %get-tuple-element.145), channel_id=1, source_target_pairs={{0,23},{1,24},{2,25},{3,26},{4,27},{5,28},{6,29},{7,30},{8,31},{9,... | collective-permute-start | bytes 442376
  1744.2 68.6 %collective-permute-start.63 = (f32[8,4608]{1,0:T(8,128)}, f32[8,4608]{1,0:T(8,128)}, u32[]{:S(2)}, u32[]{:S(2)}) collective-permute-start(f32[8,4608]{1,0:T(8,128)} %get-tuple-element.145), channel_id=1, source_target_pairs={{0,24},{1,25},{2,26},{3,27},{4,28},{5,29},{6,30},{7,31},{8,32},{9,... | collective-permute-start | bytes 442376
  1746.1 68.6 %collective-permute-start.64 = (f32[8,4608]{1,0:T(8,128)}, f32[8,4608]{1,0:T(8,128)}, u32[]{:S(2)}, u32[]{:S(2)}) collective-permute-start(f32[8,4608]{1,0:T(8,128)} %get-tuple-element.145), channel_id=1, source_target_pairs={{0,25},{1,26},{2,27},{3,28},{4,29},{5,30},{6,31},{7,32},{8,33},{9,... | collective-permute-start | bytes 442376
  1748.1 68.6 %collective-permute-start.65 = (f32[8,4608]{1,0:T(8,128)}, f32[8,4608]{1,0:T(8,128)}, u32[]{:S(2)}, u32[]{:S(2)}) collective-permute-start(f32[8,4608]{1,0:T(8,128)} %get-tuple-element.145), channel_id=1, source_target_pairs={{0,26},{1,27},{2,28},{3,29},{4,30},{5,31},{6,32},{7,33},{8,34},{9,... | collective-permute-start | bytes 442376
  (335 other events, 7700.9 us)
Sparse Core Ops, SparseCore 0:
  42.3 54.3 all-gather.1
  388.4 133.4 all-reduce.30
  526.6 640.8 all-reduce.32
  1175.4 141.3 all-reduce.34
  1319.6 656.8 reduce-scatter.16
where the time goes:
time: 2010 us; the launch traced here: 1980 us
  blocking collectives  548 us (27%)
  local copies, waits for them, and re-layouts  527 us (26%)
  starting transfers between devices  446 us (22%)
  waiting for transfers between devices  208 us (10%)
  matrix products  145 us (7%)
  other arithmetic  89.5 us (4%)
  between operations  20.3 us (1%)
    unnamed x1, blocking collectives  532 us
    unnamed x163, starting transfers between devices  425 us
    unnamed x454, local copies, waits for them, and re-layouts  348 us
    unnamed x168, waiting for transfers between devices  114 us
    another operation x8, local copies, waits for them, and re-layouts, split_heads(): return values.reshape(slot_count, 4, -1, HEADS, head_dim)  56.5 us
    dot_general x4, matrix products, project_back(): jnp.einsum('srwd,cd->srwc', values, matrix, preferred_element_type=jnp.fl...  54.1 us
    reduce_scatter x1, waiting for transfers between devices, local(): lax.psum_scatter(fc2_grad, ('dp', 'seq'), scatter_dimension=0, tiled=True)  45.8 us
  transfers between devices with their start and end apart: 173, of which 8 were waited for; matrix products, arithmetic and copies ran while one was open for 50% of the time, Pallas kernels for 0%

commit v1 on v0

v1 whole, which is shorter than its diff:
```python
import functools

import jax
import jax.numpy as jnp
import numpy as np
from jax import lax
from jax.experimental import pallas as pl
from jax.experimental.pallas import tpu as pltpu
from jax.sharding import PartitionSpec as P

F32 = jnp.float32
BF16 = jnp.bfloat16
D = 768
FF = 3072
FC = 768
NFC = FF // FC
EPS = 1e-6


def mm(a, b):
    return lax.dot_general(a, b, (((1,), (0,)), ((), ())), preferred_element_type=F32)


def mm_nt(a, b):
    return lax.dot_general(a, b, (((1,), (1,)), ((), ())), preferred_element_type=F32)


def mm_tn(a, b):
    return lax.dot_general(a, b, (((0,), (0,)), ((), ())), preferred_element_type=F32)


def fold8(v):
    total = v[0:8]
    for at in range(8, v.shape[0], 8):
        total = total + v[at : at + 8]
    return total


def norm_parts(v):
    center = v - jnp.mean(v, axis=-1, keepdims=True)
    rs = lax.rsqrt(jnp.mean(center * center, axis=-1, keepdims=True) + EPS)
    return center * rs, rs


def by_core(taps, at, core):
    return jnp.where(core == 1, taps[3 * (2 - at // 3) + at % 3], taps[at])


def gelu_pair(v):
    z = jnp.abs(v) * 0.7071067811865476
    t = 1.0 / (1.0 + 0.3275911 * z)
    e = jnp.exp(-0.5 * (v * v))
    poly = t * (
        0.127414796
        + t * (-0.142248368 + t * (0.7107068705 + t * (-0.7265760135 + t * 0.5307027145)))
    )
    tail = poly * e
    cdf = jnp.where(v >= 0, 1.0 - tail, tail)
    return v * cdf, cdf + v * (e * 0.3989422804014327)


def side_masks():
    place = lax.broadcasted_iota(jnp.int32, (16, 128), 0)
    return place == 0, place == 15


def with_sides(even, odd, masks):
    left = jnp.where(masks[0], 0.0, pltpu.roll(odd, 1, 0))
    right = jnp.where(masks[1], 0.0, pltpu.roll(even, 15, 0))
    return even, odd, left, right


def conv_row(rows, taps):
    even = odd = None
    for a in range(3):
        if rows[a] is None:
            continue
        ev, od, left, right = rows[a]
        for tap, ce, co in ((3 * a, left, ev), (3 * a + 1, ev, od), (3 * a + 2, od, right)):
            even = taps[tap] * ce if even is None else even + taps[tap] * ce
            odd = taps[tap] * co if odd is None else odd + taps[tap] * co
    return even, odd


def tap_products(sums, rows, d_even, d_odd):
    for a in range(3):
        if rows[a] is None:
            continue
        ev, od, left, right = rows[a]
        for tap, ce, co in ((3 * a, left, ev), (3 * a + 1, ev, od), (3 * a + 2, od, right)):
            term = fold8(d_even * ce + d_odd * co)
            sums[tap] = term if sums[tap] is None else sums[tap] + term


def ffn_kernel(
    x_ref, at_ref, ct_ref, mod_ref, alive_ref, perm_ref, ow_ref, ob_ref, f1_ref, f1b_ref,
    tap_ref, cb_ref, f2_ref, f2b_ref,
    out_ref, fg_ref, go_ref, da_ref, dx_ref, s2_ref, sm_ref,
    x1_s, br_s, h2_s, h2t_s, dffn_s, u_s, duc_s, act_s, du_s, dact_s, ffn_s, dh2_s, acc_s,
    fg_s, fg_sem,
):
    step = pl.program_id(0)
    core = lax.axis_index("seq") % 2
    alive = alive_ref[0]

    @pl.when(step == 0)
    def _():
        br_s[...] = mm(at_ref[...], ow_ref[...]) + ob_ref[...].astype(F32)
        shift2, scale2, gate1, gate2 = (mod_ref[i : i + 1, :] for i in (3, 4, 2, 5))

        def rows_a(r, _):
            at = pl.ds(pl.multiple_of(r * 32, 32), 32)
            x1 = x_ref[at, :].astype(F32) + gate1 * br_s[at, :]
            x1_s[at, :] = x1
            n2, _unused = norm_parts(x1)
            h2_s[at, :] = (n2 * (1.0 + scale2) + shift2).astype(BF16)
            return 0

        lax.fori_loop(0, 18, rows_a, 0)

        def rows_b(r, _):
            at = pl.ds(pl.multiple_of(r * 32, 32), 32)
            dffn_s[at, :] = (ct_ref[at, :].astype(F32) * alive * gate2).astype(BF16)
            return 0

        lax.fori_loop(0, 17, rows_b, 0)
        for p in range(3):
            h2t_s[p] = mm_nt(perm_ref[p], h2_s[0:512, :]).astype(BF16)
        ffn_s[...] = jnp.zeros_like(ffn_s)
        dh2_s[...] = jnp.zeros_like(dh2_s)

    for j in range(3):
        cols = slice(256 * j, 256 * j + 256)
        u_s[:, cols] = (mm(h2_s[...], f1_ref[:, cols]) + f1b_ref[:, cols].astype(F32)).astype(BF16)
        dact_s[:, cols] = mm_nt(dffn_s[...], f2_ref[cols, :])

    masks = side_masks()

    def lanes(j, _):
        cols = pl.ds(pl.multiple_of(j * 128, 128), 128)
        taps = [tap_ref[t : t + 1, cols] for t in range(9)]
        taps = [by_core(taps, t, core) for t in range(9)]
        offset = cb_ref[:, cols].astype(F32)

        def sided(ref, l):
            return with_sides(
                ref[32 * l : 32 * l + 16, cols].astype(F32),
                ref[32 * l + 16 : 32 * l + 32, cols].astype(F32),
                masks,
            )

        rows = [None, sided(u_s, 0), sided(u_s, 1)]
        sums = [None] * 9
        bias_sum = None
        for l in range(17):
            ce, co = conv_row(rows, taps)
            ae, ge = gelu_pair(ce + offset)
            ao, go = gelu_pair(co + offset)
            de = (ge * dact_s[32 * l : 32 * l + 16, cols]).astype(BF16)
            do = (go * dact_s[32 * l + 16 : 32 * l + 32, cols]).astype(BF16)
            duc_s[32 * l : 32 * l + 16, cols] = de
            duc_s[32 * l + 16 : 32 * l + 32, cols] = do
            if l < 16:
                act_s[32 * l : 32 * l + 16, cols] = ae.astype(BF16)
                act_s[32 * l + 16 : 32 * l + 32, cols] = ao.astype(BF16)
                de, do = de.astype(F32), do.astype(F32)
                tap_products(sums, rows, de, do)
                term = fold8(de + do)
                bias_sum = term if bias_sum is None else bias_sum + term
                rows = [rows[1], rows[2], sided(u_s, l + 2) if l + 2 < 18 else None]
        for t in range(9):
            s2_ref[t : t + 1, cols] = jnp.sum(by_core(sums, t, core), axis=0, keepdims=True)
        s2_ref[9:10, cols] = jnp.sum(bias_sum, axis=0, keepdims=True)
        back = [taps[8 - t] for t in range(9)]
        rows = [None, sided(duc_s, 0), sided(duc_s, 1)]
        bias_sum = None
        for l in range(16):
            ue, uo = conv_row(rows, back)
            ue, uo = ue.astype(BF16), uo.astype(BF16)
            du_s[32 * l : 32 * l + 16, cols] = ue
            du_s[32 * l + 16 : 32 * l + 32, cols] = uo
            term = fold8(ue.astype(F32) + uo.astype(F32))
            bias_sum = term if bias_sum is None else bias_sum + term
            rows = [rows[1], rows[2], sided(duc_s, l + 2) if l + 2 < 17 else None]
        s2_ref[10:11, cols] = jnp.sum(bias_sum, axis=0, keepdims=True)
        return 0

    lax.fori_loop(0, FC // 128, lanes, 0)

    ffn_s[...] += mm(act_s[...], f2_ref[...])
    dh2_s[...] += mm_nt(du_s[...], f1_ref[...])
    for j in range(3):
        cols = slice(256 * j, 256 * j + 256)
        fg_s[0, j, step] = mm(h2t_s[j], du_s[:, cols]).astype(BF16).reshape(4, 4, 48, 256)
    for part in range(3):
        grad = mm_tn(act_s[...], dffn_s[0:512, 256 * part : 256 * part + 256]).astype(BF16)
        for zl in range(2):
            for y in range(4):
                for zh in range(2):
                    at = ((zl * 4 + y) * 2 + zh) * 48
                    z = zh * 2 + zl
                    rows = grad[at : at + 48, :]
                    if part == 0:
                        fg_s[1, 0, z, step, y] = rows
                    elif part == 1:
                        fg_s[1, 1, step, y, z] = rows
                    else:
                        fg_s[1, 2, y, z, step] = rows

    def moved(at, i):
        spots = (
            lambda ref: ref.at[0, :, at],
            lambda ref: ref.at[1, 0, :, at],
            lambda ref: ref.at[1, 1, at],
            lambda ref: ref.at[1, 2, :, :, at],
        )
        return pltpu.make_async_copy(spots[i](fg_s), spots[i](fg_ref), fg_sem.at[at, i])

    for i in range(4):
        moved(step, i).start()

    @pl.when(step == NFC - 1)
    def _():
        shift2, scale2, gate1, gate2 = (mod_ref[i : i + 1, :] for i in (3, 4, 2, 5))
        acc_s[...] = jnp.zeros_like(acc_s)
        f2b = f2b_ref[...].astype(F32)

        def rows_c(r, _):
            at = pl.ds(pl.multiple_of(r * 32, 32), 32)
            x1 = x1_s[at, :]
            ffn = ffn_s[at, :] + f2b
            dy = ct_ref[at, :].astype(F32) * alive
            out_ref[at, :] = (alive * (x1 + gate2 * ffn)).astype(BF16)
            n2, rs = norm_parts(x1)
            dh2 = dh2_s[at, :]
            g2 = dh2 * (1.0 + scale2)
            dx1 = dy + rs * (
                g2
                - jnp.mean(g2, axis=-1, keepdims=True)
                - n2 * jnp.mean(g2 * n2, axis=-1, keepdims=True)
            )
            dx_ref[at, :] = dx1
            dbr = (dx1 * gate1).astype(BF16)
            da_ref[at, :] = dbr
            acc_s[0] += fold8(dx1 * br_s[at, :])
            acc_s[1] += fold8(dh2)
            acc_s[2] += fold8(dh2 * n2)
            acc_s[3] += fold8(dy * ffn)
            acc_s[4] += fold8(dbr.astype(F32))
            acc_s[5] += fold8(dffn_s[at, :].astype(F32))
            return 0

        lax.fori_loop(0, 16, rows_c, 0)
        for i in range(6):
            sm_ref[i : i + 1, :] = jnp.sum(acc_s[i], axis=0, keepdims=True)
        for p in range(3):
            h2t_s[p] = mm_nt(perm_ref[p], at_ref[0:512, :]).astype(BF16)
            go_ref[p] = mm(h2t_s[p], da_ref[:, 256 * p : 256 * p + 256]).astype(BF16)
        da_ref[...] = mm_nt(da_ref[...], ow_ref[...]).astype(BF16)
        for at in range(NFC):
            for i in range(4):
                moved(at, i).wait()


def ffn_call(x, at, ct, mod, alive, perm, ow, ob, f1, f1b, taps, cb, f2, f2b):
    whole = lambda s: pl.BlockSpec(s, lambda i: (0,) * len(s))
    return pl.pallas_call(
        ffn_kernel,
        grid=(NFC,),
        in_specs=[
            whole((576, D)), whole((576, D)), whole((576, D)), whole((8, D)),
            pl.BlockSpec(memory_space=pltpu.SMEM),
            whole((3, D, D)), whole((D, D)), whole((1, D)),
            pl.BlockSpec((D, FC), lambda i: (0, i)),
            pl.BlockSpec((1, FC), lambda i: (0, i)),
            pl.BlockSpec((16, FC), lambda i: (0, i)),
            pl.BlockSpec((1, FC), lambda i: (0, i)),
            pl.BlockSpec((FC, D), lambda i: (i, 0)),
            whole((1, D)),
        ],
        out_specs=[
            whole((512, D)),
            pl.BlockSpec(memory_space=pl.ANY),
            whole((3, D, 256)),
            whole((512, D)), whole((512, D)),
            pl.BlockSpec((16, FC), lambda i: (0, i)),
            whole((8, D)),
        ],
        out_shape=[
            jax.ShapeDtypeStruct((512, D), BF16),
            jax.ShapeDtypeStruct((2, 3, 4, 4, 4, 48, 256), BF16),
            jax.ShapeDtypeStruct((3, D, 256), BF16),
            jax.ShapeDtypeStruct((512, D), BF16),
            jax.ShapeDtypeStruct((512, D), F32),
            jax.ShapeDtypeStruct((16, FF), F32),
            jax.ShapeDtypeStruct((8, D), F32),
        ],
        scratch_shapes=[
            pltpu.VMEM((576, D), F32), pltpu.VMEM((576, D), F32), pltpu.VMEM((576, D), BF16),
            pltpu.VMEM((3, D, 512), BF16), pltpu.VMEM((544, D), BF16),
            pltpu.VMEM((576, FC), BF16), pltpu.VMEM((544, FC), BF16), pltpu.VMEM((512, FC), BF16),
            pltpu.VMEM((512, FC), BF16), pltpu.VMEM((544, FC), F32),
            pltpu.VMEM((512, D), F32), pltpu.VMEM((512, D), F32), pltpu.VMEM((6, 8, D), F32),
            pltpu.VMEM((2, 3, 4, 4, 4, 48, 256), BF16), pltpu.SemaphoreType.DMA((NFC, 4)),
        ],
        compiler_params=pltpu.CompilerParams(
            dimension_semantics=("arbitrary",), vmem_limit_bytes=60 * 2**20
        ),
        name="ffn",
    )(x, at, ct, mod, alive, perm, ow, ob, f1, f1b, taps, cb, f2, f2b)


MESH = pl.DeviceIdType.MESH


def spot():
    dp = lax.axis_index("dp")
    seq = lax.axis_index("seq")
    return dict(dp=dp, seq=seq, x=dp // 8, zl=(dp // 4) % 2, y=dp % 4, zh=seq // 2, core=seq % 2)


def seq_peer(me, zh, core):
    return (me["dp"], zh * 2 + core)


def axis_peer(me, axis, offset):
    x, y, z = me["x"], me["y"], me["zh"] * 2 + me["zl"]
    if axis == "x":
        x = (x + offset) % 4
    elif axis == "y":
        y = (y + offset) % 4
    else:
        z = (z + offset) % 4
    return ((x * 2 + z % 2) * 4 + y, (z // 2) * 2 + me["core"])


def remote(src, dst, send, recv, device):
    return pltpu.make_async_remote_copy(
        src_ref=src, dst_ref=dst, send_sem=send, recv_sem=recv, device_id=device,
        device_id_type=MESH,
    )


def arrived(ref, sem):
    pltpu.make_async_copy(ref, ref, sem).wait()


def place_matrix(count, flip, inverse):
    rows = count // 32
    out = lax.broadcasted_iota(jnp.int32, (count, count), 0)
    at = lax.broadcasted_iota(jnp.int32, (count, count), 1)
    row = out // 32
    row = jnp.where(flip, rows - 1 - row, row)
    low = out % 32
    if inverse:
        low = (low % 2) * 16 + low // 2
    else:
        low = (low % 16) * 2 + low // 16
    return jnp.where(at == row * 32 + low, 1.0, 0.0).astype(BF16)


def head_lanes(values, half):
    lane = lax.broadcasted_iota(jnp.int32, values.shape, 1)
    return jnp.where((lane // 64) == half, values, jnp.zeros_like(values))


def attn_kernel(
    lat_ref, ct_ref, mod_ref, w_ref, qb_ref, tap_ref, cb_ref,
    x_out, ct_out, h_out, hcg_out, qkv_out, p_out, at_out,
    xr_s, xh_s, x_s, c_s, h_s, hcg_s, sb_s, w_s, qkv_s, p_s, ag_s, at_s,
    send0, recv0, sem_pair, sem_loc,
):
    me = spot()
    zh, core, seq = me["zh"], me["core"], me["seq"]
    other = seq_peer(me, zh, 1 - core)
    w_load = pltpu.make_async_copy(w_ref, w_s, sem_loc.at[0])
    w_load.start()

    barrier = pltpu.get_barrier_semaphore()
    for dz, dc in ((0, 1), (1, 0), (1, 1)):
        pl.semaphore_signal(
            barrier, inc=1, device_id=seq_peer(me, (zh + dz) % 2, (core + dc) % 2),
            device_id_type=MESH,
        )
    pl.semaphore_wait(barrier, 3)

    slot = jnp.where(zh == 0, core, 1 - core)
    inner = jnp.logical_or(seq == 1, seq == 2)
    halo_core = jnp.where(seq == 1, 1, 0)
    halo_at = pl.multiple_of(jnp.where(seq == 1, 192, 0), 64)

    def sends(act):
        for a, ref in enumerate((lat_ref, ct_ref)):
            for j in range(2):
                own = jnp.logical_and(zh == j, core == zh)
                main = (ref.at[j], xr_s.at[a, slot])
                halo = (ref.at[j, pl.ds(halo_at, 64)], xh_s.at[a])

                @pl.when(own)
                def _():
                    act(lambda: pltpu.make_async_copy(*main, recv0.at[a, slot]), True)

                @pl.when(jnp.logical_not(own))
                def _():
                    act(
                        lambda: remote(*main, send0.at[a, j, 0], recv0.at[a, slot], seq_peer(me, j, zh)),
                        False,
                    )

                @pl.when(jnp.logical_and(inner, zh == j))
                def _():
                    act(lambda: pltpu.make_async_copy(*halo, recv0.at[a, 2]), True)

                @pl.when(jnp.logical_and(inner, zh != j))
                def _():
                    act(
                        lambda: remote(
                            *halo, send0.at[a, j, 1], recv0.at[a, 2], seq_peer(me, j, halo_core)
                        ),
                        False,
                    )

    sends(lambda make, local: make().start())

    flip = core == 1
    big = place_matrix(256, flip, False)
    small = place_matrix(64, flip, False)
    shift1, scale1 = mod_ref[0:1, :], mod_ref[1:2, :]

    def placed(a, into):
        for b in range(2):
            arrived(xr_s.at[a, b], recv0.at[a, b])
            into[256 * b : 256 * b + 256, :] = mm(big, xr_s[a, b]).astype(BF16)
        arrived(xh_s.at[a], recv0.at[a, 2])
        into[512:576, :] = mm(small, xh_s[a]).astype(BF16)

    placed(0, x_s)

    def rows_a(r, _):
        at = pl.ds(pl.multiple_of(r * 32, 32), 32)
        n1, _unused = norm_parts(x_s[at, :].astype(F32))
        h_s[at, :] = (n1 * (1.0 + scale1) + shift1).astype(BF16)
        return 0

    lax.fori_loop(0, 18, rows_a, 0)
    outs = [
        pltpu.make_async_copy(x_s, x_out, sem_loc.at[1]),
        pltpu.make_async_copy(h_s, h_out, sem_loc.at[2]),
    ]
    for copy in outs:
        copy.start()
    masks = side_masks()

    def lanes(j, _):
        cols = pl.ds(pl.multiple_of(j * 128, 128), 128)
        taps = [tap_ref[t : t + 1, cols] for t in range(9)]
        taps = [by_core(taps, t, core) for t in range(9)]
        offset = cb_ref[:, cols].astype(F32)

        def sided(l):
            return with_sides(
                h_s[32 * l : 32 * l + 16, cols].astype(F32),
                h_s[32 * l + 16 : 32 * l + 32, cols].astype(F32),
                masks,
            )

        rows = [None, sided(0), sided(1)]
        for l in range(16):
            ce, co = conv_row(rows, taps)
            ce, co = (ce + offset).astype(BF16), (co + offset).astype(BF16)
            if l % 2 == 0:
                hcg_s[0, l // 2, 0, :, cols] = ce
                hcg_s[0, l // 2, 1, :, cols] = co
            else:
                sb_s[l // 2, 0, :, cols] = ce
                sb_s[l // 2, 1, :, cols] = co
            rows = [rows[1], rows[2], sided(l + 2) if l < 15 else None]
        return 0

    lax.fori_loop(0, D // 128, lanes, 0)
    hc_copy = remote(sb_s, hcg_s.at[1], sem_pair.at[0], sem_pair.at[1], other)
    hc_copy.start()
    w_load.wait()

    def project(half):
        got = mm(hcg_s[half].reshape(256, D), w_s[...]) + qb_ref[...]
        qkv_s[half] = got.astype(BF16).reshape(8, 2, 16, 3 * D)

    project(0)
    hc_copy.wait()
    outs.append(pltpu.make_async_copy(hcg_s, hcg_out, sem_loc.at[3]))
    outs[-1].start()
    project(1)
    outs.append(pltpu.make_async_copy(qkv_s, qkv_out, sem_loc.at[4]))
    outs[-1].start()

    def attend(i, _):
        pc, pair = i // 6, i % 6

        def part(which):
            cols = pl.ds(pl.multiple_of(which * D + pair * 128, 128), 128)
            return jnp.concatenate(
                [qkv_s[half, :, pc, :, cols].reshape(128, 128) for half in range(2)], axis=0
            )

        q, k, v = part(0), part(1), part(2)
        v_t = v.T
        got = []
        for half in range(2):
            scores = mm_nt(k, head_lanes(q, half)) * 0.125
            e = jnp.exp(scores - jnp.max(scores, axis=0, keepdims=True))
            low = (e * (1.0 / jnp.sum(e, axis=0, keepdims=True))).astype(BF16)
            p_s[2 * i + half] = low
            got.append(mm(v_t[64 * half : 64 * half + 64], low))
        o = jnp.concatenate(got, axis=0).T.astype(BF16)
        cols = pl.ds(pl.multiple_of(pair * 128, 128), 128)
        for half in range(2):
            ag_s[half, :, pc, :, cols] = o[128 * half : 128 * half + 128].reshape(8, 16, 128)
        return 0

    lax.fori_loop(0, 12, attend, 0)
    back = [
        remote(ag_s.at[1], at_s.at[pl.ds(0, 8), 1], sem_pair.at[2], sem_pair.at[3], other),
        remote(ag_s.at[0, 7], at_s.at[8, 1], sem_pair.at[4], sem_pair.at[5], other),
        pltpu.make_async_copy(ag_s.at[0], at_s.at[pl.ds(0, 8), 0], sem_loc.at[5]),
        pltpu.make_async_copy(ag_s.at[1, 7], at_s.at[8, 0], sem_loc.at[6]),
    ]
    for copy in back:
        copy.start()
    outs.append(pltpu.make_async_copy(p_s, p_out, sem_loc.at[7]))
    outs[-1].start()
    placed(1, c_s)
    outs.append(pltpu.make_async_copy(c_s, ct_out, sem_loc.at[8]))
    outs[-1].start()
    for copy in back:
        copy.wait()
    outs.append(pltpu.make_async_copy(at_s, at_out, sem_loc.at[9]))
    outs[-1].start()
    for copy in outs:
        copy.wait()

    def finish(make, local):
        if not local:
            make().wait_send()

    sends(finish)


VMEM_SPEC = pl.BlockSpec(memory_space=pltpu.VMEM)
ANY_SPEC = pl.BlockSpec(memory_space=pl.ANY)


def attn_call(lat, ct, mod, w, qb, taps, cb):
    G = (2, 8, 2, 16)
    shape = jax.ShapeDtypeStruct
    return pl.pallas_call(
        attn_kernel,
        in_specs=[ANY_SPEC, ANY_SPEC, VMEM_SPEC, ANY_SPEC, VMEM_SPEC, VMEM_SPEC, VMEM_SPEC],
        out_specs=[ANY_SPEC] * 7,
        out_shape=[
            shape((576, D), BF16), shape((576, D), BF16), shape((576, D), BF16),
            shape(G + (D,), BF16), shape(G + (3 * D,), BF16), shape((24, 256, 256), BF16),
            shape((9, 2, 2, 16, D), BF16),
        ],
        scratch_shapes=[
            pltpu.VMEM((2, 2, 256, D), BF16), pltpu.VMEM((2, 64, D), BF16),
            pltpu.VMEM((576, D), BF16), pltpu.VMEM((576, D), BF16), pltpu.VMEM((576, D), BF16),
            pltpu.VMEM(G + (D,), BF16), pltpu.VMEM((8, 2, 16, D), BF16),
            pltpu.VMEM((D, 3 * D), BF16), pltpu.VMEM(G + (3 * D,), BF16),
            pltpu.VMEM((24, 256, 256), BF16), pltpu.VMEM(G + (D,), BF16),
            pltpu.VMEM((9, 2, 2, 16, D), BF16),
            pltpu.SemaphoreType.DMA((2, 2, 2)), pltpu.SemaphoreType.DMA((2, 3)),
            pltpu.SemaphoreType.DMA((6,)), pltpu.SemaphoreType.DMA((10,)),
        ],
        compiler_params=pltpu.CompilerParams(
            collective_id=1, has_side_effects=True, vmem_limit_bytes=56 * 2**20
        ),
        name="attend",
    )(lat, ct, mod, w, qb, taps, cb)


ORDERS = (("x", "y", "z"), ("y", "z", "x"), ("z", "x", "y"))


def axis_spot(me, axis):
    return me["zh"] * 2 + me["zl"] if axis == "z" else me[axis]


def back_kernel(
    da_ref, qkv_ref, p_ref, hcg_ref, h_ref, x_ref, dx_ref, mod_ref, w_ref, tap_ref, perm_ref,
    o_ref, fg_ref, go_ref, s2_ref, sb_ref,
    oret_out, iret_out, fe_out, fl_out, sm_out, dm_out,
    qkv_s, p_s, w_s, perm_s, dag_s, dqkv_s, hct_s, dhc_s, dh_s, gh_s, ig_s, os_s, is_s,
    own_s, pre_s, lg_s, prl_s, r1e, r1l, s1e, s1l, r2e, r2l, t3e, t3l, r3e, r3l, fe_s, fl_s,
    acc_s, sv_s, sp_s, sr_s, sx_s, mp_s, mr_s, dm_s, smf_s,
    loc, pair_sem, ret_send, ret_recv, st_send, st_recv, sx_send, sx_recv, dm_send, dm_recv,
):
    me = spot()
    zh, core = me["zh"], me["core"]
    other = seq_peer(me, zh, 1 - core)
    loads = [
        pltpu.make_async_copy(qkv_ref, qkv_s, loc.at[0]),
        pltpu.make_async_copy(p_ref, p_s, loc.at[1]),
        pltpu.make_async_copy(w_ref, w_s, loc.at[2]),
        pltpu.make_async_copy(perm_ref, perm_s, loc.at[3]),
        pltpu.make_async_copy(da_ref.at[:, 0], dag_s.at[0], loc.at[4]),
        pltpu.make_async_copy(fg_ref.at[core], own_s, loc.at[5]),
        pltpu.make_async_copy(go_ref, lg_s.at[1, :, 0], loc.at[6]),
    ]
    for at in (4, 0, 1, 2, 3, 5, 6):
        loads[at].start()
    barrier = pltpu.get_barrier_semaphore()
    peers = [axis_peer(me, axis, o) for axis in "xyz" for o in (1, 2, 3)]
    peers += [other, seq_peer(me, 1 - zh, 1 - core)]
    for peer in peers:
        pl.semaphore_signal(barrier, inc=1, device_id=peer, device_id_type=MESH)
    pl.semaphore_wait(barrier, len(peers))

    da_copy = remote(da_ref.at[:, 1], dag_s.at[1], pair_sem.at[0, 0], pair_sem.at[0, 1], other)
    da_copy.start()
    early = [
        remote(fg_ref.at[1 - core, p], pre_s.at[p], pair_sem.at[1 + p, 0], pair_sem.at[1 + p, 1], other)
        for p in range(3)
    ]
    for copy in early:
        copy.start()

    home = place_matrix(256, core == 1, True)

    def give_back(which, act):
        ref, out = ((os_s, oret_out), (is_s, iret_out))[which]
        for b in range(2):
            to_core = jnp.where(core == 0, b, 1 - b)
            own = jnp.logical_and(zh == core, b == 0)

            @pl.when(own)
            def _():
                act(lambda: pltpu.make_async_copy(ref.at[b], out.at[zh], ret_recv.at[which, zh]), True)

            @pl.when(jnp.logical_not(own))
            def _():
                act(
                    lambda: remote(
                        ref.at[b], out.at[zh], ret_send.at[which, b], ret_recv.at[which, zh],
                        seq_peer(me, core, to_core),
                    ),
                    False,
                )

    for b in range(2):
        os_s[b] = mm(home, o_ref[256 * b : 256 * b + 256, :]).astype(BF16)
    give_back(0, lambda make, local: make().start())

    loads[3].wait()
    for p in range(3):
        hct_s[p] = mm_nt(perm_s[p], hcg_ref[...]).astype(BF16)
    loads[4].wait()
    loads[0].wait()
    loads[1].wait()
    da_copy.wait()

    def attend_back(i, _):
        pc, pair = i // 6, i % 6
        lanes_at = [
            pl.ds(pl.multiple_of(which * D + pair * 128, 128), 128) for which in range(3)
        ]

        def part(ref, cols):
            return jnp.concatenate(
                [ref[half, :, pc, :, cols].reshape(128, 128) for half in range(2)], axis=0
            )

        q, k, v = (part(qkv_s, cols) for cols in lanes_at)
        do = part(dag_s, lanes_at[0])
        k_t = k.T
        dq_t, dk, dv = [], None, None
        for half in range(2):
            dom, qm = head_lanes(do, half), head_lanes(q, half)
            low = p_s[2 * i + half]
            probs = low.astype(F32)
            dp = mm_nt(v, dom)
            ds = (probs * (dp - jnp.sum(probs * dp, axis=0, keepdims=True))).astype(BF16)
            dq_t.append(mm(k_t[64 * half : 64 * half + 64], ds))
            dk_h, dv_h = mm(ds, qm), mm(low, dom)
            dk = dk_h if dk is None else dk + dk_h
            dv = dv_h if dv is None else dv + dv_h
        dq = jnp.concatenate(dq_t, axis=0).T
        for cols, got in zip(lanes_at, (0.125 * dq, 0.125 * dk, dv)):
            got = got.astype(BF16)
            for half in range(2):
                dqkv_s[half, :, pc, :, cols] = got[128 * half : 128 * half + 128].reshape(8, 16, 128)
        return 0

    def stage_sends(stage, bufs, panels, late):
        out = []
        for p in range(3):
            axis = ORDERS[p][stage]
            here = axis_spot(me, axis)
            for o in (1, 2, 3):
                there = (here + o) % 4
                src, dst = bufs(p, o, there)
                copy = remote(
                    src, dst, st_send.at[late, stage, p, o - 1], st_recv.at[late, stage, p, o - 1],
                    axis_peer(me, axis, o),
                )
                copy.start()
                out.append(copy)
        return out

    def chunk(there, rows):
        return pl.ds(pl.multiple_of(there * rows, 16), rows)

    lax.fori_loop(0, 6, attend_back, 0)
    loads[5].wait()
    for p in range(3):
        early[p].wait()

        def add_early(k, _):
            own_s[p, k] = own_s[p, k] + pre_s[p, k]
            return 0

        lax.fori_loop(0, 4, add_early, 0)
    st1e = stage_sends(
        0, lambda p, o, a: (own_s.at[p, :, chunk(a, 192)], r1e.at[o - 1, p]), 4, 0
    )
    lax.fori_loop(6, 12, attend_back, 0)

    loads[2].wait()
    for half in (1, 0):
        got = mm_nt(dqkv_s[half].reshape(256, 3 * D), w_s[...]).astype(BF16)
        dhc_s[half] = got.reshape(8, 2, 16, D)
        if half == 1:
            dhc_copy = remote(
                dhc_s.at[1], dh_s.at[pl.ds(0, 8), 1], pair_sem.at[4, 0], pair_sem.at[4, 1], other
            )
            dhc_copy.start()
    near = [
        pltpu.make_async_copy(dhc_s.at[0], dh_s.at[pl.ds(0, 8), 0], loc.at[7]),
        pltpu.make_async_copy(dhc_s.at[1, 7], dh_s.at[8, 0], loc.at[8]),
    ]
    for copy in near:
        copy.start()
    loads[6].wait()
    for p in range(3):
        for at, to in (
            (512 * p, (0, p, 0)), (512 * p + 256, (0, p, 1)), (1536 + 256 * p, (1, p, 1))
        ):
            lg_s[to] = mm(
                hct_s[p], dqkv_s[:, :, :, :, at : at + 256].reshape(512, 256)
            ).astype(BF16)
    late = [
        remote(lg_s.at[1 - core, p], prl_s.at[p], pair_sem.at[5 + p, 0], pair_sem.at[5 + p, 1], other)
        for p in range(3)
    ]
    for copy in late:
        copy.start()
    ones = jnp.ones((8, 512), BF16)
    sv_s[64:96, :] = jnp.zeros((32, D), F32)
    for row, at in ((74, 0), (75, 2 * D)):
        sums = mm(ones, dqkv_s[:, :, :, :, at : at + D].reshape(512, D))
        sv_s[row : row + 1, :] = sums[0:1]
    sv_s[76:78, :] = sb_ref[4:6, :]
    for q in range(4):
        sv_s[16 * q : 16 * q + 16, :] = s2_ref[:, D * q : D * q + D]

    dhc_copy.wait()
    for copy in near:
        copy.wait()
    masks = side_masks()

    def lanes(j, _):
        cols = pl.ds(pl.multiple_of(j * 128, 128), 128)
        taps = [tap_ref[t : t + 1, cols] for t in range(9)]
        back = [by_core(taps, 8 - t, core) for t in range(9)]

        def sided_d(l):
            return with_sides(
                dh_s[l // 2, l % 2, 0, :, cols].astype(F32),
                dh_s[l // 2, l % 2, 1, :, cols].astype(F32),
                masks,
            )

        def sided_h(l):
            return with_sides(
                h_ref[32 * l : 32 * l + 16, cols].astype(F32),
                h_ref[32 * l + 16 : 32 * l + 32, cols].astype(F32),
                masks,
            )

        rows = [None, sided_d(0), sided_d(1)]
        rows_h = [None, sided_h(0), sided_h(1)]
        sums = [None] * 9
        bias_sum = None
        for l in range(16):
            ge, go = conv_row(rows, back)
            gh_s[32 * l : 32 * l + 16, cols] = ge
            gh_s[32 * l + 16 : 32 * l + 32, cols] = go
            de, do = rows[1][0], rows[1][1]
            tap_products(sums, rows_h, de, do)
            term = fold8(de + do)
            bias_sum = term if bias_sum is None else bias_sum + term
            if l < 15:
                rows = [rows[1], rows[2], sided_d(l + 2)]
                rows_h = [rows_h[1], rows_h[2], sided_h(l + 2)]
        for t in range(9):
            total = jnp.sum(by_core(sums, t, core), axis=0, keepdims=True)
            sv_s[64 + t : 65 + t, cols] = total
        sv_s[73:74, cols] = jnp.sum(bias_sum, axis=0, keepdims=True)
        return 0

    lax.fori_loop(0, D // 128, lanes, 0)
    scale1 = mod_ref[1:2, :]
    acc_s[...] = jnp.zeros_like(acc_s)

    def rows_n(r, _):
        at = pl.ds(pl.multiple_of(r * 32, 32), 32)
        n1, rs = norm_parts(x_ref[at, :].astype(F32))
        dh = gh_s[at, :]
        g1 = dh * (1.0 + scale1)
        got = dx_ref[at, :] + rs * (
            g1
            - jnp.mean(g1, axis=-1, keepdims=True)
            - n1 * jnp.mean(g1 * n1, axis=-1, keepdims=True)
        )
        ig_s[at, :] = got.astype(BF16)
        acc_s[0] += fold8(dh)
        acc_s[1] += fold8(dh * n1)
        return 0

    lax.fori_loop(0, 16, rows_n, 0)
    for i in range(2):
        mp_s[i : i + 1, :] = jnp.sum(acc_s[i], axis=0, keepdims=True)
    mp_s[2:6, :] = sb_ref[0:4, :]
    mp_s[6:8, :] = jnp.zeros((2, D), F32)
    mp_copy = remote(mp_s, mr_s, pair_sem.at[8, 0], pair_sem.at[8, 1], other)
    mp_copy.start()
    for half in range(2):
        sp_s[half] = sv_s[48 * half : 48 * half + 48, :].astype(BF16)
    sp_copy = remote(sp_s.at[1 - core], sr_s, pair_sem.at[9, 0], pair_sem.at[9, 1], other)
    sp_copy.start()
    for b in range(2):
        is_s[b] = mm(home, ig_s[256 * b : 256 * b + 256, :]).astype(BF16)
    give_back(1, lambda make, local: make().start())

    for copy in late:
        copy.wait()
    for p in range(3):
        for k in range(2):
            lg_s[core, p, k] = lg_s[core, p, k] + prl_s[p, k]
    st1l = stage_sends(
        0, lambda p, o, a: (lg_s.at[core, p, :, chunk(a, 192)], r1l.at[o - 1, p]), 2, 1
    )

    mp_copy.wait()
    item = (mp_s[...] + mr_s[...]).astype(BF16).astype(F32)
    dm_rows = [item[i : i + 1, 128 * l : 128 * l + 128] for i in range(6) for l in range(6)]
    z_me = axis_spot(me, "z")
    dm_s[z_me, me["y"], me["x"]] = jnp.concatenate(
        dm_rows + [jnp.zeros((12, 128), F32)], axis=0
    ).astype(BF16)
    sp_copy.wait()
    sx_s[0] = (sp_s[core].astype(F32) + sr_s[...].astype(F32)).astype(BF16)

    def small_stage(stage):
        axis = "xyz"[stage]
        view = (
            lambda ref: ref.at[z_me, me["y"], me["x"]],
            lambda ref: ref.at[z_me, me["y"]],
            lambda ref: ref.at[z_me],
        )[stage]
        out = []
        for o in (1, 2, 3):
            out.append(
                remote(
                    sx_s.at[4 * stage], sx_s.at[4 * stage + o], sx_send.at[stage, o - 1],
                    sx_recv.at[stage, o - 1], axis_peer(me, axis, o),
                )
            )
            out.append(
                remote(
                    view(dm_s), view(dm_s), dm_send.at[stage, o - 1], dm_recv.at[stage, o - 1],
                    axis_peer(me, axis, o),
                )
            )
        for copy in out:
            copy.start()
        return out

    def small_take(stage, copies):
        axis = "xyz"[stage]
        here = axis_spot(me, axis)
        for copy in copies:
            copy.wait_send()
        for o in (1, 2, 3):
            arrived(sx_s.at[4 * stage + o], sx_recv.at[stage, o - 1])
            there = (here + 4 - o) % 4
            view = (
                lambda: dm_s.at[z_me, me["y"], there],
                lambda: dm_s.at[z_me, there],
                lambda: dm_s.at[there],
            )[stage]
            arrived(view(), dm_recv.at[stage, o - 1])
        total = sx_s[4 * stage].astype(F32)
        for o in (1, 2, 3):
            total = total + sx_s[4 * stage + o].astype(F32)
        if stage < 2:
            sx_s[4 * stage + 4] = total.astype(BF16)
        else:
            smf_s[...] = total

    def take(copies):
        for copy in copies:
            copy.wait()

    def sum_one(own, recv, into, panels, p):
        def body(k, _):
            total = own(k).astype(F32)
            for o in range(3):
                total = total + recv[o, p, k].astype(F32)
            into[p, k] = total.astype(BF16)
            return 0

        lax.fori_loop(0, panels, body, 0)

    small = small_stage(0)
    take(st1e)
    for p in range(3):
        here = axis_spot(me, ORDERS[p][0])
        sum_one(lambda k: own_s[p, k, chunk(here, 192), :], r1e, s1e, 4, p)
    st2e = stage_sends(1, lambda p, o, b: (s1e.at[p, :, chunk(b, 48)], r2e.at[o - 1, p]), 4, 0)
    small_take(0, small)
    small = small_stage(1)
    take(st1l)
    for p in range(3):
        here = axis_spot(me, ORDERS[p][0])
        sum_one(lambda k: lg_s[core, p, k, chunk(here, 192), :], r1l, s1l, 2, p)
    st2l = stage_sends(1, lambda p, o, b: (s1l.at[p, :, chunk(b, 48)], r2l.at[o - 1, p]), 2, 1)

    def second(own, recv, panels, p):
        here = axis_spot(me, ORDERS[p][1])
        out = []
        for k in range(panels):
            total = own[p, k, chunk(here, 48), :].astype(F32)
            for o in range(3):
                total = total + recv[o, p, k].astype(F32)
            out.append(total)
        return out

    take(st2e)
    for p in range(3):
        got = second(s1e, r2e, 4, p)

        @pl.when(core == 0)
        def _():
            for c in range(4):
                t3e[p, c] = jnp.concatenate(
                    [got[k][12 * c : 12 * c + 12] for k in range(4)], axis=0
                ).astype(BF16)

        @pl.when(core == 1)
        def _():
            for c in range(4):
                t3e[p, c] = got[c].astype(BF16)

    st3e = stage_sends(2, lambda p, o, c: (t3e.at[p, c], r3e.at[o - 1, p]), 4, 0)
    small_take(1, small)
    small = small_stage(2)
    take(st2l)
    for p in range(3):
        got = second(s1l, r2l, 2, p)
        for c in range(4):
            t3l[p, c] = jnp.concatenate(
                [got[0][12 * c : 12 * c + 12], got[1][12 * c : 12 * c + 12], jnp.zeros((8, 256), F32)],
                axis=0,
            ).astype(BF16)
    st3l = stage_sends(2, lambda p, o, c: (t3l.at[p, c], r3l.at[o - 1, p]), 2, 1)

    ends = []

    def finish(copies, own, recv, done, out, at):
        take(copies)
        for p in range(3):
            total = own[p, axis_spot(me, ORDERS[p][2])].astype(F32)
            for o in range(3):
                total = total + recv[o, p].astype(F32)
            done[p] = total
        spread(done, out, at)

    def spread(done, out, at):
        ends.append(pltpu.make_async_copy(done, out.at[core], loc.at[at]))
        ends.append(
            remote(done, out.at[core], pair_sem.at[at, 0], pair_sem.at[at, 1], other)
        )
        ends[-1].start()
        ends[-2].start()

    finish(st3e, t3e, r3e, fe_s, fe_out, 10)
    small_take(2, small)
    spread(smf_s, sm_out, 11)
    ends.append(pltpu.make_async_copy(dm_s, dm_out, loc.at[9]))
    ends[-1].start()
    finish(st3l, t3l, r3l, fl_s, fl_out, 12)
    for which in range(2):
        give_back(which, lambda make, local: None if local else make().wait_send())
        for item_slot in range(2):
            out = (oret_out, iret_out)[which]
            arrived(out.at[item_slot], ret_recv.at[which, item_slot])
    for copy in ends:
        copy.wait()


def back_call(da, qkv, p, hcg, h, x, dx, mod, w, taps, perm, o, fg, go, s2, sb):
    G = (2, 8, 2, 16)
    shape = jax.ShapeDtypeStruct
    V = pltpu.VMEM
    return pl.pallas_call(
        back_kernel,
        in_specs=[
            ANY_SPEC, ANY_SPEC, ANY_SPEC, VMEM_SPEC, VMEM_SPEC, VMEM_SPEC, VMEM_SPEC, VMEM_SPEC,
            ANY_SPEC, VMEM_SPEC, ANY_SPEC, VMEM_SPEC, ANY_SPEC, ANY_SPEC, VMEM_SPEC, VMEM_SPEC,
        ],
        out_specs=[ANY_SPEC] * 6,
        out_shape=[
            shape((2, 256, D), BF16), shape((2, 256, D), BF16),
            shape((2, 3, 48, 256), F32), shape((2, 3, 32, 256), F32),
            shape((2, 48, D), F32), shape((4, 4, 4, 48, 128), BF16),
        ],
        scratch_shapes=[
            V(G + (3 * D,), BF16), V((24, 256, 256), BF16), V((D, 3 * D), BF16),
            V((3, D, D), BF16), V(G + (D,), BF16), V(G + (3 * D,), BF16), V((3, D, 512), BF16),
            V(G + (D,), BF16), V((9, 2, 2, 16, D), BF16), V((512, D), F32), V((512, D), BF16),
            V((2, 256, D), BF16), V((2, 256, D), BF16),
            V((3, 4, D, 256), BF16), V((3, 4, D, 256), BF16), V((2, 3, 2, D, 256), BF16),
            V((3, 2, D, 256), BF16),
            V((3, 3, 4, 192, 256), BF16), V((3, 3, 2, 192, 256), BF16),
            V((3, 4, 192, 256), BF16), V((3, 2, 192, 256), BF16),
            V((3, 3, 4, 48, 256), BF16), V((3, 3, 2, 48, 256), BF16),
            V((3, 4, 48, 256), BF16), V((3, 4, 32, 256), BF16),
            V((3, 3, 48, 256), BF16), V((3, 3, 32, 256), BF16),
            V((3, 48, 256), F32), V((3, 32, 256), F32),
            V((2, 8, D), F32), V((96, D), F32), V((2, 48, D), BF16), V((48, D), BF16),
            V((12, 48, D), BF16), V((8, D), F32), V((8, D), F32), V((4, 4, 4, 48, 128), BF16),
            V((48, D), F32),
            pltpu.SemaphoreType.DMA((13,)), pltpu.SemaphoreType.DMA((13, 2)),
            pltpu.SemaphoreType.DMA((2, 2)), pltpu.SemaphoreType.DMA((2, 2)),
            pltpu.SemaphoreType.DMA((2, 3, 3, 3)), pltpu.SemaphoreType.DMA((2, 3, 3, 3)),
            pltpu.SemaphoreType.DMA((3, 3)), pltpu.SemaphoreType.DMA((3, 3)),
            pltpu.SemaphoreType.DMA((3, 3)), pltpu.SemaphoreType.DMA((3, 3)),
        ],
        compiler_params=pltpu.CompilerParams(
            collective_id=2, has_side_effects=True, vmem_limit_bytes=62 * 2**20
        ),
        name="back",
    )(da, qkv, p, hcg, h, x, dx, mod, w, taps, perm, o, fg, go, s2, sb)


def perm_matrices():
    at = np.arange(D)
    rows = []
    for order in ORDERS:
        spots = dict(zip(order, (at // 192, at // 48 % 4, at // 12 % 4)))
        x, y, z = spots["x"], spots["y"], spots["z"]
        rows.append((((x * 2 + z % 2) * 4 + y) * 2 + z // 2) * 12 + at % 12)
    return np.stack(rows).astype(np.int32)


def local(
    latents, conditioning, timesteps, item_counts, cotangent, time_table, mod_weight, mod_bias,
    conv_attn_weight, conv_attn_bias, qkv_weight, query_bias, value_bias, out_weight, out_bias,
    fc1_weight, fc1_bias, conv_ffn_weight, conv_ffn_bias, fc2_weight, fc2_bias,
):
    core = lax.axis_index("seq") % 2
    shard = lax.axis_index("dp") * 4 + lax.axis_index("seq")
    all_cond = lax.all_gather(conditioning, "dp", axis=0, tiled=True)
    all_times = lax.all_gather(timesteps, "dp", axis=0, tiled=True)
    alive = (lax.axis_index("seq") // 2 < item_counts).astype(F32)
    perm = (perm_matrices()[:, :, None] == np.arange(D)[None, None, :]).astype(BF16)
    cond = conditioning.astype(F32) + time_table[timesteps].astype(F32)
    silu_cond = jax.nn.silu(cond).astype(BF16)
    mod = jnp.dot(silu_cond, mod_weight, preferred_element_type=F32) + mod_bias.astype(F32)
    mod = jnp.pad(mod.reshape(2, 6, D), ((0, 0), (0, 2), (0, 0)))
    mod = lax.dynamic_index_in_dim(mod, lax.axis_index("seq") // 2, 0, False)
    taps_attn = jnp.pad(conv_attn_weight.astype(F32), ((0, 7), (0, 0)))
    taps_ffn = jnp.pad(conv_ffn_weight.astype(F32), ((0, 7), (0, 0)))
    qkv_bias = jnp.concatenate(
        (query_bias.astype(F32), jnp.zeros((D,), F32), value_bias.astype(F32))
    )[None]
    x, ct, h, hcg, qkv, p, at = attn_call(
        latents.reshape(2, 256, D), cotangent.reshape(2, 256, D), mod, qkv_weight, qkv_bias,
        taps_attn, conv_attn_bias[None],
    )
    out, fg, go, da, dx, s2, sb = ffn_call(
        x, at.reshape(576, D), ct, mod, alive, perm, out_weight, out_bias[None], fc1_weight,
        fc1_bias[None], taps_ffn, conv_ffn_bias[None], fc2_weight, fc2_bias[None],
    )
    out, ig, fe, fl, sm, dm = back_call(
        da.reshape(8, 2, 2, 16, D), qkv, p, hcg.reshape(512, D), h, x, dx, mod, qkv_weight,
        taps_attn, perm, out, fg.reshape(2, 3, 4, D, 256), go, s2, sb,
    )
    output = out.reshape(2, 8, 32, D)
    input_grad = ig.reshape(2, 8, 32, D).astype(F32)
    d_mod = dm.reshape(2, 2, 4, 4, 48, 128)[:, :, :, :, :36].transpose(3, 1, 2, 0, 4, 5)
    d_mod = d_mod.reshape(64, 6 * D)
    all_cond = all_cond.astype(F32) + time_table[all_times].astype(F32)
    my_cond = lax.dynamic_slice_in_dim(all_cond, shard * 6, 6, axis=1)
    my_silu = jax.nn.silu(my_cond).astype(BF16)
    mod_grad = lax.dot_general(
        my_silu, d_mod, (((0,), (0,)), ((), ())), preferred_element_type=F32
    )
    mod_bias_grad = jnp.sum(
        lax.dynamic_slice_in_dim(d_mod, shard * 36, 36, axis=1).astype(F32), axis=0
    )

    def silu_slope(v):
        s = jax.nn.sigmoid(v)
        return s * (1.0 + v * (1.0 - s))

    own_d_mod = lax.dynamic_slice_in_dim(d_mod, lax.axis_index("dp") * 2, 2, axis=0)
    cond_grad = silu_slope(cond) * mm_nt(own_d_mod, mod_weight)
    my_rows = lax.dynamic_slice_in_dim(mod_weight, shard * 6, 6, axis=0)
    my_cond_grad = silu_slope(my_cond) * mm_nt(d_mod, my_rows)
    table_grad = jnp.dot(
        (jnp.arange(1000)[:, None] == all_times[None, :]).astype(F32), my_cond_grad,
        precision=lax.Precision.HIGHEST,
    )
    six = lambda v: lax.dynamic_slice_in_dim(v, core * 6, 6, axis=-2)
    fc1_grad = six(fe[0].reshape(3, 4, 12, 256)).transpose(2, 1, 0, 3).reshape(6, FF)
    fc2_grad = lax.dynamic_slice_in_dim(fe[1], core * 24, 24, axis=1).transpose(1, 0, 2)
    late = six(fl[:, :, :24].reshape(2, 3, 2, 12, 256))
    qkv_grad = jnp.concatenate(
        (
            late[0].transpose(2, 0, 1, 3).reshape(6, 1536),
            late[1, :, 1].transpose(1, 0, 2).reshape(6, D),
        ),
        axis=1,
    )
    out_grad = late[1, :, 0].transpose(1, 0, 2).reshape(6, D)
    sums = sm.reshape(96, D)
    wide = sums[:64].reshape(4, 16, D).transpose(1, 0, 2).reshape(16, FF)
    wide = lax.dynamic_slice_in_dim(wide, shard * 24, 24, axis=1)
    slim = lax.dynamic_slice_in_dim(sums[64:80], shard * 6, 6, axis=1)
    return (
        output, input_grad, cond_grad, table_grad, mod_grad, mod_bias_grad, slim[:9], slim[9],
        qkv_grad, slim[10], slim[11], out_grad, slim[12], fc1_grad, wide[10], wide[:9], wide[9],
        fc2_grad.reshape(24, D), slim[13],
    )


def solution(mesh):
    return jax.shard_map(
        local,
        mesh=mesh,
        in_specs=(
            P("dp", "seq", None, None),
            P("dp", None),
            P("dp"),
            P("dp"),
            P("dp", "seq", None, None),
            P(),
            P(),
            P(),
            P(),
            P(),
            P(),
            P(),
            P(),
            P(),
            P(),
            P(),
            P(),
            P(),
            P(),
            P(),
            P(),
        ),
        out_specs=(
            P("dp", "seq", None, None),
            P("dp", "seq", None, None),
            P("dp", None),
            P(None, ("dp", "seq")),
            P(("dp", "seq"), None),
            P(("dp", "seq")),
            P(None, ("dp", "seq")),
            P(("dp", "seq")),
            P(("dp", "seq"), None),
            P(("dp", "seq")),
            P(("dp", "seq")),
            P(("dp", "seq"), None),
            P(("dp", "seq")),
            P(("dp", "seq"), None),
            P(("dp", "seq")),
            P(None, ("dp", "seq")),
            P(("dp", "seq")),
            P(("dp", "seq"), None),
            P(("dp", "seq")),
        ),
        check_vma=False,
    )
```

time: 2010 us -> 309 us (0.15); the launches traced: 1980 us -> 308 us
  local copies, waits for them, and re-layouts: 527 us -> 15.2 us
  blocking collectives: 548 us -> 95.3 us
  starting transfers between devices: 446 us -> 0 us
  waiting for transfers between devices: 208 us -> 0 us
  Pallas kernels: 0 us -> 176 us
  matrix products: 145 us -> 13 us
  other arithmetic: 89.5 us -> 6.5 us
    unnamed x1, blocking collectives: 532 us -> 17.7 us
    unnamed x163 -> x0, starting transfers between devices: 425 us -> none
    unnamed x454 -> x43, local copies, waits for them, and re-layouts: 348 us -> 3.84 us
    pallas_call x0 -> x3, Pallas kernels: none -> 176 us  [the longest x1 78.3 us: back_call(): pl.pallas_call(back_kernel, in_specs=[ANY_SPEC, ANY_SPEC, ANY_SPEC, VMEM_...]
    dot_general x22 -> x5, matrix products: 137 us -> 13 us  [the longest x2 6.84 us: mm_nt(): lax.dot_general(a, b, (((1,), (1,)), ((), ())), preferred_element_type=F32)]
    unnamed x168 -> x0, waiting for transfers between devices: 114 us -> none
    another operation x24 -> x1, local copies, waits for them, and re-layouts: 97.5 us -> 0.02 us  [local(): fe[0].reshape(3, 4, 12, 256)]
    all_gather x0 -> x1, blocking collectives: none -> 77.7 us  [local(): all_cond = lax.all_gather(conditioning, 'dp', axis=0, tiled=True)]
  transfers between devices with their start and end apart: 173 -> 0, of which waited for: 8 -> 0; matrix products, arithmetic and copies ran while one was open for 50% -> 0% of each run, Pallas kernels for 0% -> 0%
where the time goes in v1:
time: 309 us; the launch traced here: 308 us
  Pallas kernels  176 us (57%)
  blocking collectives  95.3 us (31%)
  local copies, waits for them, and re-layouts  15.2 us (5%)
  matrix products  13 us (4%)
  other arithmetic  6.5 us (2%)
    pallas_call x1, Pallas kernels, back_call(): pl.pallas_call(back_kernel, in_specs=[ANY_SPEC, ANY_SPEC, ANY_SPEC, VMEM_...  78.3 us
    all_gather x1, blocking collectives, local(): all_cond = lax.all_gather(conditioning, 'dp', axis=0, tiled=True)  77.7 us
    pallas_call x1, Pallas kernels, ffn_call(): pl.pallas_call(ffn_kernel, grid=(NFC,), in_specs=[whole((576, D)), whole(...  59.7 us
    pallas_call x1, Pallas kernels, attn_call(): pl.pallas_call(attn_kernel, in_specs=[ANY_SPEC, ANY_SPEC, VMEM_SPEC, ANY_...  37.8 us
    unnamed x1, blocking collectives  17.7 us
    dot_general x2, matrix products, mm_nt(): lax.dot_general(a, b, (((1,), (1,)), ((), ())), preferred_element_type=F32)  6.84 us

profile of v1, /device:TPU:0, one launch (start us, length us, event | category | flops | bytes accessed | tf_op | source)
XLA Modules:
  0.0 308.2 jit_solution(3836970147912119196)
XLA Ops:
  0.7 0.0 copy-start
  0.7 0.8 compare_select_fusion.1
  1.5 0.6 copy-done
  2.1 0.6 gather_fusion
  2.6 0.7 convert_element_type.51
  3.4 0.0 copy-start.12
  3.4 4.1 %convolution_add_fusion = f32[2,4608]{1,0:T(2,128)S(1)} fusion(bf16[768,4608]{1,0:T(8,128)(2,1)} %param.28, f32[4608]{0:T(1024)S(1)} %convert_element_type.51, bf16[2,768]{1,0:T(2,128)(2,1)S(1)} %gather_fusion, bf16[2,768]{1,0:T(2,128)(2,1)} %param.23), kind=kOutput, calls=%fused_computation.2 | convolution fusion | flops 14177280 | bytes 7139328 | tf_op jit(solution)/shard_map/dot_general | solution.py:1080
  7.5 0.6 fusion.3.mod_ref
  8.2 0.6 pad_convert_fusion.1.tap_ref
  8.8 0.6 broadcast_in_dim.32.qb_ref
  9.4 0.6 broadcast_in_dim.33.cb_ref
  10.0 37.8 %attend.1 = (bf16[576,768]{1,0:T(8,128)(2,1)}, bf16[576,768]{1,0:T(8,128)(2,1)}, bf16[576,768]{1,0:T(8,128)(2,1)}, bf16[2,8,2,16,768]{4,3,2,1,0:T(8,128)(2,1)}, ...) custom-call(bf16[2,256,768]{2,1,0:T(8,128)(2,1)} %bitcast.82, ...), custom_call_target="tpu_custom_call" | custom-call | tf_op jit(solution)/shard_map/attend/pallas_call | solution.py:556
  48.4 0.7 pad_convert_fusion.tap_ref
  49.1 0.6 broadcast_in_dim.35.f1b_ref
  49.7 0.6 broadcast_in_dim.36.cb_ref
  50.4 0.6 broadcast_in_dim.34.ob_ref
  50.9 0.6 broadcast_in_dim.37.f2b_ref
  51.5 59.7 %ffn.1 = (bf16[512,768]{1,0:T(8,128)(2,1)}, bf16[2,3,4,4,4,48,256]{6,5,4,3,2,1,0:T(8,128)(2,1)}, bf16[3,768,256]{2,1,0:T(8,128)(2,1)}, bf16[512,768]{1,0:T(8,128...) custom-call(bf16[576,768]{1,0:T(8,128)(2,1)} %get-tuple-element.39.x_ref, ...), custom_call_target="tpu_custom_call" | custom-call | tf_op jit(solution)/shard_map/ffn/pallas_call | solution.py:267
  111.3 78.3 %back.1 = (bf16[2,256,768]{2,1,0:T(8,128)(2,1)}, bf16[2,256,768]{2,1,0:T(8,128)(2,1)}, f32[2,3,48,256]{3,2,1,0:T(8,128)}, f32[2,3,32,256]{3,2,1,0:T(8,128)}, f32...) custom-call(bf16[8,2,2,16,768]{4,3,2,1,0:T(8,128)(2,1)} %bitcast.85, ...), custom_call_target="tpu_custom_call" | custom-call | tf_op jit(solution)/shard_map/back/pallas_call | solution.py:1016
  189.6 0.0 copy-start.15
  189.6 0.9 slice.58
  190.6 0.1 copy.82
  190.8 0.6 pad_maximum_fusion
  191.5 1.1 slice.76
  192.6 0.1 copy.92
  192.7 0.1 copy.111
  192.8 0.6 dynamic-slice.1
  194.1 0.2 dynamic-update-slice
  194.3 17.7 %all-reduce.3 = s32[64]{0:T(128)S(1)} all-reduce(s32[64]{0:T(128)S(1)} %dynamic-update-slice), channel_id=1, replica_groups=mesh['dp'=32,'seq'=4] {'dp'}, use_global_device_ids=true, to_apply=%add.3 | all-reduce | flops 64 | bytes 512
  212.0 0.7 gather_fusion.1
  212.7 77.7 %all-gather = bf16[32,2,768]{2,1,0:T(2,128)(2,1)S(1)} all-gather(bf16[1,2,768]{2,1,0:T(2,128)(2,1)S(1)} %bitcast.96), channel_id=1, replica_groups=mesh['dp'=32,'seq'=4] {'dp'}, dimensions={0}, use_global_device_ids=true | all-gather | bytes 101376 | tf_op jit(solution)/shard_map/all_gather | solution.py:1074
  290.4 1.0 fusion.5
  291.4 1.2 convolution_multiply_fusion
  292.6 1.0 fusion
  293.7 5.6 %convolution_multiply_fusion.1 = f32[2,768]{1,0:T(2,128)} fusion(bf16[768,4608]{1,0:T(8,128)(2,1)} %param.28, bf16[64,4608]{1,0:T(8,128)(2,1)S(1)} %bitcast.75, s32[]{:T(128)S(6)} %select_n.46, bf16[2,768]{1,0:T(2,128)(2,1)S(1)} %gather_fusion, bf16[2,768]{1,0:T(2,128)(2,1)S(1)} %copy-done.5), kind=kOutput, calls=%fused_computation.4 | convolution fusion | flops 14172672 | bytes 7108612 | tf_op jit(solution)/shard_map/dot_general | solution.py:25
  299.3 0.6 convert_reduce_fusion
  299.9 2.4 convert.5
  302.5 0.1 copy.85
  302.5 0.7 reshape.116
  303.2 0.1 copy.86
  303.4 0.7 constant_dynamic-slice_fusion.1
  304.1 0.6 dynamic-slice_bitcast_fusion.3
  304.7 0.6 copy.106
  305.3 0.6 copy.91
  305.9 0.1 constant_dynamic-slice_fusion.3
  306.0 0.7 copy.95
  306.7 0.6 dynamic-slice_bitcast_fusion.2
  307.3 0.9 copy.116
  (50 shorter events, 0.4 us)
Async XLA Ops:
  0.7 1.4 copy-start
  0.7 7.5 %copy-start.6 = (bf16[9,768]{1,0:T(8,128)(2,1)S(1)}, bf16[9,768]{1,0:T(8,128)(2,1)}, u32[]{:S(2)}) copy-start(bf16[9,768]{1,0:T(8,128)(2,1)} %param.30) | copy-start | bytes 41476
  0.7 8.1 %copy-start.9 = (bf16[768]{0:T(1024)(128)(2,1)S(1)}, bf16[768]{0:T(1024)(128)(2,1)}, u32[]{:S(2)}) copy-start(bf16[768]{0:T(1024)(128)(2,1)} %param.33) | copy-start | bytes 4612
  0.7 8.1 %copy-start.10 = (bf16[768]{0:T(1024)(128)(2,1)S(1)}, bf16[768]{0:T(1024)(128)(2,1)}, u32[]{:S(2)}) copy-start(bf16[768]{0:T(1024)(128)(2,1)} %param.34) | copy-start | bytes 4612
  0.7 8.7 %copy-start.11 = (bf16[768]{0:T(1024)(128)(2,1)S(1)}, bf16[768]{0:T(1024)(128)(2,1)}, u32[]{:S(2)}) copy-start(bf16[768]{0:T(1024)(128)(2,1)} %param.31) | copy-start | bytes 4612
  3.3 45.1 %copy-start.4 = (bf16[9,3072]{1,0:T(8,128)(2,1)S(1)}, bf16[9,3072]{1,0:T(8,128)(2,1)}, u32[]{:S(2)}) copy-start(bf16[9,3072]{1,0:T(8,128)(2,1)} %param.39) | copy-start | bytes 165892
  3.3 45.8 %copy-start.7 = (bf16[3072]{0:T(1024)(128)(2,1)S(1)}, bf16[3072]{0:T(1024)(128)(2,1)}, u32[]{:S(2)}) copy-start(bf16[3072]{0:T(1024)(128)(2,1)} %param.38) | copy-start | bytes 18436
  3.3 46.4 %copy-start.8 = (bf16[3072]{0:T(1024)(128)(2,1)S(1)}, bf16[3072]{0:T(1024)(128)(2,1)}, u32[]{:S(2)}) copy-start(bf16[3072]{0:T(1024)(128)(2,1)} %param.40) | copy-start | bytes 18436
  3.4 47.0 %copy-start.12 = (bf16[768]{0:T(1024)(128)(2,1)S(1)}, bf16[768]{0:T(1024)(128)(2,1)}, u32[]{:S(2)}) copy-start(bf16[768]{0:T(1024)(128)(2,1)} %param.36) | copy-start | bytes 4612
  3.4 47.6 %copy-start.13 = (bf16[768]{0:T(1024)(128)(2,1)S(1)}, bf16[768]{0:T(1024)(128)(2,1)}, u32[]{:S(2)}) copy-start(bf16[768]{0:T(1024)(128)(2,1)} %param.42) | copy-start | bytes 4612
  189.6 3.2 %copy-start.15 = (u32[128]{0:T(128)S(1)}, u32[128]{0:T(128)}, u32[]{:S(2)}) copy-start(u32[128]{0:T(128)} %constant.95) | copy-start | bytes 1540
  189.6 4.5 %copy-start.14 = (s32[2]{0:T(128)S(1)}, s32[2]{0:T(128)}, u32[]{:S(2)}) copy-start(s32[2]{0:T(128)} %param.24) | copy-start | bytes 28
  189.6 23.1 %copy-start.5 = (bf16[2,768]{1,0:T(2,128)(2,1)S(1)}, bf16[2,768]{1,0:T(2,128)(2,1)}, u32[]{:S(2)}) copy-start(bf16[2,768]{1,0:T(2,128)(2,1)} %param.23) | copy-start | bytes 9220
  293.7 8.7 %copy-start.2 = (f32[2,3,48,256]{3,2,1,0:T(8,128)S(1)}, f32[2,3,48,256]{3,2,1,0:T(8,128)}, u32[]{:S(2)}) copy-start(f32[2,3,48,256]{3,2,1,0:T(8,128)} %get-tuple-element.58) | copy-start | bytes 884740
  293.7 9.5 %copy-start.3 = (f32[2,48,768]{2,1,0:T(8,128)S(1)}, f32[2,48,768]{2,1,0:T(8,128)}, u32[]{:S(2)}) copy-start(f32[2,48,768]{2,1,0:T(8,128)} %get-tuple-element.56) | copy-start | bytes 884740
  293.7 13.6 %copy-start.1 = (bf16[2,256,768]{2,1,0:T(8,128)(2,1)S(1)}, bf16[2,256,768]{2,1,0:T(8,128)(2,1)}, u32[]{:S(2)}) copy-start(bf16[2,256,768]{2,1,0:T(8,128)(2,1)} %get-tuple-element.53) | copy-start | bytes 2359300

commit v2 on v1

--- a/solution.py
+++ b/solution.py
@@ -92,16 +92,139 @@
             sums[tap] = term if sums[tap] is None else sums[tap] + term
 
 
+MESH = pl.DeviceIdType.MESH
+
+
+def spot():
+    dp = lax.axis_index("dp")
+    seq = lax.axis_index("seq")
+    return dict(dp=dp, seq=seq, x=dp // 8, zl=(dp // 4) % 2, y=dp % 4, zh=seq // 2, core=seq % 2)
+
+
+def seq_peer(me, zh, core):
+    return (me["dp"], zh * 2 + core)
+
+
+def axis_peer(me, axis, offset):
+    x, y, z = me["x"], me["y"], me["zh"] * 2 + me["zl"]
+    if axis == "x":
+        x = (x + offset) % 4
+    elif axis == "y":
+        y = (y + offset) % 4
+    else:
+        z = (z + offset) % 4
+    return ((x * 2 + z % 2) * 4 + y, (z // 2) * 2 + me["core"])
+
+
+def remote(src, dst, send, recv, device):
+    return pltpu.make_async_remote_copy(
+        src_ref=src, dst_ref=dst, send_sem=send, recv_sem=recv, device_id=device,
+        device_id_type=MESH,
+    )
+
+
+def arrived(ref, sem):
+    pltpu.make_async_copy(ref, ref, sem).wait()
+
+
+def greet(peers):
+    barrier = pltpu.get_barrier_semaphore()
+    for peer in peers:
+        pl.semaphore_signal(barrier, inc=1, device_id=peer, device_id_type=MESH)
+    pl.semaphore_wait(barrier, len(peers))
+
+
+ORDERS = (("x", "y", "z"), ("y", "z", "x"), ("z", "x", "y"))
+EARLY = (
+    (("x", "y", "z"), ("x", "y", "z"), ("y", "z", "x")),
+    (("y", "x", "z"), ("z", "x", "y"), ("z", "x", "y")),
+)
+
+
+def axis_spot(me, axis):
+    return me["zh"] * 2 + me["zl"] if axis == "z" else me[axis]
+
+
+def early_peer(me, stage, part, offset):
+    first, second = (EARLY[which][part][stage] for which in range(2))
+    pick = lambda a, b: jnp.where(me["core"] == 0, a, b)
+    peers = (axis_peer(me, first, offset), axis_peer(me, second, offset))
+    here = pick(axis_spot(me, first), axis_spot(me, second))
+    return here, tuple(pick(a, b) for a, b in zip(*peers))
+
+
 def ffn_kernel(
     x_ref, at_ref, ct_ref, mod_ref, alive_ref, perm_ref, ow_ref, ob_ref, f1_ref, f1b_ref,
     tap_ref, cb_ref, f2_ref, f2b_ref,
-    out_ref, fg_ref, go_ref, da_ref, dx_ref, s2_ref, sm_ref,
+    out_ref, s1_ref, go_ref, da_ref, dx_ref, s2_ref, sm_ref,
     x1_s, br_s, h2_s, h2t_s, dffn_s, u_s, duc_s, act_s, du_s, dact_s, ffn_s, dh2_s, acc_s,
-    fg_s, fg_sem,
+    ch_s, pre_s, r1_s, pair_sem, st_send, st_recv,
 ):
     step = pl.program_id(0)
-    core = lax.axis_index("seq") % 2
+    me = spot()
+    core = me["core"]
+    other = seq_peer(me, me["zh"], 1 - core)
     alive = alive_ref[0]
+
+    @pl.when(step == 0)
+    def _():
+        greet([axis_peer(me, axis, o) for axis in "xyz" for o in (1, 2, 3)] + [other])
+
+    def pair_copy(at):
+        slot = at % 2
+        return remote(
+            ch_s.at[slot, 1 - core], pre_s.at[slot], pair_sem.at[slot, 0], pair_sem.at[slot, 1],
+            other,
+        )
+
+    def first_copies(at):
+        slot = at % 2
+        out = []
+        for p in range(3):
+            for o in (1, 2, 3):
+                here, peer = early_peer(me, 0, p, o)
+                out.append(
+                    remote(
+                        ch_s.at[slot, core, p, (here + o) % 4], r1_s.at[slot, o - 1, p],
+                        st_send.at[slot, p, o - 1], st_recv.at[slot, p, o - 1], peer,
+                    )
+                )
+        return out
+
+    def first_send(at):
+        slot = at % 2
+        pair_copy(at).wait()
+        for p in range(3):
+
+            def add(a, _):
+                ch_s[slot, core, p, a] = ch_s[slot, core, p, a] + pre_s[slot, p, a]
+                return 0
+
+            lax.fori_loop(0, 4, add, 0)
+        for copy in first_copies(at):
+            copy.start()
+
+    def first_take(at):
+        slot = at % 2
+        for copy in first_copies(at):
+            copy.wait()
+        for p in range(3):
+            here, _peer = early_peer(me, 0, p, 1)
+            total = ch_s[slot, core, p, here].astype(F32)
+            for o in range(3):
+                total = total + r1_s[slot, o, p].astype(F32)
+            total = total.astype(BF16)
+
+            @pl.when(core == 0)
+            def _():
+                s1_ref[p, at] = total
+
+            @pl.when(core == 1)
+            def _():
+                for c in range(4):
+                    s1_ref[p, c, pl.ds(pl.multiple_of(at * 48, 16), 48)] = total[
+                        48 * c : 48 * c + 48
+                    ]
 
     @pl.when(step == 0)
     def _():
@@ -124,7 +247,7 @@
             return 0
 
         lax.fori_loop(0, 17, rows_b, 0)
-        for p in range(3):
+        for p in range(2):
             h2t_s[p] = mm_nt(perm_ref[p], h2_s[0:512, :]).astype(BF16)
         ffn_s[...] = jnp.zeros_like(ffn_s)
         dh2_s[...] = jnp.zeros_like(dh2_s)
@@ -133,6 +256,10 @@
         cols = slice(256 * j, 256 * j + 256)
         u_s[:, cols] = (mm(h2_s[...], f1_ref[:, cols]) + f1b_ref[:, cols].astype(F32)).astype(BF16)
         dact_s[:, cols] = mm_nt(dffn_s[...], f2_ref[cols, :])
+
+    @pl.when(step > 0)
+    def _():
+        first_send(step - 1)
 
     masks = side_masks()
 
@@ -189,9 +316,11 @@
 
     ffn_s[...] += mm(act_s[...], f2_ref[...])
     dh2_s[...] += mm_nt(du_s[...], f1_ref[...])
+    slot = step % 2
     for j in range(3):
         cols = slice(256 * j, 256 * j + 256)
-        fg_s[0, j, step] = mm(h2t_s[j], du_s[:, cols]).astype(BF16).reshape(4, 4, 48, 256)
+        got = mm(h2t_s[j // 2], du_s[:, cols]).astype(BF16)
+        ch_s[slot, 0, j] = got.reshape(4, 192, 256)
     for part in range(3):
         grad = mm_tn(act_s[...], dffn_s[0:512, 256 * part : 256 * part + 256]).astype(BF16)
         for zl in range(2):
@@ -199,25 +328,13 @@
                 for zh in range(2):
                     at = ((zl * 4 + y) * 2 + zh) * 48
                     z = zh * 2 + zl
-                    rows = grad[at : at + 48, :]
-                    if part == 0:
-                        fg_s[1, 0, z, step, y] = rows
-                    elif part == 1:
-                        fg_s[1, 1, step, y, z] = rows
-                    else:
-                        fg_s[1, 2, y, z, step] = rows
-
-    def moved(at, i):
-        spots = (
-            lambda ref: ref.at[0, :, at],
-            lambda ref: ref.at[1, 0, :, at],
-            lambda ref: ref.at[1, 1, at],
-            lambda ref: ref.at[1, 2, :, :, at],
-        )
-        return pltpu.make_async_copy(spots[i](fg_s), spots[i](fg_ref), fg_sem.at[at, i])
-
-    for i in range(4):
-        moved(step, i).start()
+                    a, c = (y, z) if part == 0 else (z, y)
+                    ch_s[slot, 1, part, a, 48 * c : 48 * c + 48] = grad[at : at + 48, :]
+    pair_copy(step).start()
+
+    @pl.when(step > 0)
+    def _():
+        first_take(step - 1)
 
     @pl.when(step == NFC - 1)
     def _():
@@ -253,13 +370,12 @@
         lax.fori_loop(0, 16, rows_c, 0)
         for i in range(6):
             sm_ref[i : i + 1, :] = jnp.sum(acc_s[i], axis=0, keepdims=True)
+        first_send(step)
         for p in range(3):
             h2t_s[p] = mm_nt(perm_ref[p], at_ref[0:512, :]).astype(BF16)
             go_ref[p] = mm(h2t_s[p], da_ref[:, 256 * p : 256 * p + 256]).astype(BF16)
         da_ref[...] = mm_nt(da_ref[...], ow_ref[...]).astype(BF16)
-        for at in range(NFC):
-            for i in range(4):
-                moved(at, i).wait()
+        first_take(step)
 
 
 def ffn_call(x, at, ct, mod, alive, perm, ow, ob, f1, f1b, taps, cb, f2, f2b):
@@ -280,7 +396,7 @@
         ],
         out_specs=[
             whole((512, D)),
-            pl.BlockSpec(memory_space=pl.ANY),
+            whole((3, 4, 192, 256)),
             whole((3, D, 256)),
             whole((512, D)), whole((512, D)),
             pl.BlockSpec((16, FC), lambda i: (0, i)),
@@ -288,7 +404,7 @@
         ],
         out_shape=[
             jax.ShapeDtypeStruct((512, D), BF16),
-            jax.ShapeDtypeStruct((2, 3, 4, 4, 4, 48, 256), BF16),
+            jax.ShapeDtypeStruct((3, 4, 192, 256), BF16),
             jax.ShapeDtypeStruct((3, D, 256), BF16),
             jax.ShapeDtypeStruct((512, D), BF16),
             jax.ShapeDtypeStruct((512, D), F32),
@@ -301,48 +417,16 @@
             pltpu.VMEM((576, FC), BF16), pltpu.VMEM((544, FC), BF16), pltpu.VMEM((512, FC), BF16),
             pltpu.VMEM((512, FC), BF16), pltpu.VMEM((544, FC), F32),
             pltpu.VMEM((512, D), F32), pltpu.VMEM((512, D), F32), pltpu.VMEM((6, 8, D), F32),
-            pltpu.VMEM((2, 3, 4, 4, 4, 48, 256), BF16), pltpu.SemaphoreType.DMA((NFC, 4)),
+            pltpu.VMEM((2, 2, 3, 4, 192, 256), BF16), pltpu.VMEM((2, 3, 4, 192, 256), BF16),
+            pltpu.VMEM((2, 3, 3, 192, 256), BF16), pltpu.SemaphoreType.DMA((2, 2)),
+            pltpu.SemaphoreType.DMA((2, 3, 3)), pltpu.SemaphoreType.DMA((2, 3, 3)),
         ],
         compiler_params=pltpu.CompilerParams(
-            dimension_semantics=("arbitrary",), vmem_limit_bytes=60 * 2**20
+            dimension_semantics=("arbitrary",), vmem_limit_bytes=60 * 2**20,
+            collective_id=3, has_side_effects=True,
         ),
         name="ffn",
     )(x, at, ct, mod, alive, perm, ow, ob, f1, f1b, taps, cb, f2, f2b)
-
-
-MESH = pl.DeviceIdType.MESH
-
-
-def spot():
-    dp = lax.axis_index("dp")
-    seq = lax.axis_index("seq")
-    return dict(dp=dp, seq=seq, x=dp // 8, zl=(dp // 4) % 2, y=dp % 4, zh=seq // 2, core=seq % 2)
-
-
-def seq_peer(me, zh, core):
-    return (me["dp"], zh * 2 + core)
-
-
-def axis_peer(me, axis, offset):
-    x, y, z = me["x"], me["y"], me["zh"] * 2 + me["zl"]
-    if axis == "x":
-        x = (x + offset) % 4
-    elif axis == "y":
-        y = (y + offset) % 4
-    else:
-        z = (z + offset) % 4
-    return ((x * 2 + z % 2) * 4 + y, (z // 2) * 2 + me["core"])
-
-
-def remote(src, dst, send, recv, device):
-    return pltpu.make_async_remote_copy(
-        src_ref=src, dst_ref=dst, send_sem=send, recv_sem=recv, device_id=device,
-        device_id_type=MESH,
-    )
-
-
-def arrived(ref, sem):
-    pltpu.make_async_copy(ref, ref, sem).wait()
 
 
 def place_matrix(count, flip, inverse):
@@ -365,32 +449,34 @@
 
 
 def attn_kernel(
-    lat_ref, ct_ref, mod_ref, w_ref, qb_ref, tap_ref, cb_ref,
-    x_out, ct_out, h_out, hcg_out, qkv_out, p_out, at_out,
-    xr_s, xh_s, x_s, c_s, h_s, hcg_s, sb_s, w_s, qkv_s, p_s, ag_s, at_s,
+    lat_ref, ct_ref, cond_ref, time_ref, table_ref, mw_ref, mb_ref, w_ref, qb_ref, tap_ref, cb_ref,
+    x_out, ct_out, h_out, hcg_out, qkv_out, p_out, at_out, mod_out,
+    xr_s, xh_s, x_s, c_s, h_s, hcg_s, sb_s, w_s, qkv_s, p_s, ag_s, at_s, mod_s, table_s, mw_s,
     send0, recv0, sem_pair, sem_loc,
 ):
     me = spot()
     zh, core, seq = me["zh"], me["core"], me["seq"]
     other = seq_peer(me, zh, 1 - core)
     w_load = pltpu.make_async_copy(w_ref, w_s, sem_loc.at[0])
-    w_load.start()
-
-    barrier = pltpu.get_barrier_semaphore()
-    for dz, dc in ((0, 1), (1, 0), (1, 1)):
-        pl.semaphore_signal(
-            barrier, inc=1, device_id=seq_peer(me, (zh + dz) % 2, (core + dc) % 2),
-            device_id_type=MESH,
-        )
-    pl.semaphore_wait(barrier, 3)
-
+    table_load = pltpu.make_async_copy(table_ref, table_s, sem_loc.at[10])
+    mw_load = pltpu.make_async_copy(mw_ref, mw_s, sem_loc.at[11])
+    for copy in (table_load, mw_load, w_load):
+        copy.start()
+
+    greet(
+        [
+            seq_peer(me, (zh + dz) % 2, (core + dc) % 2)
+            for dz, dc in ((0, 1), (1, 0), (1, 1))
+        ]
+    )
     slot = jnp.where(zh == 0, core, 1 - core)
     inner = jnp.logical_or(seq == 1, seq == 2)
     halo_core = jnp.where(seq == 1, 1, 0)
     halo_at = pl.multiple_of(jnp.where(seq == 1, 192, 0), 64)
 
-    def sends(act):
-        for a, ref in enumerate((lat_ref, ct_ref)):
+    def sends(arrays, act):
+        for a in arrays:
+            ref = (lat_ref, ct_ref)[a]
             for j in range(2):
                 own = jnp.logical_and(zh == j, core == zh)
                 main = (ref.at[j], xr_s.at[a, slot])
@@ -420,12 +506,24 @@
                         False,
                     )
 
-    sends(lambda make, local: make().start())
+    sends((0,), lambda make, local: make().start())
 
     flip = core == 1
     big = place_matrix(256, flip, False)
     small = place_matrix(64, flip, False)
-    shift1, scale1 = mod_ref[0:1, :], mod_ref[1:2, :]
+
+    table_load.wait()
+    here = lax.broadcasted_iota(jnp.int32, (8, table_s.shape[0]), 1)
+    one_hot = jnp.where(here == time_ref[zh], 1.0, 0.0).astype(BF16)
+    cond = jnp.where(zh == 0, cond_ref[0:1, :], cond_ref[1:2, :]) + mm(one_hot, table_s[...])
+    silu = (cond / (1.0 + jnp.exp(-cond))).astype(BF16)
+    mw_load.wait()
+    for i in range(6):
+        cols = slice(D * i, D * i + D)
+        mod_s[i : i + 1, :] = (mm(silu, mw_s[:, cols]) + mb_ref[:, cols])[0:1]
+    mod_s[6:7, :] = cond[0:1]
+    mod_s[7:8, :] = silu[0:1].astype(F32)
+    shift1, scale1 = mod_s[0:1, :], mod_s[1:2, :]
 
     def placed(a, into):
         for b in range(2):
@@ -435,6 +533,7 @@
         into[512:576, :] = mm(small, xh_s[a]).astype(BF16)
 
     placed(0, x_s)
+    sends((1,), lambda make, local: make().start())
 
     def rows_a(r, _):
         at = pl.ds(pl.multiple_of(r * 32, 32), 32)
@@ -446,6 +545,7 @@
     outs = [
         pltpu.make_async_copy(x_s, x_out, sem_loc.at[1]),
         pltpu.make_async_copy(h_s, h_out, sem_loc.at[2]),
+        pltpu.make_async_copy(mod_s, mod_out, sem_loc.at[12]),
     ]
     for copy in outs:
         copy.start()
@@ -543,24 +643,28 @@
         if not local:
             make().wait_send()
 
-    sends(finish)
+    sends((0, 1), finish)
 
 
 VMEM_SPEC = pl.BlockSpec(memory_space=pltpu.VMEM)
 ANY_SPEC = pl.BlockSpec(memory_space=pl.ANY)
-
-
-def attn_call(lat, ct, mod, w, qb, taps, cb):
+SMEM_SPEC = pl.BlockSpec(memory_space=pltpu.SMEM)
+
+
+def attn_call(lat, ct, cond, times, table, mw, mb, w, qb, taps, cb):
     G = (2, 8, 2, 16)
     shape = jax.ShapeDtypeStruct
     return pl.pallas_call(
         attn_kernel,
-        in_specs=[ANY_SPEC, ANY_SPEC, VMEM_SPEC, ANY_SPEC, VMEM_SPEC, VMEM_SPEC, VMEM_SPEC],
-        out_specs=[ANY_SPEC] * 7,
+        in_specs=[
+            ANY_SPEC, ANY_SPEC, VMEM_SPEC, SMEM_SPEC, ANY_SPEC, ANY_SPEC, VMEM_SPEC, ANY_SPEC,
+            VMEM_SPEC, VMEM_SPEC, VMEM_SPEC,
+        ],
+        out_specs=[ANY_SPEC] * 8,
         out_shape=[
             shape((576, D), BF16), shape((576, D), BF16), shape((576, D), BF16),
             shape(G + (D,), BF16), shape(G + (3 * D,), BF16), shape((24, 256, 256), BF16),
-            shape((9, 2, 2, 16, D), BF16),
+            shape((9, 2, 2, 16, D), BF16), shape((8, D), F32),
         ],
         scratch_shapes=[
             pltpu.VMEM((2, 2, 256, D), BF16), pltpu.VMEM((2, 64, D), BF16),
@@ -569,31 +673,26 @@
             pltpu.VMEM((D, 3 * D), BF16), pltpu.VMEM(G + (3 * D,), BF16),
             pltpu.VMEM((24, 256, 256), BF16), pltpu.VMEM(G + (D,), BF16),
             pltpu.VMEM((9, 2, 2, 16, D), BF16),
+            pltpu.VMEM((8, D), F32), pltpu.VMEM(table.shape, BF16), pltpu.VMEM(mw.shape, BF16),
             pltpu.SemaphoreType.DMA((2, 2, 2)), pltpu.SemaphoreType.DMA((2, 3)),
-            pltpu.SemaphoreType.DMA((6,)), pltpu.SemaphoreType.DMA((10,)),
+            pltpu.SemaphoreType.DMA((6,)), pltpu.SemaphoreType.DMA((13,)),
         ],
         compiler_params=pltpu.CompilerParams(
             collective_id=1, has_side_effects=True, vmem_limit_bytes=56 * 2**20
         ),
         name="attend",
-    )(lat, ct, mod, w, qb, taps, cb)
-
-
-ORDERS = (("x", "y", "z"), ("y", "z", "x"), ("z", "x", "y"))
-
-
-def axis_spot(me, axis):
-    return me["zh"] * 2 + me["zl"] if axis == "z" else me[axis]
+    )(lat, ct, cond, times, table, mw, mb, w, qb, taps, cb)
 
 
 def back_kernel(
-    da_ref, qkv_ref, p_ref, hcg_ref, h_ref, x_ref, dx_ref, mod_ref, w_ref, tap_ref, perm_ref,
-    o_ref, fg_ref, go_ref, s2_ref, sb_ref,
-    oret_out, iret_out, fe_out, fl_out, sm_out, dm_out,
-    qkv_s, p_s, w_s, perm_s, dag_s, dqkv_s, hct_s, dhc_s, dh_s, gh_s, ig_s, os_s, is_s,
-    own_s, pre_s, lg_s, prl_s, r1e, r1l, s1e, s1l, r2e, r2l, t3e, t3l, r3e, r3l, fe_s, fl_s,
-    acc_s, sv_s, sp_s, sr_s, sx_s, mp_s, mr_s, dm_s, smf_s,
-    loc, pair_sem, ret_send, ret_recv, st_send, st_recv, sx_send, sx_recv, dm_send, dm_recv,
+    da_ref, qkv_ref, p_ref, hcg_ref, h_ref, x_ref, dx_ref, mod_ref, time_ref, w_ref, mw_ref,
+    tap_ref, perm_ref, o_ref, s1_ref, go_ref, s2_ref, sb_ref,
+    oret_out, iret_out, fe_out, fl_out, se_out, sl_out, de_out, dl_out,
+    qkv_s, p_s, w_s, mw_s, perm_s, dag_s, dqkv_s, hct_s, dhc_s, dh_s, gh_s, ig_s, os_s, is_s,
+    lg_s, prl_s, r1l, s1l, r2e, r2l, t3e, t3l, r3e, r3l, fe_s, fl_s,
+    acc_s, sv_s, se_p, se_r, se_s, se_f, sl_p, sl_r, sl_s, sl_f, mp_s, mr_s, mpl_s, mrl_s,
+    item_s, de_s, dl_s,
+    loc, pair_sem, ret_send, ret_recv, st_send, st_recv, sm_send, sm_recv, dm_send, dm_recv,
 ):
     me = spot()
     zh, core = me["zh"], me["core"]
@@ -604,26 +703,48 @@
         pltpu.make_async_copy(w_ref, w_s, loc.at[2]),
         pltpu.make_async_copy(perm_ref, perm_s, loc.at[3]),
         pltpu.make_async_copy(da_ref.at[:, 0], dag_s.at[0], loc.at[4]),
-        pltpu.make_async_copy(fg_ref.at[core], own_s, loc.at[5]),
+        pltpu.make_async_copy(mw_ref, mw_s, loc.at[5]),
         pltpu.make_async_copy(go_ref, lg_s.at[1, :, 0], loc.at[6]),
     ]
-    for at in (4, 0, 1, 2, 3, 5, 6):
+    for at in (4, 0, 1, 3, 2, 6, 5):
         loads[at].start()
-    barrier = pltpu.get_barrier_semaphore()
     peers = [axis_peer(me, axis, o) for axis in "xyz" for o in (1, 2, 3)]
-    peers += [other, seq_peer(me, 1 - zh, 1 - core)]
-    for peer in peers:
-        pl.semaphore_signal(barrier, inc=1, device_id=peer, device_id_type=MESH)
-    pl.semaphore_wait(barrier, len(peers))
+    greet(peers + [other, seq_peer(me, 1 - zh, 1 - core)])
 
     da_copy = remote(da_ref.at[:, 1], dag_s.at[1], pair_sem.at[0, 0], pair_sem.at[0, 1], other)
     da_copy.start()
-    early = [
-        remote(fg_ref.at[1 - core, p], pre_s.at[p], pair_sem.at[1 + p, 0], pair_sem.at[1 + p, 1], other)
-        for p in range(3)
-    ]
-    for copy in early:
-        copy.start()
+
+    def stage_sends(stage, bufs, late):
+        out = []
+        for p in range(3):
+            for o in (1, 2, 3):
+                if late:
+                    axis = ORDERS[p][stage]
+                    here, peer = axis_spot(me, axis), axis_peer(me, axis, o)
+                else:
+                    here, peer = early_peer(me, stage, p, o)
+                src, dst = bufs(p, o, (here + o) % 4)
+                copy = remote(
+                    src, dst, st_send.at[late, stage, p, o - 1], st_recv.at[late, stage, p, o - 1],
+                    peer,
+                )
+                copy.start()
+                out.append(copy)
+        return out
+
+    def chunk(there, rows):
+        return pl.ds(pl.multiple_of(there * rows, 16), rows)
+
+    st2e = stage_sends(1, lambda p, o, b: (s1_ref.at[p, :, chunk(b, 48)], r2e.at[o - 1, p]), 0)
+    mp_s[...] = sb_ref[...]
+    mp_copy = remote(mp_s, mr_s, pair_sem.at[1, 0], pair_sem.at[1, 1], other)
+    mp_copy.start()
+    for half in range(2):
+        for q in range(2):
+            at = D * (2 * half + q)
+            se_p[half, 16 * q : 16 * q + 16, :] = s2_ref[:, at : at + D].astype(BF16)
+    se_copy = remote(se_p.at[1 - core], se_r, pair_sem.at[2, 0], pair_sem.at[2, 1], other)
+    se_copy.start()
 
     home = place_matrix(256, core == 1, True)
 
@@ -691,39 +812,109 @@
                 dqkv_s[half, :, pc, :, cols] = got[128 * half : 128 * half + 128].reshape(8, 16, 128)
         return 0
 
-    def stage_sends(stage, bufs, panels, late):
+    z_me = axis_spot(me, "z")
+
+    def small_stage(stage, sums, items, kind):
+        axis = "xyz"[stage]
+        spots = ((z_me, me["y"], me["x"]), (z_me, me["y"]), (z_me,))[stage]
+        if stage == 0:
+            ref = items.at[core, z_me, me["y"], me["x"]]
+        elif stage == 1:
+            ref = items.at[core, z_me, me["y"]]
+        else:
+            ref = items.at[core, z_me]
         out = []
-        for p in range(3):
-            axis = ORDERS[p][stage]
-            here = axis_spot(me, axis)
-            for o in (1, 2, 3):
-                there = (here + o) % 4
-                src, dst = bufs(p, o, there)
-                copy = remote(
-                    src, dst, st_send.at[late, stage, p, o - 1], st_recv.at[late, stage, p, o - 1],
-                    axis_peer(me, axis, o),
-                )
-                copy.start()
-                out.append(copy)
+        for o in (1, 2, 3):
+            peer = axis_peer(me, axis, o)
+            at = (kind, stage, o - 1)
+            out.append(
+                remote(sums.at[4 * stage], sums.at[4 * stage + o], sm_send.at[at], sm_recv.at[at], peer)
+            )
+            out.append(remote(ref, ref, dm_send.at[at], dm_recv.at[at], peer))
+        for copy in out:
+            copy.start()
         return out
 
-    def chunk(there, rows):
-        return pl.ds(pl.multiple_of(there * rows, 16), rows)
+    def small_take(stage, sums, items, kind, copies, last):
+        axis = "xyz"[stage]
+        for copy in copies:
+            copy.wait_send()
+        for o in (1, 2, 3):
+            at = (kind, stage, o - 1)
+            arrived(sums.at[4 * stage + o], sm_recv.at[at])
+            there = (axis_spot(me, axis) + 4 - o) % 4
+            if stage == 0:
+                ref = items.at[core, z_me, me["y"], there]
+            elif stage == 1:
+                ref = items.at[core, z_me, there]
+            else:
+                ref = items.at[core, there]
+            arrived(ref, dm_recv.at[at])
+        total = sums[4 * stage].astype(F32)
+        for o in (1, 2, 3):
+            total = total + sums[4 * stage + o].astype(F32)
+        if stage < 2:
+            sums[4 * stage + 4] = total.astype(BF16)
+        else:
+            last[...] = total
+
+    def lane_rows(values, count):
+        return [
+            values[i : i + 1, 128 * l : 128 * l + 128] for i in range(count) for l in range(6)
+        ]
+
+    ends = []
+
+    def spread(done, out, at):
+        for copy in (
+            pltpu.make_async_copy(done, out.at[core], loc.at[at]),
+            remote(done, out.at[core], pair_sem.at[at, 0], pair_sem.at[at, 1], other),
+        ):
+            copy.start()
+            ends.append(copy)
+
+    def second(own, recv, panels, p, here):
+        out = []
+        for k in range(panels):
+            total = own[p, k, chunk(here, 48), :].astype(F32)
+            for o in range(3):
+                total = total + recv[o, p, k].astype(F32)
+            out.append(total)
+        return out
 
     lax.fori_loop(0, 6, attend_back, 0)
-    loads[5].wait()
+    mp_copy.wait()
+    item_s[2:6, :] = (mp_s[0:4, :] + mr_s[0:4, :]).astype(BF16).astype(F32)
+    time_id = time_ref[zh]
+    stamp = jnp.ones((1, 128), F32)
+    rows = lane_rows(item_s[2:6, :], 4) + lane_rows(mod_ref[7:8, :], 1)
+    rows += [stamp * (time_id // 32).astype(F32), stamp * (time_id % 32).astype(F32)]
+    both = jnp.concatenate(rows, axis=0).astype(BF16)
+    de_s[core, z_me, me["y"], me["x"]] = jnp.where(core == 0, both[0:16], both[16:32])
+    se_copy.wait()
+    se_s[0] = (se_p[core].astype(F32) + se_r[...].astype(F32)).astype(BF16)
+    small = small_stage(0, se_s, de_s, 0)
+    for copy in st2e:
+        copy.wait()
     for p in range(3):
-        early[p].wait()
-
-        def add_early(k, _):
-            own_s[p, k] = own_s[p, k] + pre_s[p, k]
-            return 0
-
-        lax.fori_loop(0, 4, add_early, 0)
-    st1e = stage_sends(
-        0, lambda p, o, a: (own_s.at[p, :, chunk(a, 192)], r1e.at[o - 1, p]), 4, 0
-    )
+        got = second(s1_ref, r2e, 4, p, early_peer(me, 1, p, 1)[0])
+
+        @pl.when(core == 0)
+        def _():
+            for c in range(4):
+                t3e[p, c] = jnp.concatenate(
+                    [got[k][12 * c : 12 * c + 12] for k in range(4)], axis=0
+                ).astype(BF16)
+
+        @pl.when(core == 1)
+        def _():
+            for c in range(4):
+                t3e[p, c] = got[c].astype(BF16)
+
+    st3e = stage_sends(2, lambda p, o, c: (t3e.at[p, c], r3e.at[o - 1, p]), 0)
     lax.fori_loop(6, 12, attend_back, 0)
+    small_take(0, se_s, de_s, 0, small, se_f)
+    small = small_stage(1, se_s, de_s, 0)
 
     loads[2].wait()
     for half in (1, 0):
@@ -731,7 +922,7 @@
         dhc_s[half] = got.reshape(8, 2, 16, D)
         if half == 1:
             dhc_copy = remote(
-                dhc_s.at[1], dh_s.at[pl.ds(0, 8), 1], pair_sem.at[4, 0], pair_sem.at[4, 1], other
+                dhc_s.at[1], dh_s.at[pl.ds(0, 8), 1], pair_sem.at[3, 0], pair_sem.at[3, 1], other
             )
             dhc_copy.start()
     near = [
@@ -749,19 +940,17 @@
                 hct_s[p], dqkv_s[:, :, :, :, at : at + 256].reshape(512, 256)
             ).astype(BF16)
     late = [
-        remote(lg_s.at[1 - core, p], prl_s.at[p], pair_sem.at[5 + p, 0], pair_sem.at[5 + p, 1], other)
+        remote(lg_s.at[1 - core, p], prl_s.at[p], pair_sem.at[4 + p, 0], pair_sem.at[4 + p, 1], other)
         for p in range(3)
     ]
     for copy in late:
         copy.start()
     ones = jnp.ones((8, 512), BF16)
-    sv_s[64:96, :] = jnp.zeros((32, D), F32)
-    for row, at in ((74, 0), (75, 2 * D)):
+    for row, at in ((10, 0), (11, 2 * D)):
         sums = mm(ones, dqkv_s[:, :, :, :, at : at + D].reshape(512, D))
         sv_s[row : row + 1, :] = sums[0:1]
-    sv_s[76:78, :] = sb_ref[4:6, :]
-    for q in range(4):
-        sv_s[16 * q : 16 * q + 16, :] = s2_ref[:, D * q : D * q + D]
+    sv_s[12:14, :] = sb_ref[4:6, :]
+    sv_s[14:16, :] = jnp.zeros((2, D), F32)
 
     dhc_copy.wait()
     for copy in near:
@@ -804,8 +993,8 @@
                 rows_h = [rows_h[1], rows_h[2], sided_h(l + 2)]
         for t in range(9):
             total = jnp.sum(by_core(sums, t, core), axis=0, keepdims=True)
-            sv_s[64 + t : 65 + t, cols] = total
-        sv_s[73:74, cols] = jnp.sum(bias_sum, axis=0, keepdims=True)
+            sv_s[t : t + 1, cols] = total
+        sv_s[9:10, cols] = jnp.sum(bias_sum, axis=0, keepdims=True)
         return 0
 
     lax.fori_loop(0, D // 128, lanes, 0)
@@ -828,178 +1017,95 @@
         return 0
 
     lax.fori_loop(0, 16, rows_n, 0)
+    mpl_s[...] = jnp.zeros_like(mpl_s)
     for i in range(2):
-        mp_s[i : i + 1, :] = jnp.sum(acc_s[i], axis=0, keepdims=True)
-    mp_s[2:6, :] = sb_ref[0:4, :]
-    mp_s[6:8, :] = jnp.zeros((2, D), F32)
-    mp_copy = remote(mp_s, mr_s, pair_sem.at[8, 0], pair_sem.at[8, 1], other)
-    mp_copy.start()
+        mpl_s[i : i + 1, :] = jnp.sum(acc_s[i], axis=0, keepdims=True)
+    mpl_copy = remote(mpl_s, mrl_s, pair_sem.at[7, 0], pair_sem.at[7, 1], other)
+    mpl_copy.start()
     for half in range(2):
-        sp_s[half] = sv_s[48 * half : 48 * half + 48, :].astype(BF16)
-    sp_copy = remote(sp_s.at[1 - core], sr_s, pair_sem.at[9, 0], pair_sem.at[9, 1], other)
-    sp_copy.start()
-    for b in range(2):
-        is_s[b] = mm(home, ig_s[256 * b : 256 * b + 256, :]).astype(BF16)
-    give_back(1, lambda make, local: make().start())
-
+        sl_p[half] = sv_s[:, 384 * half : 384 * half + 384].astype(BF16)
+    sl_copy = remote(sl_p.at[1 - core], sl_r, pair_sem.at[8, 0], pair_sem.at[8, 1], other)
+    sl_copy.start()
     for copy in late:
         copy.wait()
     for p in range(3):
         for k in range(2):
             lg_s[core, p, k] = lg_s[core, p, k] + prl_s[p, k]
     st1l = stage_sends(
-        0, lambda p, o, a: (lg_s.at[core, p, :, chunk(a, 192)], r1l.at[o - 1, p]), 2, 1
-    )
-
-    mp_copy.wait()
-    item = (mp_s[...] + mr_s[...]).astype(BF16).astype(F32)
-    dm_rows = [item[i : i + 1, 128 * l : 128 * l + 128] for i in range(6) for l in range(6)]
-    z_me = axis_spot(me, "z")
-    dm_s[z_me, me["y"], me["x"]] = jnp.concatenate(
-        dm_rows + [jnp.zeros((12, 128), F32)], axis=0
-    ).astype(BF16)
-    sp_copy.wait()
-    sx_s[0] = (sp_s[core].astype(F32) + sr_s[...].astype(F32)).astype(BF16)
-
-    def small_stage(stage):
-        axis = "xyz"[stage]
-        view = (
-            lambda ref: ref.at[z_me, me["y"], me["x"]],
-            lambda ref: ref.at[z_me, me["y"]],
-            lambda ref: ref.at[z_me],
-        )[stage]
-        out = []
-        for o in (1, 2, 3):
-            out.append(
-                remote(
-                    sx_s.at[4 * stage], sx_s.at[4 * stage + o], sx_send.at[stage, o - 1],
-                    sx_recv.at[stage, o - 1], axis_peer(me, axis, o),
-                )
-            )
-            out.append(
-                remote(
-                    view(dm_s), view(dm_s), dm_send.at[stage, o - 1], dm_recv.at[stage, o - 1],
-                    axis_peer(me, axis, o),
-                )
-            )
-        for copy in out:
-            copy.start()
-        return out
-
-    def small_take(stage, copies):
-        axis = "xyz"[stage]
-        here = axis_spot(me, axis)
-        for copy in copies:
-            copy.wait_send()
-        for o in (1, 2, 3):
-            arrived(sx_s.at[4 * stage + o], sx_recv.at[stage, o - 1])
-            there = (here + 4 - o) % 4
-            view = (
-                lambda: dm_s.at[z_me, me["y"], there],
-                lambda: dm_s.at[z_me, there],
-                lambda: dm_s.at[there],
-            )[stage]
-            arrived(view(), dm_recv.at[stage, o - 1])
-        total = sx_s[4 * stage].astype(F32)
-        for o in (1, 2, 3):
-            total = total + sx_s[4 * stage + o].astype(F32)
-        if stage < 2:
-            sx_s[4 * stage + 4] = total.astype(BF16)
-        else:
-            smf_s[...] = total
-
-    def take(copies):
+        0, lambda p, o, a: (lg_s.at[core, p, :, chunk(a, 192)], r1l.at[o - 1, p]), 1
+    )
+    for b in range(2):
+        is_s[b] = mm(home, ig_s[256 * b : 256 * b + 256, :]).astype(BF16)
+    give_back(1, lambda make, local: make().start())
+    small_take(1, se_s, de_s, 0, small, se_f)
+    small = small_stage(2, se_s, de_s, 0)
+
+    mpl_copy.wait()
+    item_s[0:2, :] = (mpl_s[0:2, :] + mrl_s[0:2, :]).astype(BF16).astype(F32)
+    loads[5].wait()
+    cond = mod_ref[6:7, :]
+    d_silu = jnp.zeros((8, D), F32)
+    for i in range(6):
+        row = jnp.concatenate([item_s[i : i + 1, :]] * 8, axis=0).astype(BF16)
+        d_silu = d_silu + mm_nt(row, mw_s[:, D * i : D * i + D])
+    slope = 1.0 / (1.0 + jnp.exp(-cond))
+    d_cond = (slope * (1.0 + cond * (1.0 - slope))) * d_silu[0:1]
+    zeros = [jnp.zeros((1, 128), F32)]
+    rows_0 = jnp.concatenate(lane_rows(item_s[0:2, :], 2) + zeros * 4, axis=0)
+    rows_1 = jnp.concatenate(lane_rows(d_cond, 1) + zeros * 10, axis=0)
+    dl_s[core, z_me, me["y"], me["x"]] = jnp.where(core == 0, rows_0, rows_1).astype(BF16)
+    sl_copy.wait()
+    sl_s[0] = (sl_p[core].astype(F32) + sl_r[...].astype(F32)).astype(BF16)
+    small_l = small_stage(0, sl_s, dl_s, 1)
+
+    def finish(copies, own, recv, done, out, at, spots):
         for copy in copies:
             copy.wait()
-
-    def sum_one(own, recv, into, panels, p):
-        def body(k, _):
-            total = own(k).astype(F32)
+        for p in range(3):
+            total = own[p, spots[p]].astype(F32)
             for o in range(3):
-                total = total + recv[o, p, k].astype(F32)
-            into[p, k] = total.astype(BF16)
-            return 0
-
-        lax.fori_loop(0, panels, body, 0)
-
-    small = small_stage(0)
-    take(st1e)
+                total = total + recv[o, p].astype(F32)
+            done[p] = total
+        spread(done, out, at)
+
+    finish(st3e, t3e, r3e, fe_s, fe_out, 9, [early_peer(me, 2, p, 1)[0] for p in range(3)])
+    spots = [[axis_spot(me, ORDERS[p][stage]) for p in range(3)] for stage in range(3)]
+    for copy in st1l:
+        copy.wait()
     for p in range(3):
-        here = axis_spot(me, ORDERS[p][0])
-        sum_one(lambda k: own_s[p, k, chunk(here, 192), :], r1e, s1e, 4, p)
-    st2e = stage_sends(1, lambda p, o, b: (s1e.at[p, :, chunk(b, 48)], r2e.at[o - 1, p]), 4, 0)
-    small_take(0, small)
-    small = small_stage(1)
-    take(st1l)
+        for k in range(2):
+            total = lg_s[core, p, k, chunk(spots[0][p], 192), :].astype(F32)
+            for o in range(3):
+                total = total + r1l[o, p, k].astype(F32)
+            s1l[p, k] = total.astype(BF16)
+    st2l = stage_sends(1, lambda p, o, b: (s1l.at[p, :, chunk(b, 48)], r2l.at[o - 1, p]), 1)
+    small_take(0, sl_s, dl_s, 1, small_l, sl_f)
+    small_l = small_stage(1, sl_s, dl_s, 1)
+    small_take(2, se_s, de_s, 0, small, se_f)
+    spread(se_f, se_out, 10)
+    ends.append(
+        remote(de_s.at[core], de_s.at[core], pair_sem.at[11, 0], pair_sem.at[11, 1], other)
+    )
+    ends[-1].start()
+    for copy in st2l:
+        copy.wait()
     for p in range(3):
-        here = axis_spot(me, ORDERS[p][0])
-        sum_one(lambda k: lg_s[core, p, k, chunk(here, 192), :], r1l, s1l, 2, p)
-    st2l = stage_sends(1, lambda p, o, b: (s1l.at[p, :, chunk(b, 48)], r2l.at[o - 1, p]), 2, 1)
-
-    def second(own, recv, panels, p):
-        here = axis_spot(me, ORDERS[p][1])
-        out = []
-        for k in range(panels):
-            total = own[p, k, chunk(here, 48), :].astype(F32)
-            for o in range(3):
-                total = total + recv[o, p, k].astype(F32)
-            out.append(total)
-        return out
-
-    take(st2e)
-    for p in range(3):
-        got = second(s1e, r2e, 4, p)
-
-        @pl.when(core == 0)
-        def _():
-            for c in range(4):
-                t3e[p, c] = jnp.concatenate(
-                    [got[k][12 * c : 12 * c + 12] for k in range(4)], axis=0
-                ).astype(BF16)
-
-        @pl.when(core == 1)
-        def _():
-            for c in range(4):
-                t3e[p, c] = got[c].astype(BF16)
-
-    st3e = stage_sends(2, lambda p, o, c: (t3e.at[p, c], r3e.at[o - 1, p]), 4, 0)
-    small_take(1, small)
-    small = small_stage(2)
-    take(st2l)
-    for p in range(3):
-        got = second(s1l, r2l, 2, p)
+        got = second(s1l, r2l, 2, p, spots[1][p])
         for c in range(4):
             t3l[p, c] = jnp.concatenate(
                 [got[0][12 * c : 12 * c + 12], got[1][12 * c : 12 * c + 12], jnp.zeros((8, 256), F32)],
                 axis=0,
             ).astype(BF16)
-    st3l = stage_sends(2, lambda p, o, c: (t3l.at[p, c], r3l.at[o - 1, p]), 2, 1)
-
-    ends = []
-
-    def finish(copies, own, recv, done, out, at):
-        take(copies)
-        for p in range(3):
-            total = own[p, axis_spot(me, ORDERS[p][2])].astype(F32)
-            for o in range(3):
-                total = total + recv[o, p].astype(F32)
-            done[p] = total
-        spread(done, out, at)
-
-    def spread(done, out, at):
-        ends.append(pltpu.make_async_copy(done, out.at[core], loc.at[at]))
-        ends.append(
-            remote(done, out.at[core], pair_sem.at[at, 0], pair_sem.at[at, 1], other)
-        )
-        ends[-1].start()
-        ends[-2].start()
-
-    finish(st3e, t3e, r3e, fe_s, fe_out, 10)
-    small_take(2, small)
-    spread(smf_s, sm_out, 11)
-    ends.append(pltpu.make_async_copy(dm_s, dm_out, loc.at[9]))
+    st3l = stage_sends(2, lambda p, o, c: (t3l.at[p, c], r3l.at[o - 1, p]), 1)
+    small_take(1, sl_s, dl_s, 1, small_l, sl_f)
+    small_l = small_stage(2, sl_s, dl_s, 1)
+    finish(st3l, t3l, r3l, fl_s, fl_out, 12, spots[2])
+    small_take(2, sl_s, dl_s, 1, small_l, sl_f)
+    spread(sl_f, sl_out, 13)
+    ends.append(
+        remote(dl_s.at[core], dl_s.at[core], pair_sem.at[14, 0], pair_sem.at[14, 1], other)
+    )
     ends[-1].start()
-    finish(st3l, t3l, r3l, fl_s, fl_out, 12)
     for which in range(2):
         give_back(which, lambda make, local: None if local else make().wait_send())
         for item_slot in range(2):
@@ -1007,51 +1113,60 @@
             arrived(out.at[item_slot], ret_recv.at[which, item_slot])
     for copy in ends:
         copy.wait()
-
-
-def back_call(da, qkv, p, hcg, h, x, dx, mod, w, taps, perm, o, fg, go, s2, sb):
+    last = [
+        pltpu.make_async_copy(de_s, de_out, loc.at[11]),
+        pltpu.make_async_copy(dl_s, dl_out, loc.at[14]),
+    ]
+    for copy in last:
+        copy.start()
+    for copy in last:
+        copy.wait()
+
+
+def back_call(
+    da, qkv, p, hcg, h, x, dx, mod, times, w, mw, taps, perm, o, s1, go, s2, sb
+):
     G = (2, 8, 2, 16)
     shape = jax.ShapeDtypeStruct
     V = pltpu.VMEM
+    items = (2, 4, 4, 4, 16, 128)
+    DMA = pltpu.SemaphoreType.DMA
     return pl.pallas_call(
         back_kernel,
         in_specs=[
             ANY_SPEC, ANY_SPEC, ANY_SPEC, VMEM_SPEC, VMEM_SPEC, VMEM_SPEC, VMEM_SPEC, VMEM_SPEC,
-            ANY_SPEC, VMEM_SPEC, ANY_SPEC, VMEM_SPEC, ANY_SPEC, ANY_SPEC, VMEM_SPEC, VMEM_SPEC,
+            SMEM_SPEC, ANY_SPEC, ANY_SPEC, VMEM_SPEC, ANY_SPEC, VMEM_SPEC, VMEM_SPEC, ANY_SPEC,
+            VMEM_SPEC, VMEM_SPEC,
         ],
-        out_specs=[ANY_SPEC] * 6,
+        out_specs=[ANY_SPEC] * 8,
         out_shape=[
             shape((2, 256, D), BF16), shape((2, 256, D), BF16),
             shape((2, 3, 48, 256), F32), shape((2, 3, 32, 256), F32),
-            shape((2, 48, D), F32), shape((4, 4, 4, 48, 128), BF16),
+            shape((2, 32, D), F32), shape((2, 16, 384), F32),
+            shape(items, BF16), shape(items, BF16),
         ],
         scratch_shapes=[
             V(G + (3 * D,), BF16), V((24, 256, 256), BF16), V((D, 3 * D), BF16),
-            V((3, D, D), BF16), V(G + (D,), BF16), V(G + (3 * D,), BF16), V((3, D, 512), BF16),
-            V(G + (D,), BF16), V((9, 2, 2, 16, D), BF16), V((512, D), F32), V((512, D), BF16),
-            V((2, 256, D), BF16), V((2, 256, D), BF16),
-            V((3, 4, D, 256), BF16), V((3, 4, D, 256), BF16), V((2, 3, 2, D, 256), BF16),
-            V((3, 2, D, 256), BF16),
-            V((3, 3, 4, 192, 256), BF16), V((3, 3, 2, 192, 256), BF16),
-            V((3, 4, 192, 256), BF16), V((3, 2, 192, 256), BF16),
-            V((3, 3, 4, 48, 256), BF16), V((3, 3, 2, 48, 256), BF16),
-            V((3, 4, 48, 256), BF16), V((3, 4, 32, 256), BF16),
-            V((3, 3, 48, 256), BF16), V((3, 3, 32, 256), BF16),
-            V((3, 48, 256), F32), V((3, 32, 256), F32),
-            V((2, 8, D), F32), V((96, D), F32), V((2, 48, D), BF16), V((48, D), BF16),
-            V((12, 48, D), BF16), V((8, D), F32), V((8, D), F32), V((4, 4, 4, 48, 128), BF16),
-            V((48, D), F32),
-            pltpu.SemaphoreType.DMA((13,)), pltpu.SemaphoreType.DMA((13, 2)),
-            pltpu.SemaphoreType.DMA((2, 2)), pltpu.SemaphoreType.DMA((2, 2)),
-            pltpu.SemaphoreType.DMA((2, 3, 3, 3)), pltpu.SemaphoreType.DMA((2, 3, 3, 3)),
-            pltpu.SemaphoreType.DMA((3, 3)), pltpu.SemaphoreType.DMA((3, 3)),
-            pltpu.SemaphoreType.DMA((3, 3)), pltpu.SemaphoreType.DMA((3, 3)),
+            V(mw.shape, BF16), V((3, D, D), BF16), V(G + (D,), BF16), V(G + (3 * D,), BF16),
+            V((3, D, 512), BF16), V(G + (D,), BF16), V((9, 2, 2, 16, D), BF16), V((512, D), F32),
+            V((512, D), BF16), V((2, 256, D), BF16), V((2, 256, D), BF16),
+            V((2, 3, 2, D, 256), BF16), V((3, 2, D, 256), BF16), V((3, 3, 2, 192, 256), BF16),
+            V((3, 2, 192, 256), BF16), V((3, 3, 4, 48, 256), BF16), V((3, 3, 2, 48, 256), BF16),
+            V((3, 4, 48, 256), BF16), V((3, 4, 32, 256), BF16), V((3, 3, 48, 256), BF16),
+            V((3, 3, 32, 256), BF16), V((3, 48, 256), F32), V((3, 32, 256), F32),
+            V((2, 8, D), F32), V((16, D), F32),
+            V((2, 32, D), BF16), V((32, D), BF16), V((12, 32, D), BF16), V((32, D), F32),
+            V((2, 16, 384), BF16), V((16, 384), BF16), V((12, 16, 384), BF16), V((16, 384), F32),
+            V((8, D), F32), V((8, D), F32), V((8, D), F32), V((8, D), F32), V((8, D), F32),
+            V(items, BF16), V(items, BF16),
+            DMA((15,)), DMA((15, 2)), DMA((2, 2)), DMA((2, 2)), DMA((2, 3, 3, 3)),
+            DMA((2, 3, 3, 3)), DMA((2, 3, 3)), DMA((2, 3, 3)), DMA((2, 3, 3)), DMA((2, 3, 3)),
         ],
         compiler_params=pltpu.CompilerParams(
-            collective_id=2, has_side_effects=True, vmem_limit_bytes=62 * 2**20
+            collective_id=2, has_side_effects=True, vmem_limit_bytes=60 * 2**20
         ),
         name="back",
-    )(da, qkv, p, hcg, h, x, dx, mod, w, taps, perm, o, fg, go, s2, sb)
+    )(da, qkv, p, hcg, h, x, dx, mod, times, w, mw, taps, perm, o, s1, go, s2, sb)
 
 
 def perm_matrices():
@@ -1071,57 +1186,52 @@
 ):
     core = lax.axis_index("seq") % 2
     shard = lax.axis_index("dp") * 4 + lax.axis_index("seq")
-    all_cond = lax.all_gather(conditioning, "dp", axis=0, tiled=True)
-    all_times = lax.all_gather(timesteps, "dp", axis=0, tiled=True)
     alive = (lax.axis_index("seq") // 2 < item_counts).astype(F32)
     perm = (perm_matrices()[:, :, None] == np.arange(D)[None, None, :]).astype(BF16)
-    cond = conditioning.astype(F32) + time_table[timesteps].astype(F32)
-    silu_cond = jax.nn.silu(cond).astype(BF16)
-    mod = jnp.dot(silu_cond, mod_weight, preferred_element_type=F32) + mod_bias.astype(F32)
-    mod = jnp.pad(mod.reshape(2, 6, D), ((0, 0), (0, 2), (0, 0)))
-    mod = lax.dynamic_index_in_dim(mod, lax.axis_index("seq") // 2, 0, False)
     taps_attn = jnp.pad(conv_attn_weight.astype(F32), ((0, 7), (0, 0)))
     taps_ffn = jnp.pad(conv_ffn_weight.astype(F32), ((0, 7), (0, 0)))
     qkv_bias = jnp.concatenate(
         (query_bias.astype(F32), jnp.zeros((D,), F32), value_bias.astype(F32))
     )[None]
-    x, ct, h, hcg, qkv, p, at = attn_call(
-        latents.reshape(2, 256, D), cotangent.reshape(2, 256, D), mod, qkv_weight, qkv_bias,
-        taps_attn, conv_attn_bias[None],
-    )
-    out, fg, go, da, dx, s2, sb = ffn_call(
+    x, ct, h, hcg, qkv, p, at, mod = attn_call(
+        latents.reshape(2, 256, D), cotangent.reshape(2, 256, D), conditioning, timesteps,
+        time_table, mod_weight, mod_bias[None], qkv_weight, qkv_bias, taps_attn,
+        conv_attn_bias[None],
+    )
+    out, s1, go, da, dx, s2, sb = ffn_call(
         x, at.reshape(576, D), ct, mod, alive, perm, out_weight, out_bias[None], fc1_weight,
         fc1_bias[None], taps_ffn, conv_ffn_bias[None], fc2_weight, fc2_bias[None],
     )
-    out, ig, fe, fl, sm, dm = back_call(
-        da.reshape(8, 2, 2, 16, D), qkv, p, hcg.reshape(512, D), h, x, dx, mod, qkv_weight,
-        taps_attn, perm, out, fg.reshape(2, 3, 4, D, 256), go, s2, sb,
+    out, ig, fe, fl, se, sl, de, dl = back_call(
+        da.reshape(8, 2, 2, 16, D), qkv, p, hcg.reshape(512, D), h, x, dx, mod, timesteps,
+        qkv_weight, mod_weight, taps_attn, perm, out, s1, go, s2, sb,
     )
     output = out.reshape(2, 8, 32, D)
     input_grad = ig.reshape(2, 8, 32, D).astype(F32)
-    d_mod = dm.reshape(2, 2, 4, 4, 48, 128)[:, :, :, :, :36].transpose(3, 1, 2, 0, 4, 5)
-    d_mod = d_mod.reshape(64, 6 * D)
-    all_cond = all_cond.astype(F32) + time_table[all_times].astype(F32)
-    my_cond = lax.dynamic_slice_in_dim(all_cond, shard * 6, 6, axis=1)
-    my_silu = jax.nn.silu(my_cond).astype(BF16)
+
+    def items(v):
+        v = v.reshape(2, 2, 2, 4, 4, 16, 128).transpose(4, 2, 3, 1, 0, 5, 6)
+        return v.reshape(64, 32, 128)
+
+    early, late_rows = items(de), items(dl)
+    d_mod = jnp.concatenate((late_rows[:, :12], early[:, :24]), axis=1).reshape(64, 6 * D)
+    all_silu = early[:, 24:30].reshape(64, D)
+    all_times = (32.0 * early[:, 30, 0].astype(F32) + early[:, 31, 0].astype(F32)).astype(jnp.int32)
+    all_cond_grad = late_rows[:, 16:22].reshape(64, D)
+    cond_grad = lax.dynamic_slice_in_dim(
+        all_cond_grad, lax.axis_index("dp") * 2, 2, axis=0
+    ).astype(F32)
+    my_silu = lax.dynamic_slice_in_dim(all_silu, shard * 6, 6, axis=1)
     mod_grad = lax.dot_general(
         my_silu, d_mod, (((0,), (0,)), ((), ())), preferred_element_type=F32
     )
     mod_bias_grad = jnp.sum(
         lax.dynamic_slice_in_dim(d_mod, shard * 36, 36, axis=1).astype(F32), axis=0
     )
-
-    def silu_slope(v):
-        s = jax.nn.sigmoid(v)
-        return s * (1.0 + v * (1.0 - s))
-
-    own_d_mod = lax.dynamic_slice_in_dim(d_mod, lax.axis_index("dp") * 2, 2, axis=0)
-    cond_grad = silu_slope(cond) * mm_nt(own_d_mod, mod_weight)
-    my_rows = lax.dynamic_slice_in_dim(mod_weight, shard * 6, 6, axis=0)
-    my_cond_grad = silu_slope(my_cond) * mm_nt(d_mod, my_rows)
+    my_cond_grad = lax.dynamic_slice_in_dim(all_cond_grad, shard * 6, 6, axis=1)
     table_grad = jnp.dot(
-        (jnp.arange(1000)[:, None] == all_times[None, :]).astype(F32), my_cond_grad,
-        precision=lax.Precision.HIGHEST,
+        (jnp.arange(1000)[:, None] == all_times[None, :]).astype(BF16), my_cond_grad,
+        preferred_element_type=F32,
     )
     six = lambda v: lax.dynamic_slice_in_dim(v, core * 6, 6, axis=-2)
     fc1_grad = six(fe[0].reshape(3, 4, 12, 256)).transpose(2, 1, 0, 3).reshape(6, FF)
@@ -1135,10 +1245,11 @@
         axis=1,
     )
     out_grad = late[1, :, 0].transpose(1, 0, 2).reshape(6, D)
-    sums = sm.reshape(96, D)
-    wide = sums[:64].reshape(4, 16, D).transpose(1, 0, 2).reshape(16, FF)
+    wide = se.reshape(4, 16, D).transpose(1, 0, 2).reshape(16, FF)
     wide = lax.dynamic_slice_in_dim(wide, shard * 24, 24, axis=1)
-    slim = lax.dynamic_slice_in_dim(sums[64:80], shard * 6, 6, axis=1)
+    slim = lax.dynamic_slice_in_dim(
+        sl.transpose(1, 0, 2).reshape(16, D), shard * 6, 6, axis=1
+    )
     return (
         output, input_grad, cond_grad, table_grad, mod_grad, mod_bias_grad, slim[:9], slim[9],
         qkv_grad, slim[10], slim[11], out_grad, slim[12], fc1_grad, wide[10], wide[:9], wide[9],

time: 309 us -> 207 us (0.67)
  blocking collectives: 95.3 us -> 0 us
  matrix products: 13 us -> 1.93 us
  Pallas kernels: 176 us -> 181 us
    all_gather x1 -> x0, blocking collectives: 77.7 us -> none  [local(): all_cond = lax.all_gather(conditioning, 'dp', axis=0, tiled=True)]
    unnamed x1 -> x0, blocking collectives: 17.7 us -> none
    pallas_call x1, Pallas kernels: 59.7 us -> 73.6 us  [ffn_call(): pl.pallas_call(ffn_kernel, grid=(NFC,), in_specs=[whole((576, D)), whole(...]
    dot_general x4 -> x1, matrix products: 12 us -> 0.94 us  [local(): jnp.dot((jnp.arange(1000)[:, None] == all_times[None, :]).astype(BF16), m...]
    pallas_call x1, Pallas kernels: 78.3 us -> 70.5 us  [back_call(): pl.pallas_call(back_kernel, in_specs=[ANY_SPEC, ANY_SPEC, ANY_SPEC, VMEM_...]
where the time goes in v2:
time: 207 us; the launch traced here: 205 us
  Pallas kernels  181 us (87%)
  local copies, waits for them, and re-layouts  14 us (7%)
  other arithmetic  6.8 us (3%)
    pallas_call x1, Pallas kernels, ffn_call(): pl.pallas_call(ffn_kernel, grid=(NFC,), in_specs=[whole((576, D)), whole(...  73.6 us
    pallas_call x1, Pallas kernels, back_call(): pl.pallas_call(back_kernel, in_specs=[ANY_SPEC, ANY_SPEC, ANY_SPEC, VMEM_...  70.5 us
    pallas_call x1, Pallas kernels, attn_call(): pl.pallas_call(attn_kernel, in_specs=[ANY_SPEC, ANY_SPEC, VMEM_SPEC, SMEM...  36.7 us

profile of v2, /device:TPU:0, one launch (start us, length us, event | category | flops | bytes accessed | tf_op | source)
XLA Modules:
  0.0 205.1 jit_solution(10901856114267428108)
XLA Ops:
  1.3 1.4 pad_convert_fusion.1.tap_ref
  2.7 0.7 convert_element_type.54
  3.4 0.7 convert_element_type.55
  4.1 0.6 broadcast_in_dim.28.qb_ref
  4.7 1.3 broadcast_in_dim.26.mb_ref
  6.0 1.3 broadcast_in_dim.29.cb_ref
  7.3 0.0 copy-start.10
  7.3 36.7 %attend.1 = (bf16[576,768]{1,0:T(8,128)(2,1)}, bf16[576,768]{1,0:T(8,128)(2,1)}, bf16[576,768]{1,0:T(8,128)(2,1)}, bf16[2,8,2,16,768]{4,3,2,1,0:T(8,128)(2,1)}, ...) custom-call(bf16[2,256,768]{2,1,0:T(8,128)(2,1)} %bitcast.91, ...), custom_call_target="tpu_custom_call" | custom-call | tf_op jit(solution)/shard_map/attend/pallas_call | solution.py:657
  44.0 0.0 copy-done.5
  44.0 0.7 pad_convert_fusion.tap_ref
  44.7 0.0 copy-done.7
  44.7 0.6 broadcast_in_dim.31.f1b_ref
  45.3 0.0 copy-done.8
  45.3 0.6 broadcast_in_dim.32.cb_ref
  45.9 0.0 copy-done.9
  45.9 0.6 broadcast_in_dim.30.ob_ref
  46.5 0.0 copy-done.10
  46.5 0.6 broadcast_in_dim.33.f2b_ref
  47.1 73.6 %ffn.1 = (bf16[512,768]{1,0:T(8,128)(2,1)}, bf16[3,4,192,256]{3,2,1,0:T(8,128)(2,1)}, bf16[3,768,256]{2,1,0:T(8,128)(2,1)}, bf16[512,768]{1,0:T(8,128)(2,1)}, f3...) custom-call(bf16[576,768]{1,0:T(8,128)(2,1)} %get-tuple-element.42.x_ref, bf16[576,768]{1,0:T(8,128)(2,1)} %bitcast.88, ...), custom_call_target="tpu_custom_call" | custom-call | tf_op jit(solution)/shard_map/ffn/pallas_call | solution.py:383
  120.7 70.5 %back.1 = (bf16[2,256,768]{2,1,0:T(8,128)(2,1)}, bf16[2,256,768]{2,1,0:T(8,128)(2,1)}, f32[2,3,48,256]{3,2,1,0:T(8,128)}, f32[2,3,32,256]{3,2,1,0:T(8,128)}, f32...) custom-call(bf16[8,2,2,16,768]{4,3,2,1,0:T(8,128)(2,1)} %bitcast.90,, ...), custom_call_target="tpu_custom_call" | custom-call | tf_op jit(solution)/shard_map/back/pallas_call | solution.py:1134
  191.2 0.0 copy-start.2
  191.2 1.0 slice.71
  192.2 0.1 copy.78
  192.4 0.6 pad_maximum_fusion.1
  193.1 1.1 copy.74
  194.2 0.1 copy.73
  194.3 0.2 pad_maximum_fusion
  194.6 0.1 copy.100
  194.7 1.0 fusion.2
  195.7 0.6 convert_reduce_fusion
  196.3 0.1 fusion.7
  196.4 0.1 copy.88
  196.5 0.1 copy.89
  196.6 0.9 fusion
  197.6 0.0 copy-done.1
  197.6 1.3 convert.5
  199.0 0.1 copy.81
  199.0 0.7 reshape.145
  199.7 0.6 dynamic-slice_convert_fusion
  200.3 0.6 copy.92
  201.0 0.6 copy.87
  201.6 0.0 copy-done.4
  201.6 0.7 constant_dynamic-slice_fusion.1
  202.3 0.6 dynamic-slice_bitcast_fusion.3
  202.9 0.1 constant_dynamic-slice_fusion.3
  202.9 0.7 copy.84
  203.6 0.6 dynamic-slice_bitcast_fusion.2
  204.2 0.9 copy.106
  (33 shorter events, 0.4 us)
Async XLA Ops:
  7.3 36.7 %copy-start.5 = (bf16[9,3072]{1,0:T(8,128)(2,1)S(1)}, bf16[9,3072]{1,0:T(8,128)(2,1)}, u32[]{:S(2)}) copy-start(bf16[9,3072]{1,0:T(8,128)(2,1)} %param.39) | copy-start | bytes 165892
  7.3 37.4 %copy-start.7 = (bf16[3072]{0:T(1024)(128)(2,1)S(1)}, bf16[3072]{0:T(1024)(128)(2,1)}, u32[]{:S(2)}) copy-start(bf16[3072]{0:T(1024)(128)(2,1)} %param.38) | copy-start | bytes 18436
  7.3 38.0 %copy-start.8 = (bf16[3072]{0:T(1024)(128)(2,1)S(1)}, bf16[3072]{0:T(1024)(128)(2,1)}, u32[]{:S(2)}) copy-start(bf16[3072]{0:T(1024)(128)(2,1)} %param.40) | copy-start | bytes 18436
  7.3 38.7 %copy-start.9 = (bf16[768]{0:T(1024)(128)(2,1)S(1)}, bf16[768]{0:T(1024)(128)(2,1)}, u32[]{:S(2)}) copy-start(bf16[768]{0:T(1024)(128)(2,1)} %param.36) | copy-start | bytes 4612
  7.3 39.2 %copy-start.10 = (bf16[768]{0:T(1024)(128)(2,1)S(1)}, bf16[768]{0:T(1024)(128)(2,1)}, u32[]{:S(2)}) copy-start(bf16[768]{0:T(1024)(128)(2,1)} %param.42) | copy-start | bytes 4612
  191.2 3.1 %copy-start.2 = (bf16[2,4,4,4,16,128]{5,4,3,2,1,0:T(8,128)(2,1)S(1)}, bf16[2,4,4,4,16,128]{5,4,3,2,1,0:T(8,128)(2,1)}, u32[]{:S(2)}) copy-start(bf16[2,4,4,4,16,128]{5,4,3,2,1,0:T(8,128)(2,1)} %get-tuple-element.59) | copy-start | bytes 1572868
  194.5 3.0 %copy-start.1 = (bf16[2,256,768]{2,1,0:T(8,128)(2,1)S(1)}, bf16[2,256,768]{2,1,0:T(8,128)(2,1)}, u32[]{:S(2)}) copy-start(bf16[2,256,768]{2,1,0:T(8,128)(2,1)} %get-tuple-element.58) | copy-start | bytes 2359300
  196.3 2.6 %copy-start.3 = (f32[2,3,48,256]{3,2,1,0:T(8,128)S(1)}, f32[2,3,48,256]{3,2,1,0:T(8,128)}, u32[]{:S(2)}) copy-start(f32[2,3,48,256]{3,2,1,0:T(8,128)} %get-tuple-element.63) | copy-start | bytes 884740
  197.6 4.0 %copy-start.4 = (f32[2,32,768]{2,1,0:T(8,128)S(1)}, f32[2,32,768]{2,1,0:T(8,128)}, u32[]{:S(2)}) copy-start(f32[2,32,768]{2,1,0:T(8,128)} %get-tuple-element.64) | copy-start | bytes 589828
  198.9 4.0 %copy-start.6 = (f32[2,16,384]{2,1,0:T(8,128)S(1)}, f32[2,16,384]{2,1,0:T(8,128)}, u32[]{:S(2)}) copy-start(f32[2,16,384]{2,1,0:T(8,128)} %get-tuple-element.61) | copy-start | bytes 147460
  198.9 5.4 %copy-start = (bf16[2,256,768]{2,1,0:T(8,128)(2,1)S(1)}, bf16[2,256,768]{2,1,0:T(8,128)(2,1)}, u32[]{:S(2)}) copy-start(bf16[2,256,768]{2,1,0:T(8,128)(2,1)} %get-tuple-element.57) | copy-start | bytes 2359300

commit v3 on v2

--- a/solution.py
+++ b/solution.py
@@ -27,6 +27,10 @@
 
 def mm_tn(a, b):
     return lax.dot_general(a, b, (((0,), (0,)), ((), ())), preferred_element_type=F32)
+
+
+def row(v):
+    return v.astype(F32).reshape(1, v.shape[0])
 
 
 def fold8(v):
@@ -127,11 +131,19 @@
     pltpu.make_async_copy(ref, ref, sem).wait()
 
 
-def greet(peers):
+def hail(peers):
     barrier = pltpu.get_barrier_semaphore()
     for peer in peers:
         pl.semaphore_signal(barrier, inc=1, device_id=peer, device_id_type=MESH)
-    pl.semaphore_wait(barrier, len(peers))
+
+
+def heard(count):
+    pl.semaphore_wait(pltpu.get_barrier_semaphore(), count)
+
+
+def greet(peers):
+    hail(peers)
+    heard(len(peers))
 
 
 ORDERS = (("x", "y", "z"), ("y", "z", "x"), ("z", "x", "y"))
@@ -156,9 +168,9 @@
 def ffn_kernel(
     x_ref, at_ref, ct_ref, mod_ref, alive_ref, perm_ref, ow_ref, ob_ref, f1_ref, f1b_ref,
     tap_ref, cb_ref, f2_ref, f2b_ref,
-    out_ref, s1_ref, go_ref, da_ref, dx_ref, s2_ref, sm_ref,
+    out_ref, s1_ref, last_ref, dbr_ref, da_ref, dx_ref, s2_ref, sm_ref,
     x1_s, br_s, h2_s, h2t_s, dffn_s, u_s, duc_s, act_s, du_s, dact_s, ffn_s, dh2_s, acc_s,
-    ch_s, pre_s, r1_s, pair_sem, st_send, st_recv,
+    ch_s, pre_s, r1_s, bias_s, das_s, dar_s, pair_sem, st_send, st_recv,
 ):
     step = pl.program_id(0)
     me = spot()
@@ -168,7 +180,9 @@
 
     @pl.when(step == 0)
     def _():
-        greet([axis_peer(me, axis, o) for axis in "xyz" for o in (1, 2, 3)] + [other])
+        bias_s[0:1, :] = row(f1b_ref[...])
+        bias_s[1:2, :] = row(cb_ref[...])
+        hail([axis_peer(me, axis, o) for axis in "xyz" for o in (1, 2, 3)] + [other])
 
     def pair_copy(at):
         slot = at % 2
@@ -191,7 +205,7 @@
                 )
         return out
 
-    def first_send(at):
+    def pair_add(at):
         slot = at % 2
         pair_copy(at).wait()
         for p in range(3):
@@ -201,6 +215,9 @@
                 return 0
 
             lax.fori_loop(0, 4, add, 0)
+
+    def first_send(at):
+        pair_add(at)
         for copy in first_copies(at):
             copy.start()
 
@@ -228,25 +245,25 @@
 
     @pl.when(step == 0)
     def _():
-        br_s[...] = mm(at_ref[...], ow_ref[...]) + ob_ref[...].astype(F32)
+        br_s[...] = mm(at_ref[...], ow_ref[...]) + row(ob_ref[...])
         shift2, scale2, gate1, gate2 = (mod_ref[i : i + 1, :] for i in (3, 4, 2, 5))
 
         def rows_a(r, _):
-            at = pl.ds(pl.multiple_of(r * 32, 32), 32)
+            at = pl.ds(pl.multiple_of(r * 96, 96), 96)
             x1 = x_ref[at, :].astype(F32) + gate1 * br_s[at, :]
             x1_s[at, :] = x1
             n2, _unused = norm_parts(x1)
             h2_s[at, :] = (n2 * (1.0 + scale2) + shift2).astype(BF16)
             return 0
 
-        lax.fori_loop(0, 18, rows_a, 0)
+        lax.fori_loop(0, 6, rows_a, 0)
 
         def rows_b(r, _):
-            at = pl.ds(pl.multiple_of(r * 32, 32), 32)
+            at = pl.ds(pl.multiple_of(r * 272, 16), 272)
             dffn_s[at, :] = (ct_ref[at, :].astype(F32) * alive * gate2).astype(BF16)
             return 0
 
-        lax.fori_loop(0, 17, rows_b, 0)
+        lax.fori_loop(0, 2, rows_b, 0)
         for p in range(2):
             h2t_s[p] = mm_nt(perm_ref[p], h2_s[0:512, :]).astype(BF16)
         ffn_s[...] = jnp.zeros_like(ffn_s)
@@ -254,8 +271,12 @@
 
     for j in range(3):
         cols = slice(256 * j, 256 * j + 256)
-        u_s[:, cols] = (mm(h2_s[...], f1_ref[:, cols]) + f1b_ref[:, cols].astype(F32)).astype(BF16)
+        u_s[:, cols] = (mm(h2_s[...], f1_ref[:, cols]) + bias_s[0:1, pl.ds(pl.multiple_of(step * FC + 256 * j, 256), 256)]).astype(BF16)
         dact_s[:, cols] = mm_nt(dffn_s[...], f2_ref[cols, :])
+
+    @pl.when(step == 0)
+    def _():
+        heard(10)
 
     @pl.when(step > 0)
     def _():
@@ -265,9 +286,10 @@
 
     def lanes(j, _):
         cols = pl.ds(pl.multiple_of(j * 128, 128), 128)
-        taps = [tap_ref[t : t + 1, cols] for t in range(9)]
+        taps = tap_ref[:, cols].astype(F32)
+        taps = [taps[t : t + 1] for t in range(9)]
         taps = [by_core(taps, t, core) for t in range(9)]
-        offset = cb_ref[:, cols].astype(F32)
+        offset = bias_s[1:2, pl.ds(pl.multiple_of(step * FC + j * 128, 128), 128)]
 
         def sided(ref, l):
             return with_sides(
@@ -314,8 +336,6 @@
 
     lax.fori_loop(0, FC // 128, lanes, 0)
 
-    ffn_s[...] += mm(act_s[...], f2_ref[...])
-    dh2_s[...] += mm_nt(du_s[...], f1_ref[...])
     slot = step % 2
     for j in range(3):
         cols = slice(256 * j, 256 * j + 256)
@@ -331,6 +351,8 @@
                     a, c = (y, z) if part == 0 else (z, y)
                     ch_s[slot, 1, part, a, 48 * c : 48 * c + 48] = grad[at : at + 48, :]
     pair_copy(step).start()
+    ffn_s[...] += mm(act_s[...], f2_ref[...])
+    dh2_s[...] += mm_nt(du_s[...], f1_ref[...])
 
     @pl.when(step > 0)
     def _():
@@ -340,10 +362,10 @@
     def _():
         shift2, scale2, gate1, gate2 = (mod_ref[i : i + 1, :] for i in (3, 4, 2, 5))
         acc_s[...] = jnp.zeros_like(acc_s)
-        f2b = f2b_ref[...].astype(F32)
+        f2b = row(f2b_ref[...])
 
         def rows_c(r, _):
-            at = pl.ds(pl.multiple_of(r * 32, 32), 32)
+            at = pl.ds(pl.multiple_of(r * 128, 128), 128)
             x1 = x1_s[at, :]
             ffn = ffn_s[at, :] + f2b
             dy = ct_ref[at, :].astype(F32) * alive
@@ -358,7 +380,7 @@
             )
             dx_ref[at, :] = dx1
             dbr = (dx1 * gate1).astype(BF16)
-            da_ref[at, :] = dbr
+            dbr_ref[pl.ds(2 * r, 2)] = dbr.reshape(2, 2, 2, 16, D)
             acc_s[0] += fold8(dx1 * br_s[at, :])
             acc_s[1] += fold8(dh2)
             acc_s[2] += fold8(dh2 * n2)
@@ -367,15 +389,19 @@
             acc_s[5] += fold8(dffn_s[at, :].astype(F32))
             return 0
 
-        lax.fori_loop(0, 16, rows_c, 0)
+        lax.fori_loop(0, 4, rows_c, 0)
         for i in range(6):
             sm_ref[i : i + 1, :] = jnp.sum(acc_s[i], axis=0, keepdims=True)
-        first_send(step)
-        for p in range(3):
-            h2t_s[p] = mm_nt(perm_ref[p], at_ref[0:512, :]).astype(BF16)
-            go_ref[p] = mm(h2t_s[p], da_ref[:, 256 * p : 256 * p + 256]).astype(BF16)
-        da_ref[...] = mm_nt(da_ref[...], ow_ref[...]).astype(BF16)
-        first_take(step)
+        halves = [dbr_ref[:, parity].reshape(256, D) for parity in range(2)]
+        odd = mm_nt(halves[1], ow_ref[...]).astype(BF16)
+        das_s[...] = odd.reshape(8, 2, 16, D)
+        da_copy = remote(das_s, dar_s, pair_sem.at[2, 0], pair_sem.at[2, 1], other)
+        da_copy.start()
+        da_ref[0] = mm_nt(halves[0], ow_ref[...]).astype(BF16).reshape(8, 2, 16, D)
+        pair_add(step)
+        last_ref[...] = ch_s[step % 2, core]
+        da_copy.wait()
+        da_ref[1] = dar_s[...]
 
 
 def ffn_call(x, at, ct, mod, alive, perm, ow, ob, f1, f1b, taps, cb, f2, f2b):
@@ -386,39 +412,41 @@
         in_specs=[
             whole((576, D)), whole((576, D)), whole((576, D)), whole((8, D)),
             pl.BlockSpec(memory_space=pltpu.SMEM),
-            whole((3, D, D)), whole((D, D)), whole((1, D)),
+            whole((2, D, D)), whole((D, D)), whole((D,)),
             pl.BlockSpec((D, FC), lambda i: (0, i)),
-            pl.BlockSpec((1, FC), lambda i: (0, i)),
-            pl.BlockSpec((16, FC), lambda i: (0, i)),
-            pl.BlockSpec((1, FC), lambda i: (0, i)),
+            whole((FF,)),
+            pl.BlockSpec((9, FC), lambda i: (0, i)),
+            whole((FF,)),
             pl.BlockSpec((FC, D), lambda i: (i, 0)),
-            whole((1, D)),
+            whole((D,)),
         ],
         out_specs=[
             whole((512, D)),
-            whole((3, 4, 192, 256)),
-            whole((3, D, 256)),
-            whole((512, D)), whole((512, D)),
+            whole((3, 4, 192, 256)), whole((3, 4, 192, 256)),
+            whole((8, 2, 2, 16, D)), whole((2, 8, 2, 16, D)), whole((512, D)),
             pl.BlockSpec((16, FC), lambda i: (0, i)),
             whole((8, D)),
         ],
         out_shape=[
             jax.ShapeDtypeStruct((512, D), BF16),
             jax.ShapeDtypeStruct((3, 4, 192, 256), BF16),
-            jax.ShapeDtypeStruct((3, D, 256), BF16),
-            jax.ShapeDtypeStruct((512, D), BF16),
+            jax.ShapeDtypeStruct((3, 4, 192, 256), BF16),
+            jax.ShapeDtypeStruct((8, 2, 2, 16, D), BF16),
+            jax.ShapeDtypeStruct((2, 8, 2, 16, D), BF16),
             jax.ShapeDtypeStruct((512, D), F32),
             jax.ShapeDtypeStruct((16, FF), F32),
             jax.ShapeDtypeStruct((8, D), F32),
         ],
         scratch_shapes=[
             pltpu.VMEM((576, D), F32), pltpu.VMEM((576, D), F32), pltpu.VMEM((576, D), BF16),
-            pltpu.VMEM((3, D, 512), BF16), pltpu.VMEM((544, D), BF16),
+            pltpu.VMEM((2, D, 512), BF16), pltpu.VMEM((544, D), BF16),
             pltpu.VMEM((576, FC), BF16), pltpu.VMEM((544, FC), BF16), pltpu.VMEM((512, FC), BF16),
             pltpu.VMEM((512, FC), BF16), pltpu.VMEM((544, FC), F32),
             pltpu.VMEM((512, D), F32), pltpu.VMEM((512, D), F32), pltpu.VMEM((6, 8, D), F32),
             pltpu.VMEM((2, 2, 3, 4, 192, 256), BF16), pltpu.VMEM((2, 3, 4, 192, 256), BF16),
-            pltpu.VMEM((2, 3, 3, 192, 256), BF16), pltpu.SemaphoreType.DMA((2, 2)),
+            pltpu.VMEM((2, 3, 3, 192, 256), BF16), pltpu.VMEM((8, FF), F32),
+            pltpu.VMEM((8, 2, 16, D), BF16), pltpu.VMEM((8, 2, 16, D), BF16),
+            pltpu.SemaphoreType.DMA((3, 2)),
             pltpu.SemaphoreType.DMA((2, 3, 3)), pltpu.SemaphoreType.DMA((2, 3, 3)),
         ],
         compiler_params=pltpu.CompilerParams(
@@ -449,9 +477,10 @@
 
 
 def attn_kernel(
-    lat_ref, ct_ref, cond_ref, time_ref, table_ref, mw_ref, mb_ref, w_ref, qb_ref, tap_ref, cb_ref,
+    lat_ref, ct_ref, cond_ref, time_ref, table_ref, mw_ref, mb_ref, w_ref, qb_ref, vb_ref,
+    tap_ref, cb_ref,
     x_out, ct_out, h_out, hcg_out, qkv_out, p_out, at_out, mod_out,
-    xr_s, xh_s, x_s, c_s, h_s, hcg_s, sb_s, w_s, qkv_s, p_s, ag_s, at_s, mod_s, table_s, mw_s,
+    xr_s, xh_s, x_s, c_s, h_s, hcg_s, sb_s, w_s, qkv_s, p_s, ag_s, at_s, mod_s, table_s, mw_s, cb_s,
     send0, recv0, sem_pair, sem_loc,
 ):
     me = spot()
@@ -520,7 +549,7 @@
     mw_load.wait()
     for i in range(6):
         cols = slice(D * i, D * i + D)
-        mod_s[i : i + 1, :] = (mm(silu, mw_s[:, cols]) + mb_ref[:, cols])[0:1]
+        mod_s[i : i + 1, :] = (mm(silu, mw_s[:, cols]) + row(mb_ref[cols]))[0:1]
     mod_s[6:7, :] = cond[0:1]
     mod_s[7:8, :] = silu[0:1].astype(F32)
     shift1, scale1 = mod_s[0:1, :], mod_s[1:2, :]
@@ -536,12 +565,12 @@
     sends((1,), lambda make, local: make().start())
 
     def rows_a(r, _):
-        at = pl.ds(pl.multiple_of(r * 32, 32), 32)
+        at = pl.ds(pl.multiple_of(r * 96, 96), 96)
         n1, _unused = norm_parts(x_s[at, :].astype(F32))
         h_s[at, :] = (n1 * (1.0 + scale1) + shift1).astype(BF16)
         return 0
 
-    lax.fori_loop(0, 18, rows_a, 0)
+    lax.fori_loop(0, 6, rows_a, 0)
     outs = [
         pltpu.make_async_copy(x_s, x_out, sem_loc.at[1]),
         pltpu.make_async_copy(h_s, h_out, sem_loc.at[2]),
@@ -553,9 +582,10 @@
 
     def lanes(j, _):
         cols = pl.ds(pl.multiple_of(j * 128, 128), 128)
-        taps = [tap_ref[t : t + 1, cols] for t in range(9)]
+        taps = tap_ref[:, cols].astype(F32)
+        taps = [taps[t : t + 1] for t in range(9)]
         taps = [by_core(taps, t, core) for t in range(9)]
-        offset = cb_ref[:, cols].astype(F32)
+        offset = cb_s[0:1, cols]
 
         def sided(l):
             return with_sides(
@@ -577,14 +607,19 @@
             rows = [rows[1], rows[2], sided(l + 2) if l < 15 else None]
         return 0
 
+    cb_s[0:1, :] = row(cb_ref[...])
     lax.fori_loop(0, D // 128, lanes, 0)
     hc_copy = remote(sb_s, hcg_s.at[1], sem_pair.at[0], sem_pair.at[1], other)
     hc_copy.start()
     w_load.wait()
 
     def project(half):
-        got = mm(hcg_s[half].reshape(256, D), w_s[...]) + qb_ref[...]
-        qkv_s[half] = got.astype(BF16).reshape(8, 2, 16, 3 * D)
+        for i, bias in enumerate((qb_ref, None, vb_ref)):
+            cols = slice(D * i, D * i + D)
+            got = mm(hcg_s[half].reshape(256, D), w_s[:, cols])
+            if bias is not None:
+                got = got + row(bias[...])
+            qkv_s[half, :, :, :, cols] = got.astype(BF16).reshape(8, 2, 16, D)
 
     project(0)
     hc_copy.wait()
@@ -618,7 +653,7 @@
             ag_s[half, :, pc, :, cols] = o[128 * half : 128 * half + 128].reshape(8, 16, 128)
         return 0
 
-    lax.fori_loop(0, 12, attend, 0)
+    lax.fori_loop(0, 12, attend, 0, unroll=2)
     back = [
         remote(ag_s.at[1], at_s.at[pl.ds(0, 8), 1], sem_pair.at[2], sem_pair.at[3], other),
         remote(ag_s.at[0, 7], at_s.at[8, 1], sem_pair.at[4], sem_pair.at[5], other),
@@ -651,14 +686,14 @@
 SMEM_SPEC = pl.BlockSpec(memory_space=pltpu.SMEM)
 
 
-def attn_call(lat, ct, cond, times, table, mw, mb, w, qb, taps, cb):
+def attn_call(lat, ct, cond, times, table, mw, mb, w, qb, vb, taps, cb):
     G = (2, 8, 2, 16)
     shape = jax.ShapeDtypeStruct
     return pl.pallas_call(
         attn_kernel,
         in_specs=[
             ANY_SPEC, ANY_SPEC, VMEM_SPEC, SMEM_SPEC, ANY_SPEC, ANY_SPEC, VMEM_SPEC, ANY_SPEC,
-            VMEM_SPEC, VMEM_SPEC, VMEM_SPEC,
+            VMEM_SPEC, VMEM_SPEC, VMEM_SPEC, VMEM_SPEC,
         ],
         out_specs=[ANY_SPEC] * 8,
         out_shape=[
@@ -674,6 +709,7 @@
             pltpu.VMEM((24, 256, 256), BF16), pltpu.VMEM(G + (D,), BF16),
             pltpu.VMEM((9, 2, 2, 16, D), BF16),
             pltpu.VMEM((8, D), F32), pltpu.VMEM(table.shape, BF16), pltpu.VMEM(mw.shape, BF16),
+            pltpu.VMEM((8, D), F32),
             pltpu.SemaphoreType.DMA((2, 2, 2)), pltpu.SemaphoreType.DMA((2, 3)),
             pltpu.SemaphoreType.DMA((6,)), pltpu.SemaphoreType.DMA((13,)),
         ],
@@ -681,42 +717,40 @@
             collective_id=1, has_side_effects=True, vmem_limit_bytes=56 * 2**20
         ),
         name="attend",
-    )(lat, ct, cond, times, table, mw, mb, w, qb, taps, cb)
+    )(lat, ct, cond, times, table, mw, mb, w, qb, vb, taps, cb)
 
 
 def back_kernel(
-    da_ref, qkv_ref, p_ref, hcg_ref, h_ref, x_ref, dx_ref, mod_ref, time_ref, w_ref, mw_ref,
-    tap_ref, perm_ref, o_ref, s1_ref, go_ref, s2_ref, sb_ref,
+    da_ref, qkv_ref, p_ref, hcg_hbm, h_hbm, x_hbm, dx_hbm, mod_ref, time_ref, w_ref, mw_ref,
+    tap_ref, perm_ref, o_hbm, s1_ref, last_hbm, dbr_hbm, at_hbm, s2_ref, sb_ref,
     oret_out, iret_out, fe_out, fl_out, se_out, sl_out, de_out, dl_out,
     qkv_s, p_s, w_s, mw_s, perm_s, dag_s, dqkv_s, hct_s, dhc_s, dh_s, gh_s, ig_s, os_s, is_s,
-    lg_s, prl_s, r1l, s1l, r2e, r2l, t3e, t3l, r3e, r3l, fe_s, fl_s,
+    lg_s, prl_s, s1_s, r1x, r1l, s1l, r2e, r2l, t3e, t3l, r3e, r3l, fe_s, fl_s,
     acc_s, sv_s, se_p, se_r, se_s, se_f, sl_p, sl_r, sl_s, sl_f, mp_s, mr_s, mpl_s, mrl_s,
-    item_s, de_s, dl_s,
+    item_s, de_s, dl_s, hcg_ref, h_ref, x_ref, dx_ref, o_ref, last_ref, dbr_ref, at_ref,
     loc, pair_sem, ret_send, ret_recv, st_send, st_recv, sm_send, sm_recv, dm_send, dm_recv,
 ):
     me = spot()
     zh, core = me["zh"], me["core"]
     other = seq_peer(me, zh, 1 - core)
     loads = [
-        pltpu.make_async_copy(qkv_ref, qkv_s, loc.at[0]),
-        pltpu.make_async_copy(p_ref, p_s, loc.at[1]),
-        pltpu.make_async_copy(w_ref, w_s, loc.at[2]),
-        pltpu.make_async_copy(perm_ref, perm_s, loc.at[3]),
-        pltpu.make_async_copy(da_ref.at[:, 0], dag_s.at[0], loc.at[4]),
-        pltpu.make_async_copy(mw_ref, mw_s, loc.at[5]),
-        pltpu.make_async_copy(go_ref, lg_s.at[1, :, 0], loc.at[6]),
+        pltpu.make_async_copy(*pair, loc.at[15 + at])
+        for at, pair in enumerate((
+            (perm_ref, perm_s), (at_hbm, at_ref), (dbr_hbm, dbr_ref), (hcg_hbm, hcg_ref),
+            (last_hbm, last_ref), (o_hbm, o_ref), (da_ref, dag_s), (qkv_ref, qkv_s),
+            (p_ref, p_s), (w_ref, w_s), (s1_ref, s1_s), (h_hbm, h_ref), (x_hbm, x_ref),
+            (dx_hbm, dx_ref), (mw_ref, mw_s),
+        ))
     ]
-    for at in (4, 0, 1, 3, 2, 6, 5):
-        loads[at].start()
+    for load in loads:
+        load.start()
     peers = [axis_peer(me, axis, o) for axis in "xyz" for o in (1, 2, 3)]
-    greet(peers + [other, seq_peer(me, 1 - zh, 1 - core)])
-
-    da_copy = remote(da_ref.at[:, 1], dag_s.at[1], pair_sem.at[0, 0], pair_sem.at[0, 1], other)
-    da_copy.start()
-
-    def stage_sends(stage, bufs, late):
+    peers += [other, seq_peer(me, 1 - zh, 1 - core)]
+    hail(peers)
+
+    def stage_sends(stage, bufs, late, parts=(0, 1, 2)):
         out = []
-        for p in range(3):
+        for p in parts:
             for o in (1, 2, 3):
                 if late:
                     axis = ORDERS[p][stage]
@@ -735,7 +769,37 @@
     def chunk(there, rows):
         return pl.ds(pl.multiple_of(there * rows, 16), rows)
 
-    st2e = stage_sends(1, lambda p, o, b: (s1_ref.at[p, :, chunk(b, 48)], r2e.at[o - 1, p]), 0)
+    home = place_matrix(256, core == 1, True)
+
+    def give_back(which, act):
+        ref, out = ((os_s, oret_out), (is_s, iret_out))[which]
+        for b in range(2):
+            to_core = jnp.where(core == 0, b, 1 - b)
+            own = jnp.logical_and(zh == core, b == 0)
+
+            @pl.when(own)
+            def _():
+                act(lambda: pltpu.make_async_copy(ref.at[b], out.at[zh], ret_recv.at[which, zh]), True)
+
+            @pl.when(jnp.logical_not(own))
+            def _():
+                act(
+                    lambda: remote(
+                        ref.at[b], out.at[zh], ret_send.at[which, b], ret_recv.at[which, zh],
+                        seq_peer(me, core, to_core),
+                    ),
+                    False,
+                )
+
+    for load in loads[:4]:
+        load.wait()
+    for p in range(3):
+        at_t = mm_nt(perm_s[p], at_ref[0:512, :]).astype(BF16)
+        lg_s[1, p, 0] = mm(at_t, dbr_ref[:, 256 * p : 256 * p + 256]).astype(BF16)
+        hct_s[p] = mm_nt(perm_s[p], hcg_ref[...]).astype(BF16)
+    heard(len(peers))
+    loads[4].wait()
+    st1x = stage_sends(0, lambda p, o, a: (last_ref.at[p, a], r1x.at[o - 1, p]), 0)
     mp_s[...] = sb_ref[...]
     mp_copy = remote(mp_s, mr_s, pair_sem.at[1, 0], pair_sem.at[1, 1], other)
     mp_copy.start()
@@ -746,39 +810,12 @@
     se_copy = remote(se_p.at[1 - core], se_r, pair_sem.at[2, 0], pair_sem.at[2, 1], other)
     se_copy.start()
 
-    home = place_matrix(256, core == 1, True)
-
-    def give_back(which, act):
-        ref, out = ((os_s, oret_out), (is_s, iret_out))[which]
-        for b in range(2):
-            to_core = jnp.where(core == 0, b, 1 - b)
-            own = jnp.logical_and(zh == core, b == 0)
-
-            @pl.when(own)
-            def _():
-                act(lambda: pltpu.make_async_copy(ref.at[b], out.at[zh], ret_recv.at[which, zh]), True)
-
-            @pl.when(jnp.logical_not(own))
-            def _():
-                act(
-                    lambda: remote(
-                        ref.at[b], out.at[zh], ret_send.at[which, b], ret_recv.at[which, zh],
-                        seq_peer(me, core, to_core),
-                    ),
-                    False,
-                )
-
+    loads[5].wait()
     for b in range(2):
         os_s[b] = mm(home, o_ref[256 * b : 256 * b + 256, :]).astype(BF16)
     give_back(0, lambda make, local: make().start())
-
-    loads[3].wait()
-    for p in range(3):
-        hct_s[p] = mm_nt(perm_s[p], hcg_ref[...]).astype(BF16)
-    loads[4].wait()
-    loads[0].wait()
-    loads[1].wait()
-    da_copy.wait()
+    for load in loads[6:9]:
+        load.wait()
 
     def attend_back(i, _):
         pc, pair = i // 6, i % 6
@@ -882,7 +919,17 @@
             out.append(total)
         return out
 
-    lax.fori_loop(0, 6, attend_back, 0)
+    def finish(copies, own, recv, done, out, at, spots):
+        for copy in copies:
+            copy.wait()
+        for p in range(3):
+            total = own[p, spots[p]].astype(F32)
+            for o in range(3):
+                total = total + recv[o, p].astype(F32)
+            done[p] = total
+        spread(done, out, at)
+
+    lax.fori_loop(0, 6, attend_back, 0, unroll=2)
     mp_copy.wait()
     item_s[2:6, :] = (mp_s[0:4, :] + mr_s[0:4, :]).astype(BF16).astype(F32)
     time_id = time_ref[zh]
@@ -894,29 +941,23 @@
     se_copy.wait()
     se_s[0] = (se_p[core].astype(F32) + se_r[...].astype(F32)).astype(BF16)
     small = small_stage(0, se_s, de_s, 0)
-    for copy in st2e:
-        copy.wait()
+    lax.fori_loop(6, 12, attend_back, 0, unroll=2)
+    late = []
     for p in range(3):
-        got = second(s1_ref, r2e, 4, p, early_peer(me, 1, p, 1)[0])
-
-        @pl.when(core == 0)
-        def _():
-            for c in range(4):
-                t3e[p, c] = jnp.concatenate(
-                    [got[k][12 * c : 12 * c + 12] for k in range(4)], axis=0
-                ).astype(BF16)
-
-        @pl.when(core == 1)
-        def _():
-            for c in range(4):
-                t3e[p, c] = got[c].astype(BF16)
-
-    st3e = stage_sends(2, lambda p, o, c: (t3e.at[p, c], r3e.at[o - 1, p]), 0)
-    lax.fori_loop(6, 12, attend_back, 0)
-    small_take(0, se_s, de_s, 0, small, se_f)
-    small = small_stage(1, se_s, de_s, 0)
-
-    loads[2].wait()
+        for at, to in (
+            (512 * p, (0, p, 0)), (512 * p + 256, (0, p, 1)), (1536 + 256 * p, (1, p, 1))
+        ):
+            lg_s[to] = mm(
+                hct_s[p], dqkv_s[:, :, :, :, at : at + 256].reshape(512, 256)
+            ).astype(BF16)
+        late.append(
+            remote(
+                lg_s.at[1 - core, p], prl_s.at[p], pair_sem.at[4 + p, 0], pair_sem.at[4 + p, 1],
+                other,
+            )
+        )
+        late[-1].start()
+    loads[9].wait()
     for half in (1, 0):
         got = mm_nt(dqkv_s[half].reshape(256, 3 * D), w_s[...]).astype(BF16)
         dhc_s[half] = got.reshape(8, 2, 16, D)
@@ -931,20 +972,28 @@
     ]
     for copy in near:
         copy.start()
-    loads[6].wait()
+    loads[10].wait()
+    for copy in st1x:
+        copy.wait()
     for p in range(3):
-        for at, to in (
-            (512 * p, (0, p, 0)), (512 * p + 256, (0, p, 1)), (1536 + 256 * p, (1, p, 1))
-        ):
-            lg_s[to] = mm(
-                hct_s[p], dqkv_s[:, :, :, :, at : at + 256].reshape(512, 256)
-            ).astype(BF16)
-    late = [
-        remote(lg_s.at[1 - core, p], prl_s.at[p], pair_sem.at[4 + p, 0], pair_sem.at[4 + p, 1], other)
-        for p in range(3)
-    ]
-    for copy in late:
-        copy.start()
+        here, _peer = early_peer(me, 0, p, 1)
+        total = last_ref[p, here].astype(F32)
+        for o in range(3):
+            total = total + r1x[o, p].astype(F32)
+        total = total.astype(BF16)
+
+        @pl.when(core == 0)
+        def _():
+            s1_s[p, 3] = total
+
+        @pl.when(core == 1)
+        def _():
+            for c in range(4):
+                s1_s[p, c, 144:192] = total[48 * c : 48 * c + 48]
+
+    st2e = stage_sends(1, lambda p, o, b: (s1_s.at[p, :, chunk(b, 48)], r2e.at[o - 1, p]), 0)
+    small_take(0, se_s, de_s, 0, small, se_f)
+    small = small_stage(1, se_s, de_s, 0)
     ones = jnp.ones((8, 512), BF16)
     for row, at in ((10, 0), (11, 2 * D)):
         sums = mm(ones, dqkv_s[:, :, :, :, at : at + D].reshape(512, D))
@@ -955,11 +1004,13 @@
     dhc_copy.wait()
     for copy in near:
         copy.wait()
+    loads[11].wait()
     masks = side_masks()
 
     def lanes(j, _):
         cols = pl.ds(pl.multiple_of(j * 128, 128), 128)
-        taps = [tap_ref[t : t + 1, cols] for t in range(9)]
+        taps = tap_ref[:, cols].astype(F32)
+        taps = [taps[t : t + 1] for t in range(9)]
         back = [by_core(taps, 8 - t, core) for t in range(9)]
 
         def sided_d(l):
@@ -998,11 +1049,21 @@
         return 0
 
     lax.fori_loop(0, D // 128, lanes, 0)
+    st1l = []
+    for p in range(3):
+        late[p].wait()
+        for k in range(2):
+            lg_s[core, p, k] = lg_s[core, p, k] + prl_s[p, k]
+        st1l += stage_sends(
+            0, lambda p, o, a: (lg_s.at[core, p, :, chunk(a, 192)], r1l.at[o - 1, p]), 1, (p,)
+        )
+    for load in loads[12:14]:
+        load.wait()
     scale1 = mod_ref[1:2, :]
     acc_s[...] = jnp.zeros_like(acc_s)
 
     def rows_n(r, _):
-        at = pl.ds(pl.multiple_of(r * 32, 32), 32)
+        at = pl.ds(pl.multiple_of(r * 128, 128), 128)
         n1, rs = norm_parts(x_ref[at, :].astype(F32))
         dh = gh_s[at, :]
         g1 = dh * (1.0 + scale1)
@@ -1016,7 +1077,7 @@
         acc_s[1] += fold8(dh * n1)
         return 0
 
-    lax.fori_loop(0, 16, rows_n, 0)
+    lax.fori_loop(0, 4, rows_n, 0)
     mpl_s[...] = jnp.zeros_like(mpl_s)
     for i in range(2):
         mpl_s[i : i + 1, :] = jnp.sum(acc_s[i], axis=0, keepdims=True)
@@ -1026,23 +1087,11 @@
         sl_p[half] = sv_s[:, 384 * half : 384 * half + 384].astype(BF16)
     sl_copy = remote(sl_p.at[1 - core], sl_r, pair_sem.at[8, 0], pair_sem.at[8, 1], other)
     sl_copy.start()
-    for copy in late:
-        copy.wait()
-    for p in range(3):
-        for k in range(2):
-            lg_s[core, p, k] = lg_s[core, p, k] + prl_s[p, k]
-    st1l = stage_sends(
-        0, lambda p, o, a: (lg_s.at[core, p, :, chunk(a, 192)], r1l.at[o - 1, p]), 1
-    )
     for b in range(2):
         is_s[b] = mm(home, ig_s[256 * b : 256 * b + 256, :]).astype(BF16)
-    give_back(1, lambda make, local: make().start())
-    small_take(1, se_s, de_s, 0, small, se_f)
-    small = small_stage(2, se_s, de_s, 0)
-
     mpl_copy.wait()
     item_s[0:2, :] = (mpl_s[0:2, :] + mrl_s[0:2, :]).astype(BF16).astype(F32)
-    loads[5].wait()
+    loads[14].wait()
     cond = mod_ref[6:7, :]
     d_silu = jnp.zeros((8, D), F32)
     for i in range(6):
@@ -1058,54 +1107,69 @@
     sl_s[0] = (sl_p[core].astype(F32) + sl_r[...].astype(F32)).astype(BF16)
     small_l = small_stage(0, sl_s, dl_s, 1)
 
-    def finish(copies, own, recv, done, out, at, spots):
-        for copy in copies:
-            copy.wait()
-        for p in range(3):
-            total = own[p, spots[p]].astype(F32)
-            for o in range(3):
-                total = total + recv[o, p].astype(F32)
-            done[p] = total
-        spread(done, out, at)
-
-    finish(st3e, t3e, r3e, fe_s, fe_out, 9, [early_peer(me, 2, p, 1)[0] for p in range(3)])
-    spots = [[axis_spot(me, ORDERS[p][stage]) for p in range(3)] for stage in range(3)]
-    for copy in st1l:
+    small_take(1, se_s, de_s, 0, small, se_f)
+    small = small_stage(2, se_s, de_s, 0)
+    for copy in st2e:
         copy.wait()
     for p in range(3):
+        got = second(s1_s, r2e, 4, p, early_peer(me, 1, p, 1)[0])
+
+        @pl.when(core == 0)
+        def _():
+            for c in range(4):
+                t3e[p, c] = jnp.concatenate(
+                    [got[k][12 * c : 12 * c + 12] for k in range(4)], axis=0
+                ).astype(BF16)
+
+        @pl.when(core == 1)
+        def _():
+            for c in range(4):
+                t3e[p, c] = got[c].astype(BF16)
+
+    st3e = stage_sends(2, lambda p, o, c: (t3e.at[p, c], r3e.at[o - 1, p]), 0)
+
+    small_take(0, sl_s, dl_s, 1, small_l, sl_f)
+    small_l = small_stage(1, sl_s, dl_s, 1)
+    spots = [[axis_spot(me, ORDERS[p][stage]) for p in range(3)] for stage in range(3)]
+    st2l, st3l = [], []
+    for p in range(3):
+        for copy in st1l[3 * p : 3 * p + 3]:
+            copy.wait()
         for k in range(2):
             total = lg_s[core, p, k, chunk(spots[0][p], 192), :].astype(F32)
             for o in range(3):
                 total = total + r1l[o, p, k].astype(F32)
             s1l[p, k] = total.astype(BF16)
-    st2l = stage_sends(1, lambda p, o, b: (s1l.at[p, :, chunk(b, 48)], r2l.at[o - 1, p]), 1)
-    small_take(0, sl_s, dl_s, 1, small_l, sl_f)
-    small_l = small_stage(1, sl_s, dl_s, 1)
+        st2l += stage_sends(
+            1, lambda p, o, b: (s1l.at[p, :, chunk(b, 48)], r2l.at[o - 1, p]), 1, (p,)
+        )
+    give_back(1, lambda make, local: make().start())
+    small_take(1, sl_s, dl_s, 1, small_l, sl_f)
+    small_l = small_stage(2, sl_s, dl_s, 1)
+    for p in range(3):
+        for copy in st2l[3 * p : 3 * p + 3]:
+            copy.wait()
+        got = second(s1l, r2l, 2, p, spots[1][p])
+        for c in range(4):
+            t3l[p, c] = jnp.concatenate(
+                [got[0][12 * c : 12 * c + 12], got[1][12 * c : 12 * c + 12], jnp.zeros((8, 256), F32)],
+                axis=0,
+            ).astype(BF16)
+        st3l += stage_sends(2, lambda p, o, c: (t3l.at[p, c], r3l.at[o - 1, p]), 1, (p,))
     small_take(2, se_s, de_s, 0, small, se_f)
     spread(se_f, se_out, 10)
     ends.append(
         remote(de_s.at[core], de_s.at[core], pair_sem.at[11, 0], pair_sem.at[11, 1], other)
     )
     ends[-1].start()
-    for copy in st2l:
-        copy.wait()
-    for p in range(3):
-        got = second(s1l, r2l, 2, p, spots[1][p])
-        for c in range(4):
-            t3l[p, c] = jnp.concatenate(
-                [got[0][12 * c : 12 * c + 12], got[1][12 * c : 12 * c + 12], jnp.zeros((8, 256), F32)],
-                axis=0,
-            ).astype(BF16)
-    st3l = stage_sends(2, lambda p, o, c: (t3l.at[p, c], r3l.at[o - 1, p]), 1)
-    small_take(1, sl_s, dl_s, 1, small_l, sl_f)
-    small_l = small_stage(2, sl_s, dl_s, 1)
-    finish(st3l, t3l, r3l, fl_s, fl_out, 12, spots[2])
+    finish(st3e, t3e, r3e, fe_s, fe_out, 9, [early_peer(me, 2, p, 1)[0] for p in range(3)])
     small_take(2, sl_s, dl_s, 1, small_l, sl_f)
     spread(sl_f, sl_out, 13)
     ends.append(
         remote(dl_s.at[core], dl_s.at[core], pair_sem.at[14, 0], pair_sem.at[14, 1], other)
     )
     ends[-1].start()
+    finish(st3l, t3l, r3l, fl_s, fl_out, 12, spots[2])
     for which in range(2):
         give_back(which, lambda make, local: None if local else make().wait_send())
         for item_slot in range(2):
@@ -1124,7 +1188,7 @@
 
 
 def back_call(
-    da, qkv, p, hcg, h, x, dx, mod, times, w, mw, taps, perm, o, s1, go, s2, sb
+    da, qkv, p, hcg, h, x, dx, mod, times, w, mw, taps, perm, o, s1, last, dbr, at, s2, sb
 ):
     G = (2, 8, 2, 16)
     shape = jax.ShapeDtypeStruct
@@ -1134,9 +1198,9 @@
     return pl.pallas_call(
         back_kernel,
         in_specs=[
-            ANY_SPEC, ANY_SPEC, ANY_SPEC, VMEM_SPEC, VMEM_SPEC, VMEM_SPEC, VMEM_SPEC, VMEM_SPEC,
-            SMEM_SPEC, ANY_SPEC, ANY_SPEC, VMEM_SPEC, ANY_SPEC, VMEM_SPEC, VMEM_SPEC, ANY_SPEC,
-            VMEM_SPEC, VMEM_SPEC,
+            ANY_SPEC, ANY_SPEC, ANY_SPEC, ANY_SPEC, ANY_SPEC, ANY_SPEC, ANY_SPEC, VMEM_SPEC,
+            SMEM_SPEC, ANY_SPEC, ANY_SPEC, VMEM_SPEC, ANY_SPEC, ANY_SPEC, ANY_SPEC, ANY_SPEC,
+            ANY_SPEC, ANY_SPEC, VMEM_SPEC, VMEM_SPEC,
         ],
         out_specs=[ANY_SPEC] * 8,
         out_shape=[
@@ -1150,7 +1214,8 @@
             V(mw.shape, BF16), V((3, D, D), BF16), V(G + (D,), BF16), V(G + (3 * D,), BF16),
             V((3, D, 512), BF16), V(G + (D,), BF16), V((9, 2, 2, 16, D), BF16), V((512, D), F32),
             V((512, D), BF16), V((2, 256, D), BF16), V((2, 256, D), BF16),
-            V((2, 3, 2, D, 256), BF16), V((3, 2, D, 256), BF16), V((3, 3, 2, 192, 256), BF16),
+            V((2, 3, 2, D, 256), BF16), V((3, 2, D, 256), BF16), V((3, 4, 192, 256), BF16), V((3, 3, 192, 256), BF16),
+            V((3, 3, 2, 192, 256), BF16),
             V((3, 2, 192, 256), BF16), V((3, 3, 4, 48, 256), BF16), V((3, 3, 2, 48, 256), BF16),
             V((3, 4, 48, 256), BF16), V((3, 4, 32, 256), BF16), V((3, 3, 48, 256), BF16),
             V((3, 3, 32, 256), BF16), V((3, 48, 256), F32), V((3, 32, 256), F32),
@@ -1159,14 +1224,143 @@
             V((2, 16, 384), BF16), V((16, 384), BF16), V((12, 16, 384), BF16), V((16, 384), F32),
             V((8, D), F32), V((8, D), F32), V((8, D), F32), V((8, D), F32), V((8, D), F32),
             V(items, BF16), V(items, BF16),
-            DMA((15,)), DMA((15, 2)), DMA((2, 2)), DMA((2, 2)), DMA((2, 3, 3, 3)),
+            V((512, D), BF16), V((576, D), BF16), V((576, D), BF16), V((512, D), F32),
+            V((512, D), BF16), V((3, 4, 192, 256), BF16), V((512, D), BF16), V((576, D), BF16),
+            DMA((30,)), DMA((15, 2)), DMA((2, 2)), DMA((2, 2)), DMA((2, 3, 3, 3)),
             DMA((2, 3, 3, 3)), DMA((2, 3, 3)), DMA((2, 3, 3)), DMA((2, 3, 3)), DMA((2, 3, 3)),
         ],
         compiler_params=pltpu.CompilerParams(
             collective_id=2, has_side_effects=True, vmem_limit_bytes=60 * 2**20
         ),
         name="back",
-    )(da, qkv, p, hcg, h, x, dx, mod, times, w, mw, taps, perm, o, s1, go, s2, sb)
+    )(da, qkv, p, hcg, h, x, dx, mod, times, w, mw, taps, perm, o, s1, last, dbr, at, s2, sb)
+
+
+def share_kernel(
+    out_ref, ig_ref, fe_hbm, fl_hbm, se_hbm, sl_hbm, de_hbm, dl_hbm,
+    o_out, ig_out, cond_out, table_out, mw_out, mb_out, aw_out, ab_out, qkv_out, qb_out, vb_out,
+    ow_out, ob_out, f1_out, f1b_out, fw_out, fb_out, f2_out, f2b_out,
+    ig_s, o_s, igf_s, e_s, l_s, fe_ref, fl_ref, se_ref, sl_ref, de_ref, dl_ref, sem,
+):
+    me = spot()
+    core = me["core"]
+    shard = me["dp"] * 4 + me["seq"]
+    ig_load = pltpu.make_async_copy(ig_ref, ig_s, sem.at[0])
+    o_load = pltpu.make_async_copy(out_ref, o_s, sem.at[9])
+    o_move = pltpu.make_async_copy(o_s, o_out, sem.at[1])
+    loads = [
+        pltpu.make_async_copy(*pair, sem.at[3 + at])
+        for at, pair in enumerate((
+            (fe_hbm, fe_ref), (fl_hbm, fl_ref), (se_hbm, se_ref), (sl_hbm, sl_ref),
+            (de_hbm, de_ref), (dl_hbm, dl_ref),
+        ))
+    ]
+    for load in loads:
+        load.start()
+    ig_load.start()
+    o_load.start()
+    o_load.wait()
+    o_move.start()
+    ig_load.wait()
+    igf_s[...] = ig_s[...].astype(F32)
+    ig_move = pltpu.make_async_copy(igf_s, ig_out, sem.at[2])
+    ig_move.start()
+    for load in loads:
+        load.wait()
+    e_s[...] = de_ref[...].reshape(2048, 128).astype(F32)
+    l_s[...] = dl_ref[...].reshape(2048, 128).astype(F32)
+
+    def six(v, at):
+        return jnp.where(core == 0, v[at : at + 6], v[at + 6 : at + 12])
+
+    for p in range(3):
+        early0, early1 = fe_ref[0, p], fe_ref[1, p]
+        for i in range(4):
+            at = D * i + 256 * p
+            f1_out[:, at : at + 256] = six(early0, 12 * i)
+        f2_out[:, 256 * p : 256 * p + 256] = jnp.where(core == 0, early1[0:24], early1[24:48])
+        late0, late1 = fl_ref[0, p], fl_ref[1, p]
+        for k in range(2):
+            at = 512 * p + 256 * k
+            qkv_out[:, at : at + 256] = six(late0, 12 * k)
+        at = 1536 + 256 * p
+        qkv_out[:, at : at + 256] = six(late1, 12)
+        ow_out[:, 256 * p : 256 * p + 256] = six(late1, 0)
+
+    def columns(start, count=D):
+        at = lax.broadcasted_iota(jnp.int32, (count, 128), 0)
+        to = lax.broadcasted_iota(jnp.int32, (count, 128), 1)
+        return at == start + to
+
+    def exact(a, b):
+        return lax.dot_general(
+            a, b.astype(F32), (((1,), (0,)), ((), ())), preferred_element_type=F32,
+            precision=lax.Precision.HIGHEST,
+        )
+
+    mine = columns(shard * 6)
+    slim = exact(jnp.concatenate((sl_ref[0], sl_ref[1]), axis=1), mine)
+    aw_out[...] = slim.T[0:6, 0:9]
+    for ref, at in ((ab_out, 9), (qb_out, 10), (vb_out, 11), (ob_out, 12), (f2b_out, 13)):
+        ref[...] = slim[at : at + 1, 0:6].reshape(6)
+    quarter = shard // 32
+    wide = se_ref[quarter // 2, pl.ds(pl.multiple_of(quarter % 2 * 16, 16), 16), :]
+    wide = exact(wide, columns(shard % 32 * 24))
+    fw_out[...] = wide[0:9, 0:24]
+    fb_out[...] = wide[9:10, 0:24].reshape(24)
+    f1b_out[...] = wide[10:11, 0:24].reshape(24)
+
+    def item_rows(ref, at):
+        return ref[pl.ds(at // 16 * 1024 + at % 16, 64, stride=16), :]
+
+    silu = jnp.concatenate([item_rows(e_s, 24 + l) for l in range(6)], axis=1)
+    silu = mm(silu.astype(BF16), mine.astype(BF16)).astype(BF16)
+    sums = []
+    for at in range(36):
+        d_mod = item_rows(l_s, at) if at < 12 else item_rows(e_s, at - 12)
+        mw_out[:, 128 * at : 128 * at + 128] = mm_tn(silu, d_mod.astype(BF16))[0:6]
+        sums.append(jnp.sum(d_mod, axis=0, keepdims=True))
+    total = jnp.concatenate(sums, axis=1)
+    total = exact(jnp.concatenate([total] * 8, axis=0), columns(shard * 36, 6 * D))
+    mb_out[...] = total[0:1, 0:36].reshape(36)
+
+    cond = jnp.concatenate([item_rows(l_s, 16 + l) for l in range(6)], axis=1).astype(BF16)
+    here = lax.broadcasted_iota(jnp.int32, (8, 64), 1)
+    slot = lax.broadcasted_iota(jnp.int32, (8, 64), 0)
+    own = here == ((slot * 2 + me["zl"]) * 4 + me["y"]) * 4 + me["x"]
+    own = jnp.logical_and(own, slot < 2)
+    cond_out[...] = mm(own.astype(BF16), cond)[0:2]
+    times = 32.0 * item_rows(e_s, 30) + item_rows(e_s, 31)
+    bucket = lax.broadcasted_iota(jnp.int32, (64, 1024), 1).astype(F32)
+    hot = (bucket == jnp.concatenate([times] * 8, axis=1)).astype(BF16)
+    my_cond = mm(cond, mine.astype(BF16)).astype(BF16)
+    table_out[...] = mm_tn(my_cond, hot)[0:6, 0 : table_out.shape[1]]
+
+    ig_move.wait()
+    o_move.wait()
+
+
+def share_call(buckets, *args):
+    shapes = [
+        ((2, 256, D), BF16), ((2, 256, D), F32), ((2, D), F32), ((6, buckets), F32),
+        ((6, 6 * D), F32), ((36,), F32), ((6, 9), F32), ((6,), F32), ((6, 3 * D), F32),
+        ((6,), F32), ((6,), F32), ((6, D), F32), ((6,), F32), ((6, FF), F32), ((24,), F32),
+        ((9, 24), F32), ((24,), F32), ((24, D), F32), ((6,), F32),
+    ]
+    return pl.pallas_call(
+        share_kernel,
+        in_specs=[ANY_SPEC] * 8,
+        out_specs=[ANY_SPEC] * 2 + [VMEM_SPEC] * 17,
+        out_shape=[jax.ShapeDtypeStruct(*s) for s in shapes],
+        scratch_shapes=[
+            pltpu.VMEM((2, 256, D), BF16), pltpu.VMEM((2, 256, D), BF16),
+            pltpu.VMEM((2, 256, D), F32), pltpu.VMEM((2048, 128), F32), pltpu.VMEM((2048, 128), F32),
+            *[pltpu.VMEM(v.shape, v.dtype) for v in args[2:]],
+            pltpu.SemaphoreType.DMA((10,)),
+        ],
+        compiler_params=pltpu.CompilerParams(vmem_limit_bytes=60 * 2**20),
+        name="share",
+    )(*args)
 
 
 def perm_matrices():
@@ -1184,77 +1378,27 @@
     conv_attn_weight, conv_attn_bias, qkv_weight, query_bias, value_bias, out_weight, out_bias,
     fc1_weight, fc1_bias, conv_ffn_weight, conv_ffn_bias, fc2_weight, fc2_bias,
 ):
-    core = lax.axis_index("seq") % 2
-    shard = lax.axis_index("dp") * 4 + lax.axis_index("seq")
     alive = (lax.axis_index("seq") // 2 < item_counts).astype(F32)
     perm = (perm_matrices()[:, :, None] == np.arange(D)[None, None, :]).astype(BF16)
-    taps_attn = jnp.pad(conv_attn_weight.astype(F32), ((0, 7), (0, 0)))
-    taps_ffn = jnp.pad(conv_ffn_weight.astype(F32), ((0, 7), (0, 0)))
-    qkv_bias = jnp.concatenate(
-        (query_bias.astype(F32), jnp.zeros((D,), F32), value_bias.astype(F32))
-    )[None]
     x, ct, h, hcg, qkv, p, at, mod = attn_call(
         latents.reshape(2, 256, D), cotangent.reshape(2, 256, D), conditioning, timesteps,
-        time_table, mod_weight, mod_bias[None], qkv_weight, qkv_bias, taps_attn,
-        conv_attn_bias[None],
+        time_table, mod_weight, mod_bias, qkv_weight, query_bias, value_bias, conv_attn_weight,
+        conv_attn_bias,
     )
-    out, s1, go, da, dx, s2, sb = ffn_call(
-        x, at.reshape(576, D), ct, mod, alive, perm, out_weight, out_bias[None], fc1_weight,
-        fc1_bias[None], taps_ffn, conv_ffn_bias[None], fc2_weight, fc2_bias[None],
+    at = at.reshape(576, D)
+    out, s1, last, dbr, da, dx, s2, sb = ffn_call(
+        x, at, ct, mod, alive, perm, out_weight, out_bias, fc1_weight, fc1_bias, conv_ffn_weight,
+        conv_ffn_bias, fc2_weight, fc2_bias,
     )
-    out, ig, fe, fl, se, sl, de, dl = back_call(
-        da.reshape(8, 2, 2, 16, D), qkv, p, hcg.reshape(512, D), h, x, dx, mod, timesteps,
-        qkv_weight, mod_weight, taps_attn, perm, out, s1, go, s2, sb,
+    got = back_call(
+        da, qkv, p, hcg.reshape(512, D), h, x, dx, mod, timesteps,
+        qkv_weight, mod_weight, conv_attn_weight, perm, out, s1, last,
+        dbr.reshape(512, D), at, s2, sb,
     )
-    output = out.reshape(2, 8, 32, D)
-    input_grad = ig.reshape(2, 8, 32, D).astype(F32)
-
-    def items(v):
-        v = v.reshape(2, 2, 2, 4, 4, 16, 128).transpose(4, 2, 3, 1, 0, 5, 6)
-        return v.reshape(64, 32, 128)
-
-    early, late_rows = items(de), items(dl)
-    d_mod = jnp.concatenate((late_rows[:, :12], early[:, :24]), axis=1).reshape(64, 6 * D)
-    all_silu = early[:, 24:30].reshape(64, D)
-    all_times = (32.0 * early[:, 30, 0].astype(F32) + early[:, 31, 0].astype(F32)).astype(jnp.int32)
-    all_cond_grad = late_rows[:, 16:22].reshape(64, D)
-    cond_grad = lax.dynamic_slice_in_dim(
-        all_cond_grad, lax.axis_index("dp") * 2, 2, axis=0
-    ).astype(F32)
-    my_silu = lax.dynamic_slice_in_dim(all_silu, shard * 6, 6, axis=1)
-    mod_grad = lax.dot_general(
-        my_silu, d_mod, (((0,), (0,)), ((), ())), preferred_element_type=F32
-    )
-    mod_bias_grad = jnp.sum(
-        lax.dynamic_slice_in_dim(d_mod, shard * 36, 36, axis=1).astype(F32), axis=0
-    )
-    my_cond_grad = lax.dynamic_slice_in_dim(all_cond_grad, shard * 6, 6, axis=1)
-    table_grad = jnp.dot(
-        (jnp.arange(1000)[:, None] == all_times[None, :]).astype(BF16), my_cond_grad,
-        preferred_element_type=F32,
-    )
-    six = lambda v: lax.dynamic_slice_in_dim(v, core * 6, 6, axis=-2)
-    fc1_grad = six(fe[0].reshape(3, 4, 12, 256)).transpose(2, 1, 0, 3).reshape(6, FF)
-    fc2_grad = lax.dynamic_slice_in_dim(fe[1], core * 24, 24, axis=1).transpose(1, 0, 2)
-    late = six(fl[:, :, :24].reshape(2, 3, 2, 12, 256))
-    qkv_grad = jnp.concatenate(
-        (
-            late[0].transpose(2, 0, 1, 3).reshape(6, 1536),
-            late[1, :, 1].transpose(1, 0, 2).reshape(6, D),
-        ),
-        axis=1,
-    )
-    out_grad = late[1, :, 0].transpose(1, 0, 2).reshape(6, D)
-    wide = se.reshape(4, 16, D).transpose(1, 0, 2).reshape(16, FF)
-    wide = lax.dynamic_slice_in_dim(wide, shard * 24, 24, axis=1)
-    slim = lax.dynamic_slice_in_dim(
-        sl.transpose(1, 0, 2).reshape(16, D), shard * 6, 6, axis=1
-    )
-    return (
-        output, input_grad, cond_grad, table_grad, mod_grad, mod_bias_grad, slim[:9], slim[9],
-        qkv_grad, slim[10], slim[11], out_grad, slim[12], fc1_grad, wide[10], wide[:9], wide[9],
-        fc2_grad.reshape(24, D), slim[13],
-    )
+    outs = list(share_call(time_table.shape[0], *got))
+    outs[0], outs[1] = outs[0].reshape(latents.shape), outs[1].reshape(latents.shape)
+    outs[3], outs[6] = outs[3].T, outs[6].T
+    return tuple(outs)
 
 
 def solution(mesh):

time: 207 us -> 167 us (0.81)
  Pallas kernels: 181 us -> 164 us
  local copies, waits for them, and re-layouts: 14 us -> 0 us
  other arithmetic: 6.8 us -> 0 us
    pallas_call x1, Pallas kernels: 73.6 us -> 56.7 us  [ffn_call(): pl.pallas_call(ffn_kernel, grid=(NFC,), in_specs=[whole((576, D)), whole(...]
    broadcast_in_dim x8 -> x0, local copies, waits for them, and re-layouts: 5.57 us -> none  [the longest x1 1.32 us: local(): mod_bias[None]]
    pallas_call x1 -> x2, Pallas kernels: 70.5 us -> 74.2 us  [the longest x1 68.5 us: back_call(): pl.pallas_call(back_kernel, in_specs=[ANY_SPEC, ANY_SPEC, ANY_SPEC, ANY_S...]
    pallas_call x1, Pallas kernels: 36.7 us -> 33.3 us  [attn_call(): pl.pallas_call(attn_kernel, in_specs=[ANY_SPEC, ANY_SPEC, VMEM_SPEC, SMEM...]
    convert_element_type x5 -> x0, other arithmetic: 3.28 us -> none  [the longest x1 1.3 us: local(): input_grad = ig.reshape(2, 8, 32, D).astype(F32)]
    reshape x7 -> x0, local copies, waits for them, and re-layouts: 2.53 us -> none  [the longest x2 1.15 us: items(): v = v.reshape(2, 2, 2, 4, 4, 16, 128).transpose(4, 2, 3, 1, 0, 5, 6)]
    unnamed x32 -> x0, local copies, waits for them, and re-layouts: 2.52 us -> none
    slice x12 -> x0, local copies, waits for them, and re-layouts: 2.08 us -> none  [the longest x2 1.06 us: local(): late = six(fl[:, :, :24].reshape(2, 3, 2, 12, 256))]
where the time goes in v3:
time: 167 us; the launch traced here: 166 us
  Pallas kernels  164 us (98%)
    pallas_call x1, Pallas kernels, back_call(): pl.pallas_call(back_kernel, in_specs=[ANY_SPEC, ANY_SPEC, ANY_SPEC, ANY_S...  68.5 us
    pallas_call x1, Pallas kernels, ffn_call(): pl.pallas_call(ffn_kernel, grid=(NFC,), in_specs=[whole((576, D)), whole(...  56.7 us
    pallas_call x1, Pallas kernels, attn_call(): pl.pallas_call(attn_kernel, in_specs=[ANY_SPEC, ANY_SPEC, VMEM_SPEC, SMEM...  33.3 us
    pallas_call x1, Pallas kernels, share_call(): pl.pallas_call(share_kernel, in_specs=[ANY_SPEC] * 8, out_specs=[ANY_SPEC...  5.73 us

profile of v3, /device:TPU:0, one launch (start us, length us, event | category | flops | bytes accessed | tf_op | source)
XLA Modules:
  0.0 165.8 jit_solution(14604327942849723668)
XLA Ops:
  1.3 33.3 %attend.1 = (bf16[576,768]{1,0:T(8,128)(2,1)}, bf16[576,768]{1,0:T(8,128)(2,1)}, bf16[576,768]{1,0:T(8,128)(2,1)}, bf16[2,8,2,16,768]{4,3,2,1,0:T(8,128)(2,1)}, ...) custom-call(bf16[2,256,768]{2,1,0:T(8,128)(2,1)} %bitcast.12, ...), custom_call_target="tpu_custom_call" | custom-call | tf_op jit(solution)/shard_map/attend/pallas_call | solution.py:692
  34.7 56.7 %ffn.1 = (bf16[512,768]{1,0:T(8,128)(2,1)}, bf16[3,4,192,256]{3,2,1,0:T(8,128)(2,1)}, bf16[3,4,192,256]{3,2,1,0:T(8,128)(2,1)}, bf16[8,2,2,16,768]{4,3,2,1,0:T(8...) custom-call(bf16[576,768]{1,0:T(8,128)(2,1)} %get-tuple-element.62.x, ...), custom_call_target="tpu_custom_call" | custom-call | tf_op jit(solution)/shard_map/ffn/pallas_call | solution.py:409
  91.4 68.5 %back.1 = (bf16[2,256,768]{2,1,0:T(8,128)(2,1)}, bf16[2,256,768]{2,1,0:T(8,128)(2,1)}, f32[2,3,48,256]{3,2,1,0:T(8,128)}, f32[2,3,32,256]{3,2,1,0:T(8,128)}, f32...) custom-call(bf16[2,8,2,16,768]{4,3,2,1,0:T(8,128)(2,1)} %get-tuple-e, ...), custom_call_target="tpu_custom_call" | custom-call | tf_op jit(solution)/shard_map/back/pallas_call | solution.py:1198
  159.9 5.7 %share.1 = (bf16[2,256,768]{2,1,0:T(8,128)(2,1)}, f32[2,256,768]{2,1,0:T(8,128)}, f32[2,768]{1,0:T(2,128)}, f32[6,1000]{1,0:T(8,128)}, f32[6,4608]{1,0:T(8,128)}...) custom-call(bf16[2,256,768]{2,1,0:T(8,128)(2,1)} %get-tuple-element., ...), custom_call_target="tpu_custom_call" | custom-call | tf_op jit(solution)/shard_map/share/pallas_call | solution.py:1350
